TPU v7x, 256 devices: a whole 4x4x8 slice. The times are simulated.
256 devices in a mesh: dp: 16 (over z, core), mp: 16 (over x, y).
Axes of the slice: x: 4, y: 4, z: 8, core: 2. Of those that a mesh axis runs over, the one named last changes fastest.
Arguments:
- hidden_in: bfloat16 [64, 64, 7168], P('dp', None, 'mp'), may hold values from -6 to 6
- norm_gain: bfloat16 [7168], P('mp'), may hold values from 0.099609375 to 1.8984375
- w_query: bfloat16 [7168, 7168], P('dp', 'mp'), may hold values from -0.070868339 to 0.070868339
- w_key: bfloat16 [7168, 1024], P('dp', 'mp'), may hold values from -0.070868339 to 0.070868339
- w_value: bfloat16 [7168, 1024], P('dp', 'mp'), may hold values from -0.0625 to 0.0625
- w_out: bfloat16 [7168, 7168], P('mp', 'dp'), may hold values from -0.09375 to 0.09375
- key_cache: bfloat16 [64, 16, 1, 2048, 128], P('dp', 'mp'), may hold values from -52 to 52
- value_cache: bfloat16 [64, 16, 1, 2048, 128], P('dp', 'mp'), may hold values from -3 to 3
- cache_len: int32 [64], P('dp'), may hold values from 256 to 4096, as said below
- tree_parent: int32 [64, 64], P('dp'), may hold values from 0 to 62, as said below
- valid_nodes: int32 [64, 64], P('dp'), may hold values from 0 to 1, as said below
- accepted_path: int32 [64, 8], P('dp'), may hold values from 0 to 63, as said below
- slot_owner: int32 [64], replicated, may hold values from 0 to 63, each once
Outputs:
- layer_out: bfloat16 [64, 64, 7168], P('dp', None, 'mp')
- accepted_kv: bfloat16 [64, 8, 2, 1024], P('dp', None, None, 'mp')
Inputs may be any that keep to these rules, and one draw needn't show every extreme that they name: `cache_len`: some request holds exactly 4096 positions in every draw. `tree_parent`: node 0 is its own parent; every other node's parent is one of the three nodes before it. `valid_nodes`: the 1 entries of each request form a prefix of 32 to 64 nodes. `accepted_path`: each row is a chain in which every node is the parent of the next (node 0 may repeat at the start), ending at the request's last real node. `slot_owner`: each slot is named once.
All inputs are finite; a program needn't handle non-finite values.
Results may differ from a plain program's by a relative error of at most 0.007.
The roundings to bfloat16 on the way count: a program that leaves them out, or rounds other values in their place, can miss the bound.
Values may be sent and summed in bfloat16 or wider, within the bound.
No kernel may reach another device: no remote copies, remote signals or barrier semaphores. Data moves between devices by JAX's collectives and lax.ppermute only.
A program may use at most 128 MiB of HBM per device.

v0:
```python
import functools
import math

import jax
import jax.numpy as jnp
from jax import lax
from jax.experimental import pallas as pl
from jax.experimental.pallas import tpu as pltpu
from jax.sharding import PartitionSpec as P

GROUP = 7
SIDE = 4
epsilon = 1e-05
rope_base = 5000000.0
masked_score = -1e30
bf16 = jnp.bfloat16
f32 = jnp.float32
VMEM = pltpu.VMEM


def whole():
    return pl.BlockSpec(memory_space=VMEM)


def scalars():
    return pl.BlockSpec(memory_space=pltpu.SMEM)


def params(mib):
    return pltpu.CompilerParams(vmem_limit_bytes=mib * 2**20)


DP, CORES, Z = 16, 2, 8
BLOCKS = 16
CUT_COST = 2 * 10**10
ATTENTION_COST = 25 * 10**9


def moved(block, target):
    route = []
    for d in range(DP):
        for m in range(SIDE * SIDE):
            z, core, x, y = target(d // CORES, d % CORES, m // SIDE, m % SIDE)
            to = (z % Z * CORES + core) * SIDE * SIDE + x % SIDE * SIDE + y % SIDE
            route.append((d * SIDE * SIDE + m, to))
    return lax.ppermute(block, ("dp", "mp"), route)


def other_core(block):
    return moved(block, lambda z, c, x, y: (z, c ^ 1, x, y))


def along_z(block, step):
    return moved(block, lambda z, c, x, y: (z + step, c, x, y))


def first_axis(block, step):
    return moved(block, lambda z, c, x, y: (z, c, x, y + step) if c == 0 else (z, c, x + step, y))


def second_axis(block, step):
    return moved(block, lambda z, c, x, y: (z, c, x + step, y) if c == 0 else (z, c, x, y + step))


def partner(block):
    return moved(block, lambda z, c, x, y: (z, c, x, y ^ 1))


def tree_closure(parents):
    width = parents.shape[-1]
    nodes = jnp.arange(width, dtype=jnp.int32)
    onehot = (parents[..., None] == nodes).astype(f32)
    reach = jnp.minimum(jnp.eye(width, dtype=f32) + onehot, 1.0)
    for _ in range((width - 1).bit_length()):
        small = reach.astype(bf16)
        reach = jnp.minimum(
            jnp.einsum("rij,rjk->rik", small, small, preferred_element_type=f32), 1.0
        )
    return reach


def unfolded(tile):
    wide = tile.astype(f32)
    return jnp.concatenate([wide[:, :64], wide[:, 64:]], 0).astype(tile.dtype)


def folded(array):
    half = array.shape[0] // 2
    wide = array.astype(f32)
    return jnp.concatenate([wide[:half], wide[half:]], 1).astype(array.dtype)


def pack_kernel(hidden_ref, gain_ref, query_ref, key_ref, value_ref, x_ref, w_ref):
    rows = hidden_ref.shape[0]
    w_ref[:448, :384] = query_ref[:, :384]
    w_ref[:448, 384:] = jnp.concatenate(
        [query_ref[:, 384:448].astype(f32), key_ref[...].astype(f32)], 1
    ).astype(bf16)
    w_ref[448:, :] = jnp.concatenate([value_ref[...].astype(f32), jnp.zeros((64, 64), f32)], 1).astype(bf16)
    for t in range(3):
        x_ref[t * rows : (t + 1) * rows, :] = hidden_ref[:, 128 * t : 128 * t + 128]
    x_ref[3 * rows : 3 * rows + rows // 2, :] = folded(hidden_ref[:, 384:448])
    gain = jnp.concatenate([gain_ref[...].astype(f32), jnp.zeros((1, 64), f32)], 1)
    gain = jnp.concatenate([gain[:, 128 * t : 128 * t + 128] for t in range(4)] + [jnp.zeros((28, 128), f32)], 0)
    x_ref[3 * rows + rows // 2 :, :] = gain.astype(bf16)


def pack(hidden, gain, w_query, w_key, w_value):
    rows = hidden.shape[0]
    return pl.pallas_call(
        pack_kernel,
        out_shape=[
            jax.ShapeDtypeStruct((rows * 7 // 2 + 32, 128), bf16),
            jax.ShapeDtypeStruct((512, 512), bf16),
        ],
        in_specs=[whole()] * 5,
        out_specs=[whole()] * 2,
        compiler_params=params(60),
        name="pack",
    )(hidden, gain, w_query, w_key, w_value)


def join_kernel(upper_ref, lower_ref, out_ref):
    cut = upper_ref.shape[0]
    out_ref[:cut, :] = upper_ref[...]
    out_ref[cut:, :] = lower_ref[...]


def join(upper, lower):
    return pl.pallas_call(
        join_kernel,
        out_shape=jax.ShapeDtypeStruct((2 * upper.shape[0], upper.shape[1]), bf16),
        in_specs=[whole(), whole()],
        out_specs=whole(),
        compiler_params=params(4),
        name="join",
    )(upper, lower)


def cut_kernel(up_ref, down_ref, upper_ref, lower_ref):
    cut = upper_ref.shape[0]
    upper_ref[...] = up_ref[:cut, :]
    lower_ref[...] = down_ref[cut:, :]


def cut_blocks(up, down):
    half = jax.ShapeDtypeStruct((up.shape[0] // 2, up.shape[1]), bf16)
    return pl.pallas_call(
        cut_kernel,
        out_shape=[half, half],
        in_specs=[whole(), whole()],
        out_specs=[whole(), whole()],
        compiler_params=params(4),
        cost_estimate=pl.CostEstimate(flops=CUT_COST, bytes_accessed=10**6, transcendentals=0),
        name="cut_blocks",
    )(up, down)


def norm_kernel(x_ref, out_ref, squares, folds, inverse):
    rows = out_ref.shape[1]
    half = rows // 2

    @pl.loop(0, rows // 32)
    def _(chunk):
        total = jnp.zeros((32, 128), f32)
        for b in range(BLOCKS):
            for t in range(3):
                at = pl.ds(pl.multiple_of(t * rows + chunk * 32, 32), 32)
                part = x_ref[b, at, :].astype(f32)
                total = total + part * part
        squares[pl.ds(pl.multiple_of(chunk * 32, 32), 32), :] = total

    @pl.loop(0, half // 32)
    def _(chunk):
        total = jnp.zeros((32, 128), f32)
        at = pl.ds(pl.multiple_of(3 * rows + chunk * 32, 32), 32)
        for b in range(BLOCKS):
            part = x_ref[b, at, :].astype(f32)
            total = total + part * part
        folds[pl.ds(pl.multiple_of(chunk * 32, 32), 32), :] = total

    rest = folds[...]
    rest = jnp.concatenate(
        [jnp.sum(rest[:, :64], -1, keepdims=True), jnp.sum(rest[:, 64:], -1, keepdims=True)], 0
    )
    mean = (jnp.sum(squares[...], -1, keepdims=True) + rest) / (BLOCKS * 448)
    inverse[...] = jnp.broadcast_to(lax.rsqrt(mean + epsilon), inverse.shape)
    for b in range(BLOCKS):
        gain = x_ref[b, 3 * rows + half : 3 * rows + half + 16, :].astype(f32)
        for t in range(3):
            part = x_ref[b, t * rows : (t + 1) * rows, :].astype(f32)
            out_ref[b, :, 128 * t : 128 * t + 128] = (
                part * inverse[...] * gain[t : t + 1]
            ).astype(bf16)
        part = unfolded(x_ref[b, 3 * rows : 3 * rows + half, :]).astype(f32)
        out_ref[b, :, 384:448] = (part * inverse[:, :64] * gain[3:4, :64]).astype(bf16)


def norm(gathered, rows):
    return pl.pallas_call(
        norm_kernel,
        out_shape=jax.ShapeDtypeStruct((BLOCKS, rows, 448), bf16),
        in_specs=[whole()],
        out_specs=whole(),
        scratch_shapes=[
            pltpu.VMEM((rows, 128), f32),
            pltpu.VMEM((rows // 2, 128), f32),
            pltpu.VMEM((rows, 128), f32),
        ],
        compiler_params=params(16),
        cost_estimate=pl.CostEstimate(flops=10**7, bytes_accessed=8 * 10**6, transcendentals=0),
        name="norm",
    )(gathered)


def project_kernel(count, start, last, order, normed_ref, *refs):
    weights, rest = refs[:count], refs[count:]
    if start == 0:
        outs, total = rest, None
    else:
        total, outs = rest[0][...], rest[1:]
    for k in range(count):
        normed = normed_ref[order[start + k]]
        both = jnp.dot(normed, weights[k][:448, :], preferred_element_type=f32)
        value = lax.dot_general(
            normed, weights[k][448:, :448], (((1,), (1,)), ((), ())), preferred_element_type=f32
        )
        term = jnp.concatenate([both, value], 1)
        total = term if total is None else total + term
    if last:
        half = total.shape[0] // 2
        rounded = total.astype(bf16)
        for h in range(2):
            outs[h][...] = rounded[h * half : (h + 1) * half]
    else:
        outs[0][...] = total


def project(start, last, order, normed, slots, *total):
    rows, count = normed.shape[1], len(slots)
    if last:
        shape = [jax.ShapeDtypeStruct((rows // 2, 576), bf16)] * 2
    else:
        shape = [jax.ShapeDtypeStruct((rows, 576), f32)]
    return pl.pallas_call(
        functools.partial(project_kernel, count, start, last),
        out_shape=shape,
        in_specs=[scalars()] + [whole()] * (1 + count + len(total)),
        out_specs=[whole()] * len(shape),
        compiler_params=params(20),
        cost_estimate=pl.CostEstimate(
            flops=2 * rows * 448 * 576 * count, bytes_accessed=10**6 * count, transcendentals=0
        ),
        name="project",
    )(order, normed, *slots, *total)


def attention_kernel(
    facts, own_ref, oth_ref, cos_ref, sin_ref, reach_ref, pick_ref, key_ref, value_ref,
    kept_ref, sent_ref, stats_ref, chosen_ref, scores,
):
    request = pl.program_id(0)
    first = facts[0] == 0
    count = facts[1 + request]
    nodes = own_ref.shape[0]
    q_cols = 448
    cosine, sine = cos_ref[...], sin_ref[...]
    own, other = own_ref[...].astype(f32), oth_ref[...].astype(f32)

    def paired(lo, hi):
        low = jnp.where(first, own[:, lo:hi], other[:, lo:hi])
        high = jnp.where(first, other[:, lo:hi], own[:, lo:hi])
        return jnp.concatenate([low, high], 1)

    def turned(u):
        return (u * cosine + pltpu.roll(u, 64, 1) * sine).astype(bf16)

    query = paired(0, q_cols)
    queries = jnp.concatenate(
        [turned(query[:, 128 * g : 128 * g + 128]) for g in range(GROUP)], 0
    )
    rot_key = turned(paired(448, 512))
    node_value = paired(512, 576).astype(bf16)

    wide = rot_key.astype(f32)
    own_key = jnp.where(first, wide[:, :64], wide[:, 64:])
    kv_rows = jnp.concatenate([own_key, own[:, 512:576]], 1).astype(bf16)
    chosen_ref[0] = jnp.dot(pick_ref[0], kv_rows, preferred_element_type=f32).astype(bf16)

    pieces, rows, span = scores.shape
    nt = (((1,), (1,)), ((), ()))
    tree = lax.dot_general(queries, rot_key, nt, preferred_element_type=f32)
    reach = jnp.concatenate([reach_ref[0]] * GROUP, 0)
    tree = jnp.where(jnp.logical_and(reach > 0.5, first), tree, masked_score)
    highest = jnp.full((rows, 128), masked_score, f32)
    for c in range(pieces):
        part = lax.dot_general(
            queries, key_ref[0, c * span : (c + 1) * span, :], nt, preferred_element_type=f32
        )
        live = lax.broadcasted_iota(jnp.int32, (1, span), 1) + c * span < count
        part = jnp.where(live, part, masked_score)
        scores[c] = part
        for t in range(span // 128):
            highest = jnp.maximum(highest, part[:, 128 * t : 128 * t + 128])
    highest = jnp.maximum(
        jnp.max(highest, -1, keepdims=True), jnp.max(tree, -1, keepdims=True)
    )

    factor = math.log2(math.e) / math.sqrt(128.0)
    ones = jnp.ones((span, 128), bf16)
    weights = jnp.exp2((tree - highest) * factor).astype(bf16)
    summed = jnp.dot(
        weights, jnp.concatenate([node_value, ones[:nodes]], 1), preferred_element_type=f32
    )
    for c in range(pieces):
        weights = jnp.exp2((scores[c] - highest) * factor).astype(bf16)
        values = jnp.concatenate([value_ref[0, c * span : (c + 1) * span, :], ones], 1)
        summed = summed + jnp.dot(weights, values, preferred_element_type=f32)

    total = summed[:, 128:129]
    mean = summed[:, :128] / total
    some = jnp.logical_or(first, count > 0)
    level = jnp.where(some, highest * (1.0 / math.sqrt(128.0)) + jnp.log(total), masked_score)
    every = jnp.concatenate([mean[g * nodes : (g + 1) * nodes] for g in range(GROUP)], 1)
    low, high = every[:, :q_cols], every[:, q_cols:]
    kept_ref[...] = jnp.where(first, low, high)
    levels = jnp.concatenate(
        [level[g * nodes : (g + 1) * nodes] for g in range(GROUP)]
        + [jnp.zeros((nodes, 128 - GROUP), f32)], 1,
    )
    stats_ref[...] = levels
    coarse = levels[:, :16].astype(bf16).astype(f32)
    finer = (levels[:, :16] - coarse).astype(bf16).astype(f32)
    finest = levels[:, :16] - coarse - finer
    sent_ref[...] = jnp.concatenate(
        [jnp.where(first, high, low), coarse, finer, finest, jnp.zeros((nodes, 16), f32)], 1
    ).astype(bf16)


def attention(half, facts, own, other, cosine, sine, reach, pick, keys, values):
    half_len, head = keys.shape[-2:]
    requests = keys.shape[0] // 2
    nodes = own.shape[0] // requests
    columns = own.shape[1]
    base = half * requests

    def rows_of(width, at=0):
        return pl.BlockSpec((nodes, width), lambda r, facts: (at + r, 0))

    def request_of(*shape, at=0):
        return pl.BlockSpec((1,) + shape, lambda r, facts: (at + r, 0, 0))

    span = 512
    return pl.pallas_call(
        attention_kernel,
        grid_spec=pltpu.PrefetchScalarGridSpec(
            num_scalar_prefetch=1,
            grid=(requests,),
            in_specs=[
                rows_of(columns), rows_of(columns), rows_of(head, base), rows_of(head, base),
                request_of(nodes, nodes, at=base), request_of(*pick.shape[1:], at=base),
                request_of(half_len, head, at=base), request_of(half_len, head, at=base),
            ],
            out_specs=[rows_of(448), rows_of(512), rows_of(128), request_of(pick.shape[1], 128)],
            scratch_shapes=[pltpu.VMEM((half_len // span, GROUP * nodes, span), f32)],
        ),
        out_shape=[
            jax.ShapeDtypeStruct((requests * nodes, 448), f32),
            jax.ShapeDtypeStruct((requests * nodes, 512), bf16),
            jax.ShapeDtypeStruct((requests * nodes, 128), f32),
            jax.ShapeDtypeStruct((requests, pick.shape[1], 128), bf16),
        ],
        compiler_params=params(14),
        cost_estimate=pl.CostEstimate(
            flops=requests * ATTENTION_COST,
            bytes_accessed=requests * 2**20,
            transcendentals=requests * 448 * 2112,
        ),
        name="attention",
    )(facts, own, other, cosine, sine, reach, pick, keys, values)


def attend(facts, kept_ref, stats_ref, got_ref, valid_ref):
    first = facts[0] == 0
    got = got_ref[...].astype(f32)
    theirs = got[:, 448:464] + got[:, 464:480] + got[:, 480:496]
    ours = stats_ref[:, :16]
    highest = jnp.maximum(ours, theirs)
    own_factor = jnp.exp(ours - highest)
    other_factor = jnp.exp(theirs - highest)
    both = own_factor + other_factor

    def spread(part):
        rows = part.shape[0]
        every = jnp.concatenate(
            [jnp.broadcast_to(part[:, g : g + 1], (rows, 128)) for g in range(GROUP)], 1
        )
        return jnp.where(first, every[:, :448], every[:, 448:])

    mixed = kept_ref[...] * spread(own_factor / both) + got[:, :448] * spread(other_factor / both)
    return mixed.astype(bf16) * valid_ref[...]


def combine_kernel(place, *refs):
    out_ref = refs[8]
    rows = out_ref.shape[0] // 2
    for h in range(2):
        out_ref[h * rows : (h + 1) * rows, :] = attend(place, *refs[4 * h : 4 * h + 4])


def combine(place, arrays):
    return pl.pallas_call(
        combine_kernel,
        out_shape=jax.ShapeDtypeStruct((2 * arrays[0].shape[0], 448), bf16),
        in_specs=[scalars()] + [whole()] * 8,
        out_specs=whole(),
        compiler_params=params(8),
        name="combine",
    )(place, *arrays)


def out_kernel(steps, place, att_ref, weight_hbm, *refs):
    outs, (weight_ref, arrival) = refs[: len(steps)], refs[len(steps) :]
    rows = att_ref.shape[0]
    copies = []
    for step in steps:
        for along in range(SIDE):
            block = lax.rem(place[3] + step, SIDE) * place[1] + along * place[2]
            slot = len(copies)
            copies.append(
                pltpu.make_async_copy(weight_hbm.at[block], weight_ref.at[slot], arrival.at[slot])
            )
            copies[slot].start()
    for slot, copy in enumerate(copies):
        copy.wait()
        out, along = outs[slot // SIDE], slot % SIDE
        terms = jnp.dot(att_ref[...], weight_ref[slot], preferred_element_type=f32)
        for t in range(3):
            out[along, t * rows : (t + 1) * rows, :] = terms[:, 128 * t : 128 * t + 128].astype(out.dtype)
        out[along, 3 * rows :, :] = folded(terms[:, 384:]).astype(out.dtype)


def out_terms(steps, place, attended, weights):
    rows = attended.shape[0] * 7 // 2
    return pl.pallas_call(
        functools.partial(out_kernel, steps),
        out_shape=[
            jax.ShapeDtypeStruct((SIDE, rows, 128), bf16 if step else f32) for step in steps
        ],
        in_specs=[scalars(), whole(), pl.BlockSpec(memory_space=pl.ANY)],
        out_specs=[whole()] * len(steps),
        scratch_shapes=[
            pltpu.VMEM((SIDE * len(steps),) + weights.shape[1:], bf16),
            pltpu.SemaphoreType.DMA((SIDE * len(steps),)),
        ],
        compiler_params=params(58),
        cost_estimate=pl.CostEstimate(flops=2 * 10**10, bytes_accessed=2 * 10**7, transcendentals=0),
        name="out_terms",
    )(place, attended, weights)


def partial_kernel(place, own_ref, *refs):
    got, outs = refs[:3], refs[3:]
    for step in range(SIDE):
        at = lax.rem(place[0] + step, SIDE)
        value = own_ref[at]
        for part in got:
            value = value + part[at].astype(f32)
        outs[step][...] = value.astype(outs[step].dtype)


def partial_sums(place, own, got):
    shape = own.shape[1:]
    return pl.pallas_call(
        partial_kernel,
        out_shape=[jax.ShapeDtypeStruct(shape, bf16 if step else f32) for step in range(SIDE)],
        in_specs=[scalars()] + [whole()] * 4,
        out_specs=[whole()] * SIDE,
        compiler_params=params(16),
        name="partial_sums",
    )(place, own, *got)


def final_kernel(hidden_ref, own_ref, *refs):
    got, out_ref = refs[:3], refs[3]
    rows = hidden_ref.shape[0]
    value = own_ref[...]
    for part in got:
        value = value + part[...].astype(f32)
    dense = jnp.concatenate(
        [value[t * rows : (t + 1) * rows] for t in range(3)] + [unfolded(value[3 * rows :])], 1
    )
    out_ref[...] = (hidden_ref[...].astype(f32) + dense).astype(bf16)


def final(hidden, parts):
    return pl.pallas_call(
        final_kernel,
        out_shape=jax.ShapeDtypeStruct(hidden.shape, bf16),
        in_specs=[whole()] * 5,
        out_specs=whole(),
        compiler_params=params(12),
        name="final",
    )(hidden, *parts)


def two_way(block):
    dp = lax.axis_index("dp")
    slots, order = [block, other_core(block)], [dp, dp ^ 1]
    up = down = block
    for step in range(1, 4):
        up, down = along_z(up, 1), along_z(down, -1)
        slots += [up, down, other_core(up), other_core(down)]
        order += [dp - 2 * step, dp + 2 * step, (dp ^ 1) - 2 * step, (dp ^ 1) + 2 * step]
    upper, lower = cut_blocks(up, down)
    halves = along_z(upper, 1), along_z(lower, -1)
    order += [dp + 8, (dp ^ 1) + 8]
    return slots, halves, (jnp.stack(order) % DP).astype(jnp.int32)


def shards(
    hidden_in,
    norm_gain,
    w_query,
    w_key,
    w_value,
    w_out,
    key_cache,
    value_cache,
    cache_len,
    tree_parent,
    valid_nodes,
    accepted_path,
    slot_owner,
):
    req_dev, tree_size, part_width = hidden_in.shape
    row_count = req_dev * tree_size
    head_dim = key_cache.shape[-1]
    half_len = key_cache.shape[3]
    dp, mp = lax.axis_index("dp"), lax.axis_index("mp")
    z, core = dp // CORES, dp % CORES
    x, y = mp // SIDE, mp % SIDE
    me_first, me_second = jnp.where(core == 0, y, x), jnp.where(core == 0, x, y)
    half_index = mp % 2
    hidden = hidden_in.reshape(row_count, part_width)

    packed, weights = pack(hidden, norm_gain[None], w_query, w_key, w_value.T)

    slots, halves, order = two_way(weights)

    gathered = lax.all_gather(packed, "mp")

    out_weights = lax.all_gather(w_out, "dp")
    strides = jnp.where(core == 0, jnp.array([1, SIDE]), jnp.array([SIDE, 1]))
    place = jnp.concatenate([half_index[None], strides, me_first[None]]).astype(jnp.int32)

    reach = tree_closure(tree_parent)
    depth = jnp.sum(reach, -1) - 1.0
    position = (cache_len[:, None].astype(f32) + depth).reshape(row_count, 1)
    half_dim = head_dim // 2
    inverse = jnp.exp(
        jnp.arange(half_dim, dtype=f32) * (-2.0 * math.log(rope_base) / head_dim)
    )
    angles = position * inverse
    cosine, sine = jnp.cos(angles), jnp.sin(angles)
    cosine = jnp.concatenate([cosine, cosine], -1)
    sine = jnp.concatenate([-sine, sine], -1)
    picks = accepted_path.shape[1]
    pick = (
        jnp.pad(accepted_path, ((0, 0), (0, 16 - picks)))[..., None]
        == jnp.arange(tree_size, dtype=jnp.int32)
    ).astype(bf16)
    counts = jnp.clip(cache_len - half_index * half_len, 0, half_len)
    valid = valid_nodes.reshape(row_count, 1).astype(bf16)

    normed = norm(gathered, row_count)
    furthest = join(*halves)
    total = project(0, True, order, normed, slots + [furthest, other_core(furthest)])

    half_rows = row_count // 2
    others = [partner(own) for own in total]
    arrays, chosen = [], []
    for half, own in enumerate(total):
        at = slice(half * half_rows, (half + 1) * half_rows)
        group = slice(half * req_dev // 2, (half + 1) * req_dev // 2)
        facts = jnp.concatenate([half_index[None], counts[group]]).astype(jnp.int32)
        kept, sent, stats, rows = attention(
            half, facts, own, others[half], cosine, sine, reach, pick,
            key_cache[:, 0, 0], value_cache[:, 0, 0],
        )
        chosen.append(rows)
        arrays += [kept, stats, partner(sent), valid[at]]
    attended = combine(place, arrays)
    two, one = out_terms((2, 1), place, attended, out_weights)
    three, here = out_terms((3, 0), place, attended, out_weights)
    got = [first_axis(two, 2), first_axis(one, 1), first_axis(three, 3)]
    mine = partial_sums(me_second[None].astype(jnp.int32), here, got)
    parts = [mine[0]] + [second_axis(mine[s], s) for s in (2, 1, 3)]
    layer_out = final(hidden, parts).reshape(req_dev, tree_size, part_width)

    rows = jnp.pad(jnp.concatenate(chosen), ((0, 0), (0, 80 - chosen[0].shape[1]), (0, 0)))
    every_row = lax.all_gather(rows, "dp", axis=0, tiled=True)[:, :picks]
    total_reqs = slot_owner.shape[0]
    my_slots = dp * req_dev + jnp.arange(req_dev, dtype=jnp.int32)
    senders = (slot_owner[None, :] == my_slots[:, None]).astype(bf16)
    accepted_kv = (
        jnp.dot(senders, every_row.reshape(total_reqs, -1), preferred_element_type=f32)
        .astype(bf16)
        .reshape(req_dev, picks, 2, -1)
    )
    return (layer_out, accepted_kv)


def solution(mesh):
    placed = (
        P("dp", None, "mp"),
        P("mp"),
        P("dp", "mp"),
        P("dp", "mp"),
        P("dp", "mp"),
        P("mp", "dp"),
        P("dp", "mp", None, None, None),
        P("dp", "mp", None, None, None),
        P("dp"),
        P("dp", None),
        P("dp", None),
        P("dp", None),
        P(),
    )
    return jax.shard_map(
        shards,
        mesh=mesh,
        in_specs=placed,
        out_specs=(P("dp", None, "mp"), P("dp", None, None, "mp")),
        check_vma=False,
    )
```

profile of v0, /device:TPU:6, one launch (start us, length us, event | category | flops | bytes accessed | tf_op | source)
XLA Modules:
  0.0 174.7 jit_solution(8107812722282629524)
XLA Ops:
  7.2 1.3 broadcast_in_dim.11.gain_ref
  8.5 1.6 copy.22.key_ref
  10.1 2.2 %pack.1 = (bf16[928,128]{1,0:T(8,128)(2,1)}, bf16[512,512]{1,0:T(8,128)(2,1)}) custom-call(bf16[256,448]{1,0:T(8,128)(2,1)} %bitcast.35, bf16[1,448]{1,0:T(2,128)(2,1)} %broadcast_in_dim.11.gain_ref, bf16[448,448]{1,0:T(8,128)(2,1)} %query_ref.1, bf16[448,64]{1,0:T(8,128)(2,1)} %copy.22.key_ref, bf16[64,448]{1,0:T(8,128)(2,1)} %bitcast.43), custom_call_target="tpu_custom_call" | custom-call | tf_op jit(solution)/shard_map/pack/pallas_call | solution.py:110
  12.4 2.0 %collective-permute-start.1 = (bf16[512,512]{1,0:T(8,128)(2,1)}, bf16[512,512]{1,0:T(8,128)(2,1)S(1)}, u32[]{:S(2)}, u32[]{:S(2)}) collective-permute-start(bf16[512,512]{1,0:T(8,128)(2,1)} %get-tuple-element.25.refs_0_), channel_id=1, source_target_pairs={{0,32},{1,33},{2,34},{3,35},{4,36},{5,37},{6,38},{7,39},{8,40},{9,... | collective-permute-start | bytes 1572872 | tf_op jit(solution)/shard_map/ppermute | solution.py:46
  14.4 4.0 %collective-permute-start.2 = (bf16[512,512]{1,0:T(8,128)(2,1)}, bf16[512,512]{1,0:T(8,128)(2,1)S(1)}, u32[]{:S(2)}, u32[]{:S(2)}) collective-permute-start(bf16[512,512]{1,0:T(8,128)(2,1)} %get-tuple-element.25.refs_0_), channel_id=1, source_target_pairs={{0,224},{1,225},{2,226},{3,227},{4,228},{5,229},{6,230},{7,231},{8... | collective-permute-start | bytes 1572872 | tf_op jit(solution)/shard_map/ppermute | solution.py:46
  18.5 0.7 fusion.31
  19.9 1.2 broadcast_select_fusion
  21.1 10.0 %collective-permute-done.1.refs_2_ = bf16[512,512]{1,0:T(8,128)(2,1)S(1)} collective-permute-done((bf16[512,512]{1,0:T(8,128)(2,1)}, bf16[512,512]{1,0:T(8,128)(2,1)S(1)}, u32[]{:S(2)}, u32[]{:S(2)}) %collective-permute-start.1) | collective-permute-done | bytes 524320 | tf_op jit(solution)/shard_map/ppermute | solution.py:46
  31.1 3.2 %collective-permute-start.6 = (bf16[512,512]{1,0:T(8,128)(2,1)S(1)}, bf16[512,512]{1,0:T(8,128)(2,1)S(1)}, u32[]{:S(2)}, u32[]{:S(2)}) collective-permute-start(bf16[512,512]{1,0:T(8,128)(2,1)S(1)} %collective-permute-done.2.refs_3_), channel_id=1, source_target_pairs={{0,224},{1,225},{2,226},{3,227},{4,228},{5,229},{6,230},{7,231},{8... | collective-permute-start | bytes 1572872 | tf_op jit(solution)/shard_map/ppermute | solution.py:46
  34.3 1.3 fusion.1
  35.9 10.1 %collective-permute-done.5.refs_6_ = bf16[512,512]{1,0:T(8,128)(2,1)S(1)} collective-permute-done((bf16[512,512]{1,0:T(8,128)(2,1)S(1)}, bf16[512,512]{1,0:T(8,128)(2,1)S(1)}, u32[]{:S(2)}, u32[]{:S(2)}) %collective-permute-start.5) | collective-permute-done | bytes 524320 | tf_op jit(solution)/shard_map/ppermute | solution.py:46
  46.1 3.2 %collective-permute-start.10 = (bf16[512,512]{1,0:T(8,128)(2,1)S(1)}, bf16[512,512]{1,0:T(8,128)(2,1)}, u32[]{:S(2)}, u32[]{:S(2)}) collective-permute-start(bf16[512,512]{1,0:T(8,128)(2,1)S(1)} %collective-permute-done.6.refs_7_), channel_id=1, source_target_pairs={{0,224},{1,225},{2,226},{3,227},{4,228},{5,229},{6,230},{7,231},{8... | collective-permute-start | bytes 1572872 | tf_op jit(solution)/shard_map/ppermute | solution.py:46
  50.3 9.9 %collective-permute-done.9.up_ref.refs_10_ = bf16[512,512]{1,0:T(8,128)(2,1)S(1)} collective-permute-done((bf16[512,512]{1,0:T(8,128)(2,1)S(1)}, bf16[512,512]{1,0:T(8,128)(2,1)S(1)}, u32[]{:S(2)}, u32[]{:S(2)}) %collective-permute-start.9) | collective-permute-done | bytes 524320 | tf_op jit(solution)/shard_map/ppermute | solution.py:46
  60.2 2.1 %cut_blocks.1 = (bf16[256,512]{1,0:T(8,128)(2,1)}, bf16[256,512]{1,0:T(8,128)(2,1)}) custom-call(bf16[512,512]{1,0:T(8,128)(2,1)S(1)} %collective-permute-done.9.up_ref.refs_10_, bf16[512,512]{1,0:T(8,128)(2,1)} %collective-permute-done.10.down_ref.refs_11_), custom_call_target="tpu_custom_call" | custom-call | flops 20000000000 | bytes 1000000 | tf_op jit(solution)/shard_map/cut_blocks/pallas_call | solution.py:148
  62.2 3.2 %collective-permute-start.14 = (bf16[256,512]{1,0:T(8,128)(2,1)}, bf16[256,512]{1,0:T(8,128)(2,1)S(1)}, u32[]{:S(2)}, u32[]{:S(2)}) collective-permute-start(bf16[256,512]{1,0:T(8,128)(2,1)} %get-tuple-element.27), channel_id=1, source_target_pairs={{0,224},{1,225},{2,226},{3,227},{4,228},{5,229},{6,230},{7,231},{8... | collective-permute-start | bytes 786440 | tf_op jit(solution)/shard_map/ppermute | solution.py:46
  67.4 2.7 %collective-permute-done.13.upper_ref = bf16[256,512]{1,0:T(8,128)(2,1)S(1)} collective-permute-done((bf16[256,512]{1,0:T(8,128)(2,1)}, bf16[256,512]{1,0:T(8,128)(2,1)S(1)}, u32[]{:S(2)}, u32[]{:S(2)}) %collective-permute-start.13) | collective-permute-done | bytes 262176 | tf_op jit(solution)/shard_map/ppermute | solution.py:46
  71.4 0.9 copy-done.7
  74.0 2.0 %fusion.18 = (f32[256,64]{1,0:T(8,128)}, f32[256,64]{1,0:T(8,128)}, f32[256,64]{1,0:T(8,128)}) fusion(f32[64]{0:T(128)} %multiply_exponential_fusion, f32[256]{0:T(256)S(1)} %add.106), kind=kLoop, calls=%fused_computation.29 | loop fusion | flops 32768 | bytes 197888 | tf_op jit(solution)/shard_map/neg | solution.py:567
  75.9 2.1 %copy-done = bf16[14848,128]{1,0:T(8,128)(2,1)S(1)} copy-done((bf16[14848,128]{1,0:T(8,128)(2,1)S(1)}, bf16[14848,128]{1,0:T(8,128)(2,1)}, u32[]{:S(2)}) %copy-start) | copy-done | bytes 3801112
  78.0 1.8 %norm.1.normed_ref = bf16[16,256,448]{2,1,0:T(8,128)(2,1)S(1)} custom-call(bf16[16,928,128]{2,1,0:T(8,128)(2,1)S(1)} %bitcast.34), custom_call_target="tpu_custom_call" | custom-call | flops 10000000 | bytes 8000000 | tf_op jit(solution)/shard_map/norm/pallas_call | solution.py:200
  79.9 6.2 %project.1 = (bf16[128,576]{1,0:T(8,128)(2,1)}, bf16[128,576]{1,0:T(8,128)(2,1)S(1)}) custom-call(s32[16]{0:T(128)S(1)} %and_select_fusion.order, bf16[16,256,448]{2,1,0:T(8,128)(2,1)S(1)} %norm.1.normed_ref, bf16[512,512]{1,0:T(8,128)(2,1)S(1)} %copy-done.3, bf16[512,512]{1,0:T(8,128)(2,1)S(1)} %collective-permute-done.refs_1_, ...), custom_call_target="tpu_custom_call" | custom-call | flops 2113929216 | bytes 16000000 | tf_op jit(solution)/shard_map/project/pallas_call | solution.py:245
  86.1 1.6 collective-permute-start.16
  87.8 1.2 pad_maximum_fusion
  89.6 3.8 %collective-permute-done.16.oth_ref = bf16[128,576]{1,0:T(8,128)(2,1)S(1)} collective-permute-done((bf16[128,576]{1,0:T(8,128)(2,1)}, bf16[128,576]{1,0:T(8,128)(2,1)S(1)}, u32[]{:S(2)}, u32[]{:S(2)}) %collective-permute-start.16) | collective-permute-done | bytes 147488 | tf_op jit(solution)/shard_map/ppermute | solution.py:46
  93.4 1.6 copy-done.10
  95.0 1.6 copy-done.11
  96.6 7.0 %attention.2 = (f32[128,448]{1,0:T(8,128)S(1)}, bf16[128,512]{1,0:T(8,128)(2,1)S(1)}, f32[128,128]{1,0:T(8,128)S(1)}, bf16[2,16,128]{2,1,0:T(8,128)(2,1)S(1)}) custom-call(s32[3]{0:T(128)S(1)} %pad_add_fusion.1.facts, bf16[128,576]{1,0:T(8,128)(2,1)} %get-tuple-element.28.own_ref, bf16[128,576]{1,0:T(8,128)(2,1)S(1)} %collective-permute-done.16.oth_ref, ...), custom_call_target="tpu_custom_call" | custom-call | flops 49999998976 | bytes 2097152 | tf_op jit(solution)/shard_map/attention/pallas_call | solution.py:354
  103.7 1.6 collective-permute-start.17
  105.3 6.1 %attention.3 = (f32[128,448]{1,0:T(8,128)S(1)}, bf16[128,512]{1,0:T(8,128)(2,1)S(1)}, f32[128,128]{1,0:T(8,128)S(1)}, bf16[2,16,128]{2,1,0:T(8,128)(2,1)S(1)}) custom-call(s32[3]{0:T(128)S(1)} %pad_add_fusion.2.facts, bf16[128,576]{1,0:T(8,128)(2,1)S(1)} %get-tuple-element.32.own_ref, bf16[128,576]{1,0:T(8,128)(2,1)S(1)} %collective-permute-done.18.oth_ref, ...), custom_call_target="tpu_custom_call" | custom-call | flops 49999998976 | bytes 2097152 | tf_op jit(solution)/shard_map/attention/pallas_call | solution.py:354
  111.5 0.8 collective-permute-start.19
  113.3 3.4 %collective-permute-done.19.refs_6_ = bf16[128,512]{1,0:T(8,128)(2,1)S(1)} collective-permute-done((bf16[128,512]{1,0:T(8,128)(2,1)S(1)}, bf16[128,512]{1,0:T(8,128)(2,1)S(1)}, u32[]{:S(2)}, u32[]{:S(2)}) %collective-permute-start.19) | collective-permute-done | bytes 131104 | tf_op jit(solution)/shard_map/ppermute | solution.py:46
  116.7 2.3 %combine.1.att_ref = bf16[256,448]{1,0:T(8,128)(2,1)S(1)} custom-call(s32[4]{0:T(128)S(1)} %pad_add_fusion.place, f32[128,448]{1,0:T(8,128)S(1)} %get-tuple-element.29.refs_0_, f32[128,128]{1,0:T(8,128)S(1)} %get-tuple-element.30.refs_1_, bf16[128,512]{1,0:T(8,128)(2,1)S(1)} %collective-permute-done.17.refs_2_, bf16[128,1]{1,0:T(8,128)(2,1)S(1)} %slice.28.refs_3_, ...), custom_call_target="tpu_custom_call" | custom-call | tf_op jit(solution)/shard_map/combine/pallas_call | solution.py:412
  119.8 2.9 %all-gather.10.cloned.1.call-done = bf16[7168,448]{1,0:T(8,128)(2,1)} async-done(((bf16[448,448]{1,0:T(8,128)(2,1)}), bf16[7168,448]{1,0:T(8,128)(2,1)}) %all-gather.10.cloned.1.call-update) | async-done | bytes 6422544 | tf_op jit(solution)/shard_map/all_gather | solution.py:553
  122.7 6.0 %out_terms.3 = (bf16[4,896,128]{2,1,0:T(8,128)(2,1)}, bf16[4,896,128]{2,1,0:T(8,128)(2,1)}) custom-call(s32[4]{0:T(128)} %copy-done.9, bf16[256,448]{1,0:T(8,128)(2,1)} %copy-done.8, bf16[16,448,448]{2,1,0:T(8,128)(2,1)} %bitcast.44), custom_call_target="tpu_custom_call" | custom-call | flops 20000000000 | bytes 20000000 | tf_op jit(solution)/shard_map/out_terms/pallas_call | solution.py:445
  128.6 3.1 %collective-permute-start.20 = (bf16[4,896,128]{2,1,0:T(8,128)(2,1)}, bf16[4,896,128]{2,1,0:T(8,128)(2,1)S(1)}, u32[]{:S(2)}, u32[]{:S(2)}) collective-permute-start(bf16[4,896,128]{2,1,0:T(8,128)(2,1)} %get-tuple-element.37), channel_id=1, source_target_pairs={{0,2},{1,3},{2,0},{3,1},{4,6},{5,7},{6,4},{7,5},{8,10},{9,11},{10,... | collective-permute-start | bytes 2752520 | tf_op jit(solution)/shard_map/ppermute | solution.py:46
  131.7 6.3 %out_terms.2 = (bf16[4,896,128]{2,1,0:T(8,128)(2,1)}, f32[4,896,128]{2,1,0:T(8,128)}) custom-call(s32[4]{0:T(128)} %copy-done.9, bf16[256,448]{1,0:T(8,128)(2,1)} %copy-done.8, bf16[16,448,448]{2,1,0:T(8,128)(2,1)} %bitcast.45), custom_call_target="tpu_custom_call" | custom-call | flops 20000000000 | bytes 20000000 | tf_op jit(solution)/shard_map/out_terms/pallas_call | solution.py:445
  138.7 2.7 %collective-permute-start.22 = (bf16[4,896,128]{2,1,0:T(8,128)(2,1)}, bf16[4,896,128]{2,1,0:T(8,128)(2,1)S(1)}, u32[]{:S(2)}, u32[]{:S(2)}) collective-permute-start(bf16[4,896,128]{2,1,0:T(8,128)(2,1)} %get-tuple-element.39), channel_id=1, source_target_pairs={{0,3},{1,0},{2,1},{3,2},{4,7},{5,4},{6,5},{7,6},{8,11},{9,8},{10,9... | collective-permute-start | bytes 2752520 | tf_op jit(solution)/shard_map/ppermute | solution.py:46
  141.4 2.5 %collective-permute-done.20.refs_0_ = bf16[4,896,128]{2,1,0:T(8,128)(2,1)S(1)} collective-permute-done((bf16[4,896,128]{2,1,0:T(8,128)(2,1)}, bf16[4,896,128]{2,1,0:T(8,128)(2,1)S(1)}, u32[]{:S(2)}, u32[]{:S(2)}) %collective-permute-start.20) | collective-permute-done | bytes 917536 | tf_op jit(solution)/shard_map/ppermute | solution.py:46
  143.9 9.8 %collective-permute-done.21.refs_1_ = bf16[4,896,128]{2,1,0:T(8,128)(2,1)S(1)} collective-permute-done((bf16[4,896,128]{2,1,0:T(8,128)(2,1)}, bf16[4,896,128]{2,1,0:T(8,128)(2,1)S(1)}, u32[]{:S(2)}, u32[]{:S(2)}) %collective-permute-start.21) | collective-permute-done | bytes 917536 | tf_op jit(solution)/shard_map/ppermute | solution.py:46
  153.7 1.5 copy-done.1
  155.3 1.1 partial_sums.1
  156.3 1.5 collective-permute-start.23
  157.8 2.1 %collective-permute-start.24 = (bf16[896,128]{1,0:T(8,128)(2,1)}, bf16[896,128]{1,0:T(8,128)(2,1)S(1)}, u32[]{:S(2)}, u32[]{:S(2)}) collective-permute-start(bf16[896,128]{1,0:T(8,128)(2,1)} %get-tuple-element.42), channel_id=1, source_target_pairs={{0,4},{1,5},{2,6},{3,7},{4,8},{5,9},{6,10},{7,11},{8,12},{9,13},{1... | collective-permute-start | bytes 688136 | tf_op jit(solution)/shard_map/ppermute | solution.py:46
  159.9 2.2 %all-gather.6.cloned.1.call-done = bf16[64,80,128]{2,1,0:T(8,128)(2,1)} async-done(((bf16[4,80,128]{2,1,0:T(8,128)(2,1)}), bf16[64,80,128]{2,1,0:T(8,128)(2,1)}) %all-gather.6.cloned.1.call-update) | async-done | bytes 1310736 | tf_op jit(solution)/shard_map/all_gather | solution.py:602
  162.0 0.9 slice.30
  163.2 0.7 reshape.73
  164.4 2.9 %collective-permute-done.25.refs_2_ = bf16[896,128]{1,0:T(8,128)(2,1)S(1)} collective-permute-done((bf16[896,128]{1,0:T(8,128)(2,1)}, bf16[896,128]{1,0:T(8,128)(2,1)S(1)}, u32[]{:S(2)}, u32[]{:S(2)}) %collective-permute-start.25) | collective-permute-done | bytes 229408 | tf_op jit(solution)/shard_map/ppermute | solution.py:46
  167.3 0.9 final.1
  (89 shorter events, 10.9 us)
Async XLA Ops:
  7.2 68.8 %all-gather.8.cloned.1.call-start = ((), (), s32[]{:S(2)}) async-start(), calls=%async_computation.1 | async-start | bytes 4038656 | tf_op jit(solution)/shard_map/all_gather | solution.py:551
  12.3 110.4 %all-gather.10.cloned.1.call-start = ((), (), s32[]{:S(2)}) async-start(), calls=%async_computation.2 | async-start | bytes 7798784 | tf_op jit(solution)/shard_map/all_gather | solution.py:553
  12.3 60.0 %collective-permute-start = (bf16[512,512]{1,0:T(8,128)(2,1)}, bf16[512,512]{1,0:T(8,128)(2,1)S(1)}, u32[]{:S(2)}, u32[]{:S(2)}) collective-permute-start(bf16[512,512]{1,0:T(8,128)(2,1)} %get-tuple-element.25.refs_0_), channel_id=1, source_target_pairs={{0,16},{1,17},{2,18},{3,19},{4,20},{5,21},{6,22},{7,23},{8,24},{9,... | collective-permute-start | bytes 1572872 | tf_op jit(solution)/shard_map/ppermute | solution.py:46
  12.4 18.6 %collective-permute-start.1 = (bf16[512,512]{1,0:T(8,128)(2,1)}, bf16[512,512]{1,0:T(8,128)(2,1)S(1)}, u32[]{:S(2)}, u32[]{:S(2)}) collective-permute-start(bf16[512,512]{1,0:T(8,128)(2,1)} %get-tuple-element.25.refs_0_), channel_id=1, source_target_pairs={{0,32},{1,33},{2,34},{3,35},{4,36},{5,37},{6,38},{7,39},{8,40},{9,... | collective-permute-start | bytes 1572872 | tf_op jit(solution)/shard_map/ppermute | solution.py:46
  14.4 16.7 %collective-permute-start.2 = (bf16[512,512]{1,0:T(8,128)(2,1)}, bf16[512,512]{1,0:T(8,128)(2,1)S(1)}, u32[]{:S(2)}, u32[]{:S(2)}) collective-permute-start(bf16[512,512]{1,0:T(8,128)(2,1)} %get-tuple-element.25.refs_0_), channel_id=1, source_target_pairs={{0,224},{1,225},{2,226},{3,227},{4,228},{5,229},{6,230},{7,231},{8... | collective-permute-start | bytes 1572872 | tf_op jit(solution)/shard_map/ppermute | solution.py:46
  18.5 143.6 %all-gather.6.cloned.1.call-start = ((), (), s32[]{:S(2)}) async-start(), calls=%async_computation | async-start | bytes 1392640 | tf_op jit(solution)/shard_map/all_gather | solution.py:602
  31.1 15.0 %collective-permute-start.5 = (bf16[512,512]{1,0:T(8,128)(2,1)S(1)}, bf16[512,512]{1,0:T(8,128)(2,1)S(1)}, u32[]{:S(2)}, u32[]{:S(2)}) collective-permute-start(bf16[512,512]{1,0:T(8,128)(2,1)S(1)} %collective-permute-done.1.refs_2_), channel_id=1, source_target_pairs={{0,32},{1,33},{2,34},{3,35},{4,36},{5,37},{6,38},{7,39},{8,40},{9,... | collective-permute-start | bytes 1572872 | tf_op jit(solution)/shard_map/ppermute | solution.py:46
  31.1 15.0 %collective-permute-start.6 = (bf16[512,512]{1,0:T(8,128)(2,1)S(1)}, bf16[512,512]{1,0:T(8,128)(2,1)S(1)}, u32[]{:S(2)}, u32[]{:S(2)}) collective-permute-start(bf16[512,512]{1,0:T(8,128)(2,1)S(1)} %collective-permute-done.2.refs_3_), channel_id=1, source_target_pairs={{0,224},{1,225},{2,226},{3,227},{4,228},{5,229},{6,230},{7,231},{8... | collective-permute-start | bytes 1572872 | tf_op jit(solution)/shard_map/ppermute | solution.py:46
  46.0 14.1 %collective-permute-start.9 = (bf16[512,512]{1,0:T(8,128)(2,1)S(1)}, bf16[512,512]{1,0:T(8,128)(2,1)S(1)}, u32[]{:S(2)}, u32[]{:S(2)}) collective-permute-start(bf16[512,512]{1,0:T(8,128)(2,1)S(1)} %collective-permute-done.5.refs_6_), channel_id=1, source_target_pairs={{0,32},{1,33},{2,34},{3,35},{4,36},{5,37},{6,38},{7,39},{8,40},{9,... | collective-permute-start | bytes 1572872 | tf_op jit(solution)/shard_map/ppermute | solution.py:46
  46.1 14.1 %collective-permute-start.10 = (bf16[512,512]{1,0:T(8,128)(2,1)S(1)}, bf16[512,512]{1,0:T(8,128)(2,1)}, u32[]{:S(2)}, u32[]{:S(2)}) collective-permute-start(bf16[512,512]{1,0:T(8,128)(2,1)S(1)} %collective-permute-done.6.refs_7_), channel_id=1, source_target_pairs={{0,224},{1,225},{2,226},{3,227},{4,228},{5,229},{6,230},{7,231},{8... | collective-permute-start | bytes 1572872 | tf_op jit(solution)/shard_map/ppermute | solution.py:46
  49.8 17.1 %copy-start.13 = (s32[4,64]{1,0:T(4,128)S(1)}, s32[4,64]{1,0:T(4,128)}, u32[]{:S(2)}) copy-start(s32[4,64]{1,0:T(4,128)} %param.25) | copy-start | bytes 3076
  49.8 22.7 %collective-permute-start.3 = (bf16[512,512]{1,0:T(8,128)(2,1)S(1)}, bf16[512,512]{1,0:T(8,128)(2,1)}, u32[]{:S(2)}, u32[]{:S(2)}) collective-permute-start(bf16[512,512]{1,0:T(8,128)(2,1)S(1)} %collective-permute-done.1.refs_2_), channel_id=1, source_target_pairs={{0,16},{1,17},{2,18},{3,19},{4,20},{5,21},{6,22},{7,23},{8,24},{9,... | collective-permute-start | bytes 1572872 | tf_op jit(solution)/shard_map/ppermute | solution.py:46
  49.8 23.1 %collective-permute-start.4 = (bf16[512,512]{1,0:T(8,128)(2,1)S(1)}, bf16[512,512]{1,0:T(8,128)(2,1)}, u32[]{:S(2)}, u32[]{:S(2)}) collective-permute-start(bf16[512,512]{1,0:T(8,128)(2,1)S(1)} %collective-permute-done.2.refs_3_), channel_id=1, source_target_pairs={{0,16},{1,17},{2,18},{3,19},{4,20},{5,21},{6,22},{7,23},{8,24},{9,... | collective-permute-start | bytes 1572872 | tf_op jit(solution)/shard_map/ppermute | solution.py:46
  60.2 2.1 %copy-start.4 = (bf16[512,512]{1,0:T(8,128)(2,1)}, bf16[512,512]{1,0:T(8,128)(2,1)S(1)}, u32[]{:S(2)}) copy-start(bf16[512,512]{1,0:T(8,128)(2,1)S(1)} %collective-permute-done.9.up_ref.refs_10_) | copy-start | bytes 1572868
  62.2 7.9 %collective-permute-start.13 = (bf16[256,512]{1,0:T(8,128)(2,1)}, bf16[256,512]{1,0:T(8,128)(2,1)S(1)}, u32[]{:S(2)}, u32[]{:S(2)}) collective-permute-start(bf16[256,512]{1,0:T(8,128)(2,1)} %get-tuple-element.26), channel_id=1, source_target_pairs={{0,32},{1,33},{2,34},{3,35},{4,36},{5,37},{6,38},{7,39},{8,40},{9,... | collective-permute-start | bytes 786440 | tf_op jit(solution)/shard_map/ppermute | solution.py:46
  62.2 7.9 %collective-permute-start.14 = (bf16[256,512]{1,0:T(8,128)(2,1)}, bf16[256,512]{1,0:T(8,128)(2,1)S(1)}, u32[]{:S(2)}, u32[]{:S(2)}) collective-permute-start(bf16[256,512]{1,0:T(8,128)(2,1)} %get-tuple-element.27), channel_id=1, source_target_pairs={{0,224},{1,225},{2,226},{3,227},{4,228},{5,229},{6,230},{7,231},{8... | collective-permute-start | bytes 786440 | tf_op jit(solution)/shard_map/ppermute | solution.py:46
  70.1 9.7 %collective-permute-start.7 = (bf16[512,512]{1,0:T(8,128)(2,1)S(1)}, bf16[512,512]{1,0:T(8,128)(2,1)}, u32[]{:S(2)}, u32[]{:S(2)}) collective-permute-start(bf16[512,512]{1,0:T(8,128)(2,1)S(1)} %collective-permute-done.5.refs_6_), channel_id=1, source_target_pairs={{0,16},{1,17},{2,18},{3,19},{4,20},{5,21},{6,22},{7,23},{8,24},{9,... | collective-permute-start | bytes 1572872 | tf_op jit(solution)/shard_map/ppermute | solution.py:46
  70.2 0.7 copy-start.6
  70.9 9.0 %collective-permute-start.8 = (bf16[512,512]{1,0:T(8,128)(2,1)S(1)}, bf16[512,512]{1,0:T(8,128)(2,1)}, u32[]{:S(2)}, u32[]{:S(2)}) collective-permute-start(bf16[512,512]{1,0:T(8,128)(2,1)S(1)} %collective-permute-done.6.refs_7_), channel_id=1, source_target_pairs={{0,16},{1,17},{2,18},{3,19},{4,20},{5,21},{6,22},{7,23},{8,24},{9,... | collective-permute-start | bytes 1572872 | tf_op jit(solution)/shard_map/ppermute | solution.py:46
  71.4 0.9 copy-start.7
  72.4 7.5 %collective-permute-start.11 = (bf16[512,512]{1,0:T(8,128)(2,1)}, bf16[512,512]{1,0:T(8,128)(2,1)}, u32[]{:S(2)}, u32[]{:S(2)}) collective-permute-start(bf16[512,512]{1,0:T(8,128)(2,1)} %copy-done.4), channel_id=1, source_target_pairs={{0,16},{1,17},{2,18},{3,19},{4,20},{5,21},{6,22},{7,23},{8,24},{9,... | collective-permute-start | bytes 1572872 | tf_op jit(solution)/shard_map/ppermute | solution.py:46
  72.5 7.4 %collective-permute-start.12 = (bf16[512,512]{1,0:T(8,128)(2,1)}, bf16[512,512]{1,0:T(8,128)(2,1)}, u32[]{:S(2)}, u32[]{:S(2)}) collective-permute-start(bf16[512,512]{1,0:T(8,128)(2,1)} %collective-permute-done.10.down_ref.refs_11_), channel_id=1, source_target_pairs={{0,16},{1,17},{2,18},{3,19},{4,20},{5,21},{6,22},{7,23},{8,24},{9,... | collective-permute-start | bytes 1572872 | tf_op jit(solution)/shard_map/ppermute | solution.py:46
  73.0 6.9 %collective-permute-start.15 = (bf16[512,512]{1,0:T(8,128)(2,1)S(1)}, bf16[512,512]{1,0:T(8,128)(2,1)}, u32[]{:S(2)}, u32[]{:S(2)}) collective-permute-start(bf16[512,512]{1,0:T(8,128)(2,1)S(1)} %join.1.refs_14_), channel_id=1, source_target_pairs={{0,16},{1,17},{2,18},{3,19},{4,20},{5,21},{6,22},{7,23},{8,24},{9,... | collective-permute-start | bytes 1572872 | tf_op jit(solution)/shard_map/ppermute | solution.py:46
  75.9 2.1 %copy-start = (bf16[14848,128]{1,0:T(8,128)(2,1)S(1)}, bf16[14848,128]{1,0:T(8,128)(2,1)}, u32[]{:S(2)}) copy-start(bf16[14848,128]{1,0:T(8,128)(2,1)} %all-gather.8.cloned.1.call-done) | copy-start | bytes 11403268
  78.0 1.9 %copy-start.3 = (bf16[512,512]{1,0:T(8,128)(2,1)S(1)}, bf16[512,512]{1,0:T(8,128)(2,1)}, u32[]{:S(2)}) copy-start(bf16[512,512]{1,0:T(8,128)(2,1)} %get-tuple-element.25.refs_0_) | copy-start | bytes 1572868
  78.0 1.9 %copy-start.5 = (bf16[512,512]{1,0:T(8,128)(2,1)S(1)}, bf16[512,512]{1,0:T(8,128)(2,1)}, u32[]{:S(2)}) copy-start(bf16[512,512]{1,0:T(8,128)(2,1)} %copy-done.4) | copy-start | bytes 1572868
  79.8 7.9 %copy-start.15 = (s32[2]{0:T(128)S(1)}, s32[2]{0:T(128)}, u32[]{:S(2)}) copy-start(s32[2]{0:T(128)} %get-tuple-element.51) | copy-start | bytes 28
  86.1 7.2 %collective-permute-start.16 = (bf16[128,576]{1,0:T(8,128)(2,1)}, bf16[128,576]{1,0:T(8,128)(2,1)S(1)}, u32[]{:S(2)}, u32[]{:S(2)}) collective-permute-start(bf16[128,576]{1,0:T(8,128)(2,1)} %get-tuple-element.28.own_ref), channel_id=1, source_target_pairs={{0,1},{1,0},{2,3},{3,2},{4,5},{5,4},{6,7},{7,6},{8,9},{9,8},{10,11... | collective-permute-start | bytes 442376 | tf_op jit(solution)/shard_map/ppermute | solution.py:46
  89.0 16.3 %collective-permute-start.18 = (bf16[128,576]{1,0:T(8,128)(2,1)S(1)}, bf16[128,576]{1,0:T(8,128)(2,1)S(1)}, u32[]{:S(2)}, u32[]{:S(2)}) collective-permute-start(bf16[128,576]{1,0:T(8,128)(2,1)S(1)} %get-tuple-element.32.own_ref), channel_id=1, source_target_pairs={{0,1},{1,0},{2,3},{3,2},{4,5},{5,4},{6,7},{7,6},{8,9},{9,8},{10,11... | collective-permute-start | bytes 442376 | tf_op jit(solution)/shard_map/ppermute | solution.py:46
  93.4 1.7 copy-start.10
  95.0 1.6 copy-start.11
  103.7 8.6 %copy-start.14 = (s32[2]{0:T(128)S(1)}, s32[2]{0:T(128)}, u32[]{:S(2)}) copy-start(s32[2]{0:T(128)} %broadcast_select_fusion) | copy-start | bytes 28
  103.7 8.6 %copy-start.12 = (bf16[2,64]{1,0:T(2,128)(2,1)S(1)}, bf16[2,64]{1,0:T(2,128)(2,1)}, u32[]{:S(2)}) copy-start(bf16[2,64]{1,0:T(2,128)(2,1)} %get-tuple-element.50) | copy-start | bytes 772
  103.7 9.6 %collective-permute-start.17 = (bf16[128,512]{1,0:T(8,128)(2,1)S(1)}, bf16[128,512]{1,0:T(8,128)(2,1)S(1)}, u32[]{:S(2)}, u32[]{:S(2)}) collective-permute-start(bf16[128,512]{1,0:T(8,128)(2,1)S(1)} %get-tuple-element.31), channel_id=1, source_target_pairs={{0,1},{1,0},{2,3},{3,2},{4,5},{5,4},{6,7},{7,6},{8,9},{9,8},{10,11... | collective-permute-start | bytes 393224 | tf_op jit(solution)/shard_map/ppermute | solution.py:46
  111.5 5.3 %collective-permute-start.19 = (bf16[128,512]{1,0:T(8,128)(2,1)S(1)}, bf16[128,512]{1,0:T(8,128)(2,1)S(1)}, u32[]{:S(2)}, u32[]{:S(2)}) collective-permute-start(bf16[128,512]{1,0:T(8,128)(2,1)S(1)} %get-tuple-element.35), channel_id=1, source_target_pairs={{0,1},{1,0},{2,3},{3,2},{4,5},{5,4},{6,7},{7,6},{8,9},{9,8},{10,11... | collective-permute-start | bytes 393224 | tf_op jit(solution)/shard_map/ppermute | solution.py:46
  112.3 10.4 %copy-start.9 = (s32[4]{0:T(128)}, s32[4]{0:T(128)S(1)}, u32[]{:S(2)}) copy-start(s32[4]{0:T(128)S(1)} %pad_add_fusion.place) | copy-start | bytes 52
  119.1 0.7 copy-start.8
  128.6 15.3 %collective-permute-start.20 = (bf16[4,896,128]{2,1,0:T(8,128)(2,1)}, bf16[4,896,128]{2,1,0:T(8,128)(2,1)S(1)}, u32[]{:S(2)}, u32[]{:S(2)}) collective-permute-start(bf16[4,896,128]{2,1,0:T(8,128)(2,1)} %get-tuple-element.37), channel_id=1, source_target_pairs={{0,2},{1,3},{2,0},{3,1},{4,6},{5,7},{6,4},{7,5},{8,10},{9,11},{10,... | collective-permute-start | bytes 2752520 | tf_op jit(solution)/shard_map/ppermute | solution.py:46
  138.1 15.6 %collective-permute-start.21 = (bf16[4,896,128]{2,1,0:T(8,128)(2,1)}, bf16[4,896,128]{2,1,0:T(8,128)(2,1)S(1)}, u32[]{:S(2)}, u32[]{:S(2)}) collective-permute-start(bf16[4,896,128]{2,1,0:T(8,128)(2,1)} %get-tuple-element.38), channel_id=1, source_target_pairs={{0,1},{1,2},{2,3},{3,0},{4,5},{5,6},{6,7},{7,4},{8,9},{9,10},{10,1... | collective-permute-start | bytes 2752520 | tf_op jit(solution)/shard_map/ppermute | solution.py:46
  138.7 15.0 %collective-permute-start.22 = (bf16[4,896,128]{2,1,0:T(8,128)(2,1)}, bf16[4,896,128]{2,1,0:T(8,128)(2,1)S(1)}, u32[]{:S(2)}, u32[]{:S(2)}) collective-permute-start(bf16[4,896,128]{2,1,0:T(8,128)(2,1)} %get-tuple-element.39), channel_id=1, source_target_pairs={{0,3},{1,0},{2,1},{3,2},{4,7},{5,4},{6,5},{7,6},{8,11},{9,8},{10,9... | collective-permute-start | bytes 2752520 | tf_op jit(solution)/shard_map/ppermute | solution.py:46
  153.7 1.5 copy-start.1
  155.3 7.7 %copy-start.16 = (s32[64]{0:T(128)S(1)}, s32[64]{0:T(128)}, u32[]{:S(2)}) copy-start(s32[64]{0:T(128)} %param.27) | copy-start | bytes 772
  155.3 12.0 %copy-start.2 = (bf16[4,64,448]{2,1,0:T(8,128)(2,1)S(1)}, bf16[4,64,448]{2,1,0:T(8,128)(2,1)}, u32[]{:S(2)}) copy-start(bf16[4,64,448]{2,1,0:T(8,128)(2,1)} %param.15) | copy-start | bytes 688132
  156.3 7.7 %collective-permute-start.23 = (bf16[896,128]{1,0:T(8,128)(2,1)}, bf16[896,128]{1,0:T(8,128)(2,1)S(1)}, u32[]{:S(2)}, u32[]{:S(2)}) collective-permute-start(bf16[896,128]{1,0:T(8,128)(2,1)} %get-tuple-element.41), channel_id=1, source_target_pairs={{0,8},{1,9},{2,10},{3,11},{4,12},{5,13},{6,14},{7,15},{8,0},{9,1},... | collective-permute-start | bytes 688136 | tf_op jit(solution)/shard_map/ppermute | solution.py:46
  157.8 6.6 %collective-permute-start.24 = (bf16[896,128]{1,0:T(8,128)(2,1)}, bf16[896,128]{1,0:T(8,128)(2,1)S(1)}, u32[]{:S(2)}, u32[]{:S(2)}) collective-permute-start(bf16[896,128]{1,0:T(8,128)(2,1)} %get-tuple-element.42), channel_id=1, source_target_pairs={{0,4},{1,5},{2,6},{3,7},{4,8},{5,9},{6,10},{7,11},{8,12},{9,13},{1... | collective-permute-start | bytes 688136 | tf_op jit(solution)/shard_map/ppermute | solution.py:46
  159.9 7.4 %collective-permute-start.25 = (bf16[896,128]{1,0:T(8,128)(2,1)}, bf16[896,128]{1,0:T(8,128)(2,1)S(1)}, u32[]{:S(2)}, u32[]{:S(2)}) collective-permute-start(bf16[896,128]{1,0:T(8,128)(2,1)} %get-tuple-element.43), channel_id=1, source_target_pairs={{0,12},{1,13},{2,14},{3,15},{4,0},{5,1},{6,2},{7,3},{8,4},{9,5},{1... | collective-permute-start | bytes 688136 | tf_op jit(solution)/shard_map/ppermute | solution.py:46
Sparse Core Ops, SparseCore 0:
  12.4 57.6 all-gather.7
  71.9 50.7 all-gather.9
  124.5 37.4 all-gather.5
where the time goes:
time: 175 us
  waiting for transfers between devices  60.9 us (35%)
  Pallas kernels  42 us (24%)
  starting transfers between devices  32.3 us (18%)
  local copies, waits for them, and re-layouts  16 us (9%)
  between operations  14 us (8%)
  other arithmetic  7.29 us (4%)
  matrix products  2.17 us (1%)
    ppermute x26, waiting for transfers between devices, moved(): return lax.ppermute(block, ('dp', 'mp'), route)  55.8 us
    ppermute x26, starting transfers between devices, moved(): return lax.ppermute(block, ('dp', 'mp'), route)  32.2 us
    pallas_call x2, Pallas kernels, attention(): pl.pallas_call(attention_kernel, grid_spec=pltpu.PrefetchScalarGridSpec(n...  13.1 us
    pallas_call x2, Pallas kernels, out_terms(): pl.pallas_call(functools.partial(out_kernel, steps), out_shape=[jax.Shape...  12.3 us
    unnamed x35, local copies, waits for them, and re-layouts  10.8 us
    pallas_call x1, Pallas kernels, project(): pl.pallas_call(functools.partial(project_kernel, count, start, last), out...  6.22 us
  transfers between devices with their start and end apart: 29, of which 14 were waited for; matrix products, arithmetic and copies ran while one was open for 8% of the time, Pallas kernels for 22%

commit v1 on v0

--- a/solution.py
+++ b/solution.py
@@ -90,34 +90,47 @@
     return jnp.concatenate([wide[:half], wide[half:]], 1).astype(array.dtype)
 
 
-def pack_kernel(hidden_ref, gain_ref, query_ref, key_ref, value_ref, x_ref, w_ref):
+def pack_kernel(hidden_ref, gain_ref, x_ref):
     rows = hidden_ref.shape[0]
-    w_ref[:448, :384] = query_ref[:, :384]
-    w_ref[:448, 384:] = jnp.concatenate(
-        [query_ref[:, 384:448].astype(f32), key_ref[...].astype(f32)], 1
-    ).astype(bf16)
-    w_ref[448:, :] = jnp.concatenate([value_ref[...].astype(f32), jnp.zeros((64, 64), f32)], 1).astype(bf16)
     for t in range(3):
         x_ref[t * rows : (t + 1) * rows, :] = hidden_ref[:, 128 * t : 128 * t + 128]
     x_ref[3 * rows : 3 * rows + rows // 2, :] = folded(hidden_ref[:, 384:448])
-    gain = jnp.concatenate([gain_ref[...].astype(f32), jnp.zeros((1, 64), f32)], 1)
-    gain = jnp.concatenate([gain[:, 128 * t : 128 * t + 128] for t in range(4)] + [jnp.zeros((28, 128), f32)], 0)
+    gain = gain_ref[...].astype(f32).reshape(1, 448)
+    gain = jnp.concatenate([gain, jnp.zeros((1, 64), f32)], 1)
+    gain = jnp.concatenate(
+        [gain[:, 128 * t : 128 * t + 128] for t in range(4)] + [jnp.zeros((28, 128), f32)], 0
+    )
     x_ref[3 * rows + rows // 2 :, :] = gain.astype(bf16)
 
 
-def pack(hidden, gain, w_query, w_key, w_value):
+def pack(hidden, gain):
     rows = hidden.shape[0]
     return pl.pallas_call(
         pack_kernel,
-        out_shape=[
-            jax.ShapeDtypeStruct((rows * 7 // 2 + 32, 128), bf16),
-            jax.ShapeDtypeStruct((512, 512), bf16),
-        ],
-        in_specs=[whole()] * 5,
-        out_specs=[whole()] * 2,
+        out_shape=jax.ShapeDtypeStruct((rows * 7 // 2 + 32, 128), bf16),
+        in_specs=[whole()] * 2,
+        out_specs=whole(),
         compiler_params=params(60),
         name="pack",
-    )(hidden, gain, w_query, w_key, w_value)
+    )(hidden, gain)
+
+
+def pack_weights_kernel(query_ref, key_ref, value_ref, w_ref):
+    w_ref[:448, :384] = query_ref[:, :384]
+    key = jnp.concatenate([key_ref[...].astype(f32), jnp.zeros((64, 64), f32)], 1).T
+    w_ref[:448, 384:] = jnp.concatenate([query_ref[:, 384:448].astype(f32), key[:448]], 1).astype(bf16)
+    w_ref[448:, :] = jnp.concatenate([value_ref[...].astype(f32), jnp.zeros((64, 64), f32)], 1).astype(bf16)
+
+
+def pack_weights(w_query, w_key, w_value):
+    return pl.pallas_call(
+        pack_weights_kernel,
+        out_shape=jax.ShapeDtypeStruct((512, 512), bf16),
+        in_specs=[whole()] * 3,
+        out_specs=whole(),
+        compiler_params=params(60),
+        name="pack_weights",
+    )(w_query, w_key, w_value)
 
 
 def join_kernel(upper_ref, lower_ref, out_ref):
@@ -370,7 +383,7 @@
             jax.ShapeDtypeStruct((requests * nodes, 128), f32),
             jax.ShapeDtypeStruct((requests, pick.shape[1], 128), bf16),
         ],
-        compiler_params=params(14),
+        compiler_params=params(56),
         cost_estimate=pl.CostEstimate(
             flops=requests * ATTENTION_COST,
             bytes_accessed=requests * 2**20,
@@ -414,30 +427,20 @@
         out_shape=jax.ShapeDtypeStruct((2 * arrays[0].shape[0], 448), bf16),
         in_specs=[scalars()] + [whole()] * 8,
         out_specs=whole(),
-        compiler_params=params(8),
+        compiler_params=params(56),
         name="combine",
     )(place, *arrays)
 
 
-def out_kernel(steps, place, att_ref, weight_hbm, *refs):
-    outs, (weight_ref, arrival) = refs[: len(steps)], refs[len(steps) :]
+def out_kernel(steps, place, att_ref, weight_ref, *outs):
     rows = att_ref.shape[0]
-    copies = []
-    for step in steps:
+    for out, step in zip(outs, steps):
         for along in range(SIDE):
             block = lax.rem(place[3] + step, SIDE) * place[1] + along * place[2]
-            slot = len(copies)
-            copies.append(
-                pltpu.make_async_copy(weight_hbm.at[block], weight_ref.at[slot], arrival.at[slot])
-            )
-            copies[slot].start()
-    for slot, copy in enumerate(copies):
-        copy.wait()
-        out, along = outs[slot // SIDE], slot % SIDE
-        terms = jnp.dot(att_ref[...], weight_ref[slot], preferred_element_type=f32)
-        for t in range(3):
-            out[along, t * rows : (t + 1) * rows, :] = terms[:, 128 * t : 128 * t + 128].astype(out.dtype)
-        out[along, 3 * rows :, :] = folded(terms[:, 384:]).astype(out.dtype)
+            terms = jnp.dot(att_ref[...], weight_ref[block], preferred_element_type=f32)
+            for t in range(3):
+                out[along, t * rows : (t + 1) * rows, :] = terms[:, 128 * t : 128 * t + 128].astype(out.dtype)
+            out[along, 3 * rows :, :] = folded(terms[:, 384:]).astype(out.dtype)
 
 
 def out_terms(steps, place, attended, weights):
@@ -447,14 +450,12 @@
         out_shape=[
             jax.ShapeDtypeStruct((SIDE, rows, 128), bf16 if step else f32) for step in steps
         ],
-        in_specs=[scalars(), whole(), pl.BlockSpec(memory_space=pl.ANY)],
+        in_specs=[scalars(), whole(), whole()],
         out_specs=[whole()] * len(steps),
-        scratch_shapes=[
-            pltpu.VMEM((SIDE * len(steps),) + weights.shape[1:], bf16),
-            pltpu.SemaphoreType.DMA((SIDE * len(steps),)),
-        ],
-        compiler_params=params(58),
-        cost_estimate=pl.CostEstimate(flops=2 * 10**10, bytes_accessed=2 * 10**7, transcendentals=0),
+        compiler_params=params(16),
+        cost_estimate=pl.CostEstimate(
+            flops=2 * 10**10, bytes_accessed=2 * 10**7, transcendentals=0
+        ),
         name="out_terms",
     )(place, attended, weights)
 
@@ -544,7 +545,8 @@
     half_index = mp % 2
     hidden = hidden_in.reshape(row_count, part_width)
 
-    packed, weights = pack(hidden, norm_gain[None], w_query, w_key, w_value.T)
+    packed = pack(hidden, norm_gain)
+    weights = pack_weights(w_query, w_key.T, w_value.T)
 
     slots, halves, order = two_way(weights)
 

time: 175 us -> 176 us (level)
  waiting for transfers between devices: 60.9 us -> 63.1 us
  local copies, waits for them, and re-layouts: 16 us -> 13.8 us
    ppermute x26, waiting for transfers between devices: 55.8 us -> 63 us  [moved(): return lax.ppermute(block, ('dp', 'mp'), route)]
    pallas_call x2, Pallas kernels: 12.3 us -> 5.29 us  [out_terms(): pl.pallas_call(functools.partial(out_kernel, steps), out_shape=[jax.Shape...]
    pallas_call x2, Pallas kernels: 13.1 us -> 16.7 us  [attention(): pl.pallas_call(attention_kernel, grid_spec=pltpu.PrefetchScalarGridSpec(n...]
    all_gather x1, waiting for transfers between devices: 2.92 us -> 0.01 us  [shards(): out_weights = lax.all_gather(w_out, 'dp')]
    all_gather x1, waiting for transfers between devices: 2.16 us -> 0.06 us  [shards(): every_row = lax.all_gather(rows, 'dp', axis=0, tiled=True)[:, :picks]]
    pallas_call x1 -> x2, Pallas kernels: 2.16 us -> 3.78 us  [the longest x1 2.06 us: pack_weights(): pl.pallas_call(pack_weights_kernel, out_shape=jax.ShapeDtypeStruct((512,...]
    unnamed x35 -> x46, local copies, waits for them, and re-layouts: 10.8 us -> 10.5 us
  transfers between devices with their start and end apart: 29 -> 29, of which waited for: 14 -> 12; matrix products, arithmetic and copies ran while one was open for 8% -> 7% of each run, Pallas kernels for 22% -> 23%
where the time goes in v1:
time: 176 us; the launch traced here: 175 us
  waiting for transfers between devices  63.1 us (36%)
  Pallas kernels  43.1 us (24%)
  starting transfers between devices  31.9 us (18%)
  between operations  14.1 us (8%)
  local copies, waits for them, and re-layouts  13.8 us (8%)
  other arithmetic  7.12 us (4%)
  matrix products  1.9 us (1%)
    ppermute x26, waiting for transfers between devices, moved(): return lax.ppermute(block, ('dp', 'mp'), route)  63 us
    ppermute x26, starting transfers between devices, moved(): return lax.ppermute(block, ('dp', 'mp'), route)  31.8 us
    pallas_call x2, Pallas kernels, attention(): pl.pallas_call(attention_kernel, grid_spec=pltpu.PrefetchScalarGridSpec(n...  16.7 us
    unnamed x46, local copies, waits for them, and re-layouts  10.5 us
    pallas_call x1, Pallas kernels, project(): pl.pallas_call(functools.partial(project_kernel, count, start, last), out...  6.23 us
    pallas_call x2, Pallas kernels, out_terms(): pl.pallas_call(functools.partial(out_kernel, steps), out_shape=[jax.Shape...  5.29 us
    pallas_call x1, Pallas kernels, combine(): pl.pallas_call(combine_kernel, out_shape=jax.ShapeDtypeStruct((2 * arrays...  3.71 us
  transfers between devices with their start and end apart: 29, of which 12 were waited for; matrix products, arithmetic and copies ran while one was open for 7% of the time, Pallas kernels for 23%

profile of v1, /device:TPU:6, one launch (start us, length us, event | category | flops | bytes accessed | tf_op | source)
XLA Modules:
  0.0 175.0 jit_solution(1758861231869673299)
XLA Ops:
  7.3 1.7 pack.1
  9.0 2.1 %pack_weights.1.refs_0_ = bf16[512,512]{1,0:T(8,128)(2,1)} custom-call(bf16[448,448]{1,0:T(8,128)(2,1)} %query_ref.1, bf16[64,448]{1,0:T(8,128)(2,1)} %bitcast.42, bf16[64,448]{1,0:T(8,128)(2,1)} %bitcast.43), custom_call_target="tpu_custom_call" | custom-call | tf_op jit(solution)/shard_map/pack_weights/pallas_call | solution.py:126
  11.1 1.9 %collective-permute-start.1 = (bf16[512,512]{1,0:T(8,128)(2,1)}, bf16[512,512]{1,0:T(8,128)(2,1)S(1)}, u32[]{:S(2)}, u32[]{:S(2)}) collective-permute-start(bf16[512,512]{1,0:T(8,128)(2,1)} %pack_weights.1.refs_0_), channel_id=1, source_target_pairs={{0,32},{1,33},{2,34},{3,35},{4,36},{5,37},{6,38},{7,39},{8,40},{9,... | collective-permute-start | bytes 1572872 | tf_op jit(solution)/shard_map/ppermute | solution.py:46
  13.0 3.9 %collective-permute-start.2 = (bf16[512,512]{1,0:T(8,128)(2,1)}, bf16[512,512]{1,0:T(8,128)(2,1)S(1)}, u32[]{:S(2)}, u32[]{:S(2)}) collective-permute-start(bf16[512,512]{1,0:T(8,128)(2,1)} %pack_weights.1.refs_0_), channel_id=1, source_target_pairs={{0,224},{1,225},{2,226},{3,227},{4,228},{5,229},{6,230},{7,231},{8... | collective-permute-start | bytes 1572872 | tf_op jit(solution)/shard_map/ppermute | solution.py:46
  17.3 12.5 %collective-permute-done.1.refs_2_ = bf16[512,512]{1,0:T(8,128)(2,1)S(1)} collective-permute-done((bf16[512,512]{1,0:T(8,128)(2,1)}, bf16[512,512]{1,0:T(8,128)(2,1)S(1)}, u32[]{:S(2)}, u32[]{:S(2)}) %collective-permute-start.1) | collective-permute-done | bytes 524320 | tf_op jit(solution)/shard_map/ppermute | solution.py:46
  29.8 3.2 %collective-permute-start.6 = (bf16[512,512]{1,0:T(8,128)(2,1)S(1)}, bf16[512,512]{1,0:T(8,128)(2,1)S(1)}, u32[]{:S(2)}, u32[]{:S(2)}) collective-permute-start(bf16[512,512]{1,0:T(8,128)(2,1)S(1)} %collective-permute-done.2.refs_3_), channel_id=1, source_target_pairs={{0,224},{1,225},{2,226},{3,227},{4,228},{5,229},{6,230},{7,231},{8... | collective-permute-start | bytes 1572872 | tf_op jit(solution)/shard_map/ppermute | solution.py:46
  33.8 11.0 %collective-permute-done.5.refs_6_ = bf16[512,512]{1,0:T(8,128)(2,1)S(1)} collective-permute-done((bf16[512,512]{1,0:T(8,128)(2,1)S(1)}, bf16[512,512]{1,0:T(8,128)(2,1)S(1)}, u32[]{:S(2)}, u32[]{:S(2)}) %collective-permute-start.5) | collective-permute-done | bytes 524320 | tf_op jit(solution)/shard_map/ppermute | solution.py:46
  44.8 3.2 %collective-permute-start.10 = (bf16[512,512]{1,0:T(8,128)(2,1)S(1)}, bf16[512,512]{1,0:T(8,128)(2,1)}, u32[]{:S(2)}, u32[]{:S(2)}) collective-permute-start(bf16[512,512]{1,0:T(8,128)(2,1)S(1)} %collective-permute-done.6.refs_7_), channel_id=1, source_target_pairs={{0,224},{1,225},{2,226},{3,227},{4,228},{5,229},{6,230},{7,231},{8... | collective-permute-start | bytes 1572872 | tf_op jit(solution)/shard_map/ppermute | solution.py:46
  48.0 1.0 fusion.32
  49.6 9.3 %collective-permute-done.9.up_ref.refs_10_ = bf16[512,512]{1,0:T(8,128)(2,1)S(1)} collective-permute-done((bf16[512,512]{1,0:T(8,128)(2,1)S(1)}, bf16[512,512]{1,0:T(8,128)(2,1)S(1)}, u32[]{:S(2)}, u32[]{:S(2)}) %collective-permute-start.9) | collective-permute-done | bytes 524320 | tf_op jit(solution)/shard_map/ppermute | solution.py:46
  58.9 2.1 %cut_blocks.1 = (bf16[256,512]{1,0:T(8,128)(2,1)}, bf16[256,512]{1,0:T(8,128)(2,1)}) custom-call(bf16[512,512]{1,0:T(8,128)(2,1)S(1)} %collective-permute-done.9.up_ref.refs_10_, bf16[512,512]{1,0:T(8,128)(2,1)} %collective-permute-done.10.down_ref.refs_11_), custom_call_target="tpu_custom_call" | custom-call | flops 20000000000 | bytes 1000000 | tf_op jit(solution)/shard_map/cut_blocks/pallas_call | solution.py:161
  60.9 3.2 %collective-permute-start.14 = (bf16[256,512]{1,0:T(8,128)(2,1)}, bf16[256,512]{1,0:T(8,128)(2,1)S(1)}, u32[]{:S(2)}, u32[]{:S(2)}) collective-permute-start(bf16[256,512]{1,0:T(8,128)(2,1)} %get-tuple-element.23), channel_id=1, source_target_pairs={{0,224},{1,225},{2,226},{3,227},{4,228},{5,229},{6,230},{7,231},{8... | collective-permute-start | bytes 786440 | tf_op jit(solution)/shard_map/ppermute | solution.py:46
  64.3 4.5 %collective-permute-done.13.upper_ref = bf16[256,512]{1,0:T(8,128)(2,1)S(1)} collective-permute-done((bf16[256,512]{1,0:T(8,128)(2,1)}, bf16[256,512]{1,0:T(8,128)(2,1)S(1)}, u32[]{:S(2)}, u32[]{:S(2)}) %collective-permute-start.13) | collective-permute-done | bytes 262176 | tf_op jit(solution)/shard_map/ppermute | solution.py:46
  68.8 0.7 copy-done.5
  70.0 0.9 copy-done.6
  71.9 0.7 pad_add_fusion.1.facts
  72.6 0.7 fusion.20.pick_ref
  73.2 1.2 fusion.18
  74.5 2.1 %copy-done = bf16[14848,128]{1,0:T(8,128)(2,1)S(1)} copy-done((bf16[14848,128]{1,0:T(8,128)(2,1)S(1)}, bf16[14848,128]{1,0:T(8,128)(2,1)}, u32[]{:S(2)}) %copy-start) | copy-done | bytes 3801112
  76.6 1.8 %norm.1.normed_ref = bf16[16,256,448]{2,1,0:T(8,128)(2,1)S(1)} custom-call(bf16[16,928,128]{2,1,0:T(8,128)(2,1)S(1)} %bitcast.35), custom_call_target="tpu_custom_call" | custom-call | flops 10000000 | bytes 8000000 | tf_op jit(solution)/shard_map/norm/pallas_call | solution.py:213
  78.5 6.2 %project.1 = (bf16[128,576]{1,0:T(8,128)(2,1)}, bf16[128,576]{1,0:T(8,128)(2,1)S(1)}) custom-call(s32[16]{0:T(128)S(1)} %and_select_fusion.order, bf16[16,256,448]{2,1,0:T(8,128)(2,1)S(1)} %norm.1.normed_ref, bf16[512,512]{1,0:T(8,128)(2,1)S(1)} %copy-done.1, bf16[512,512]{1,0:T(8,128)(2,1)S(1)} %collective-permute-done.refs_1_, ...), custom_call_target="tpu_custom_call" | custom-call | flops 2113929216 | bytes 16000000 | tf_op jit(solution)/shard_map/project/pallas_call | solution.py:258
  84.7 1.6 collective-permute-start.16
  86.9 1.9 %pad_maximum_fusion = (f32[256,128]{1,0:T(8,128)}, f32[256,128]{1,0:T(8,128)}) fusion(f32[256,64]{1,0:T(8,128)} %get-tuple-element.44, f32[256,64]{1,0:T(8,128)} %get-tuple-element.43, f32[256,64]{1,0:T(8,128)S(1)} %get-tuple-element.42), kind=kLoop, calls=%fused_computation.19 | loop fusion | flops 65536 | bytes 458752 | tf_op jit(solution)/shard_map/concatenate | solution.py:568
  89.2 2.0 %collective-permute-done.16.oth_ref = bf16[128,576]{1,0:T(8,128)(2,1)S(1)} collective-permute-done((bf16[128,576]{1,0:T(8,128)(2,1)}, bf16[128,576]{1,0:T(8,128)(2,1)S(1)}, u32[]{:S(2)}, u32[]{:S(2)}) %collective-permute-start.16) | collective-permute-done | bytes 147488 | tf_op jit(solution)/shard_map/ppermute | solution.py:46
  91.9 8.3 %attention.2 = (f32[128,448]{1,0:T(8,128)}, bf16[128,512]{1,0:T(8,128)(2,1)}, f32[128,128]{1,0:T(8,128)}, bf16[2,16,128]{2,1,0:T(8,128)(2,1)}) custom-call(s32[3]{0:T(128)} %pad_add_fusion.1.facts, bf16[128,576]{1,0:T(8,128)(2,1)} %get-tuple-element.24.own_ref, bf16[128,576]{1,0:T(8,128)(2,1)} %copy-done.19, f32[256,128]{1,0:T(8,128)} %get-tuple-element.53.cos_ref, ...), custom_call_target="tpu_custom_call" | custom-call | flops 49999998976 | bytes 2097152 | tf_op jit(solution)/shard_map/attention/pallas_call | solution.py:367
  100.3 2.3 %collective-permute-start.17 = (bf16[128,512]{1,0:T(8,128)(2,1)}, bf16[128,512]{1,0:T(8,128)(2,1)S(1)}, u32[]{:S(2)}, u32[]{:S(2)}) collective-permute-start(bf16[128,512]{1,0:T(8,128)(2,1)} %get-tuple-element.27), channel_id=1, source_target_pairs={{0,1},{1,0},{2,3},{3,2},{4,5},{5,4},{6,7},{7,6},{8,9},{9,8},{10,11... | collective-permute-start | bytes 393224 | tf_op jit(solution)/shard_map/ppermute | solution.py:46
  103.2 8.3 %attention.3 = (f32[128,448]{1,0:T(8,128)}, bf16[128,512]{1,0:T(8,128)(2,1)}, f32[128,128]{1,0:T(8,128)}, bf16[2,16,128]{2,1,0:T(8,128)(2,1)}) custom-call(s32[3]{0:T(128)} %pad_add_fusion.2.facts, bf16[128,576]{1,0:T(8,128)(2,1)} %copy-done.10, bf16[128,576]{1,0:T(8,128)(2,1)} %copy-done.20, f32[256,128]{1,0:T(8,128)} %get-tuple-element.53.cos_ref, ...), custom_call_target="tpu_custom_call" | custom-call | flops 49999998976 | bytes 2097152 | tf_op jit(solution)/shard_map/attention/pallas_call | solution.py:367
  112.5 0.8 slice.28.refs_3_
  113.3 0.8 slice.29.refs_7_
  114.1 1.3 fusion.9
  115.4 1.6 collective-permute-done.19.refs_6_
  117.7 3.7 %combine.1.att_ref = bf16[256,448]{1,0:T(8,128)(2,1)} custom-call(s32[4]{0:T(128)} %pad_add_fusion.place, f32[128,448]{1,0:T(8,128)} %get-tuple-element.25.refs_0_, f32[128,128]{1,0:T(8,128)} %get-tuple-element.26.refs_1_, bf16[128,512]{1,0:T(8,128)(2,1)} %copy-done.11, bf16[128,1]{1,0:T(8,128)(2,1)} %slice.28.refs_3_, ...), custom_call_target="tpu_custom_call" | custom-call | tf_op jit(solution)/shard_map/combine/pallas_call | solution.py:425
  121.5 0.9 copy-done.7
  123.1 3.1 %copy-done.9 = bf16[7168,448]{1,0:T(8,128)(2,1)S(1)} copy-done((bf16[7168,448]{1,0:T(8,128)(2,1)S(1)}, bf16[7168,448]{1,0:T(8,128)(2,1)}, u32[]{:S(2)}) %copy-start.9) | copy-done | bytes 6422552
  126.1 2.9 %out_terms.3 = (bf16[4,896,128]{2,1,0:T(8,128)(2,1)}, bf16[4,896,128]{2,1,0:T(8,128)(2,1)}) custom-call(s32[4]{0:T(128)S(1)} %copy-done.8, bf16[256,448]{1,0:T(8,128)(2,1)S(1)} %copy-done.7, bf16[16,448,448]{2,1,0:T(8,128)(2,1)S(1)} %bitcast.38), custom_call_target="tpu_custom_call" | custom-call | flops 20000000000 | bytes 20000000 | tf_op jit(solution)/shard_map/out_terms/pallas_call | solution.py:448
  129.1 3.0 %collective-permute-start.20 = (bf16[4,896,128]{2,1,0:T(8,128)(2,1)}, bf16[4,896,128]{2,1,0:T(8,128)(2,1)S(1)}, u32[]{:S(2)}, u32[]{:S(2)}) collective-permute-start(bf16[4,896,128]{2,1,0:T(8,128)(2,1)} %get-tuple-element.33), channel_id=1, source_target_pairs={{0,2},{1,3},{2,0},{3,1},{4,6},{5,7},{6,4},{7,5},{8,10},{9,11},{10,... | collective-permute-start | bytes 2752520 | tf_op jit(solution)/shard_map/ppermute | solution.py:46
  132.0 2.4 %out_terms.2 = (bf16[4,896,128]{2,1,0:T(8,128)(2,1)}, f32[4,896,128]{2,1,0:T(8,128)S(1)}) custom-call(s32[4]{0:T(128)S(1)} %copy-done.8, bf16[256,448]{1,0:T(8,128)(2,1)S(1)} %copy-done.7, bf16[16,448,448]{2,1,0:T(8,128)(2,1)S(1)} %bitcast.39), custom_call_target="tpu_custom_call" | custom-call | flops 20000000000 | bytes 20000000 | tf_op jit(solution)/shard_map/out_terms/pallas_call | solution.py:448
  134.4 3.2 %collective-permute-start.22 = (bf16[4,896,128]{2,1,0:T(8,128)(2,1)}, bf16[4,896,128]{2,1,0:T(8,128)(2,1)}, u32[]{:S(2)}, u32[]{:S(2)}) collective-permute-start(bf16[4,896,128]{2,1,0:T(8,128)(2,1)} %get-tuple-element.35), channel_id=1, source_target_pairs={{0,3},{1,0},{2,1},{3,2},{4,7},{5,4},{6,5},{7,6},{8,11},{9,8},{10,9... | collective-permute-start | bytes 2752520 | tf_op jit(solution)/shard_map/ppermute | solution.py:46
  137.6 6.6 %collective-permute-done.20.refs_0_ = bf16[4,896,128]{2,1,0:T(8,128)(2,1)S(1)} collective-permute-done((bf16[4,896,128]{2,1,0:T(8,128)(2,1)}, bf16[4,896,128]{2,1,0:T(8,128)(2,1)S(1)}, u32[]{:S(2)}, u32[]{:S(2)}) %collective-permute-start.20) | collective-permute-done | bytes 917536 | tf_op jit(solution)/shard_map/ppermute | solution.py:46
  144.3 9.8 %collective-permute-done.21.refs_1_ = bf16[4,896,128]{2,1,0:T(8,128)(2,1)} collective-permute-done((bf16[4,896,128]{2,1,0:T(8,128)(2,1)}, bf16[4,896,128]{2,1,0:T(8,128)(2,1)}, u32[]{:S(2)}, u32[]{:S(2)}) %collective-permute-start.21) | collective-permute-done | bytes 917536 | tf_op jit(solution)/shard_map/ppermute | solution.py:46
  154.1 2.6 %partial_sums.1 = (f32[896,128]{1,0:T(8,128)S(1)}, bf16[896,128]{1,0:T(8,128)(2,1)}, bf16[896,128]{1,0:T(8,128)(2,1)}, bf16[896,128]{1,0:T(8,128)(2,1)}) custom-call(s32[1]{0:T(128)} %bitcast.1.place, f32[4,896,128]{2,1,0:T(8,128)S(1)} %get-tuple-element.32.own_ref, bf16[4,896,128]{2,1,0:T(8,128)(2,1)S(1)} %collective-permute-done.20.refs_0_, ...), custom_call_target="tpu_custom_call" | custom-call | tf_op jit(solution)/shard_map/partial_sums/pallas_call | solution.py:475
  156.7 1.4 collective-permute-start.23
  158.1 2.1 %collective-permute-start.24 = (bf16[896,128]{1,0:T(8,128)(2,1)}, bf16[896,128]{1,0:T(8,128)(2,1)S(1)}, u32[]{:S(2)}, u32[]{:S(2)}) collective-permute-start(bf16[896,128]{1,0:T(8,128)(2,1)} %get-tuple-element.38), channel_id=1, source_target_pairs={{0,4},{1,5},{2,6},{3,7},{4,8},{5,9},{6,10},{7,11},{8,12},{9,13},{1... | collective-permute-start | bytes 688136 | tf_op jit(solution)/shard_map/ppermute | solution.py:46
  160.2 0.9 slice.30
  161.3 0.7 reshape.73
  162.0 2.4 %collective-permute-done.23.refs_0_ = bf16[896,128]{1,0:T(8,128)(2,1)S(1)} collective-permute-done((bf16[896,128]{1,0:T(8,128)(2,1)}, bf16[896,128]{1,0:T(8,128)(2,1)S(1)}, u32[]{:S(2)}, u32[]{:S(2)}) %collective-permute-start.23) | collective-permute-done | bytes 229408 | tf_op jit(solution)/shard_map/ppermute | solution.py:46
  164.7 2.9 %collective-permute-done.25.refs_2_ = bf16[896,128]{1,0:T(8,128)(2,1)S(1)} collective-permute-done((bf16[896,128]{1,0:T(8,128)(2,1)}, bf16[896,128]{1,0:T(8,128)(2,1)S(1)}, u32[]{:S(2)}, u32[]{:S(2)}) %collective-permute-start.25) | collective-permute-done | bytes 229408 | tf_op jit(solution)/shard_map/ppermute | solution.py:46
  167.6 0.9 final.1
  (100 shorter events, 8.5 us)
Async XLA Ops:
  7.2 10.1 %copy-start.17 = (s32[2]{0:T(128)S(1)}, s32[2]{0:T(128)}, u32[]{:S(2)}) copy-start(s32[2]{0:T(128)} %constant.91.clone) | copy-start | bytes 28
  7.2 10.1 %copy-start.18 = (s32[2]{0:T(128)S(1)}, s32[2]{0:T(128)}, u32[]{:S(2)}) copy-start(s32[2]{0:T(128)} %constant.92.clone) | copy-start | bytes 28
  7.2 9.9 %copy-start.16 = (s32[4]{0:T(128)S(1)}, s32[4]{0:T(128)}, u32[]{:S(2)}) copy-start(s32[4]{0:T(128)} %param.23) | copy-start | bytes 52
  7.2 25.8 %copy-start.21 = (s32[4,64]{1,0:T(4,128)S(1)}, s32[4,64]{1,0:T(4,128)}, u32[]{:S(2)}) copy-start(s32[4,64]{1,0:T(4,128)} %param.24) | copy-start | bytes 3076
  7.2 67.3 %all-gather.8.cloned.1.call-start = ((), (), s32[]{:S(2)}) async-start(), calls=%async_computation.1 | async-start | bytes 4038656 | tf_op jit(solution)/shard_map/all_gather | solution.py:553
  9.0 112.5 %all-gather.10.cloned.1.call-start = ((), (), s32[]{:S(2)}) async-start(), calls=%async_computation.2 | async-start | bytes 7798784 | tf_op jit(solution)/shard_map/all_gather | solution.py:555
  11.1 59.9 %collective-permute-start = (bf16[512,512]{1,0:T(8,128)(2,1)}, bf16[512,512]{1,0:T(8,128)(2,1)S(1)}, u32[]{:S(2)}, u32[]{:S(2)}) collective-permute-start(bf16[512,512]{1,0:T(8,128)(2,1)} %pack_weights.1.refs_0_), channel_id=1, source_target_pairs={{0,16},{1,17},{2,18},{3,19},{4,20},{5,21},{6,22},{7,23},{8,24},{9,... | collective-permute-start | bytes 1572872 | tf_op jit(solution)/shard_map/ppermute | solution.py:46
  11.1 18.7 %collective-permute-start.1 = (bf16[512,512]{1,0:T(8,128)(2,1)}, bf16[512,512]{1,0:T(8,128)(2,1)S(1)}, u32[]{:S(2)}, u32[]{:S(2)}) collective-permute-start(bf16[512,512]{1,0:T(8,128)(2,1)} %pack_weights.1.refs_0_), channel_id=1, source_target_pairs={{0,32},{1,33},{2,34},{3,35},{4,36},{5,37},{6,38},{7,39},{8,40},{9,... | collective-permute-start | bytes 1572872 | tf_op jit(solution)/shard_map/ppermute | solution.py:46
  13.0 16.7 %collective-permute-start.2 = (bf16[512,512]{1,0:T(8,128)(2,1)}, bf16[512,512]{1,0:T(8,128)(2,1)S(1)}, u32[]{:S(2)}, u32[]{:S(2)}) collective-permute-start(bf16[512,512]{1,0:T(8,128)(2,1)} %pack_weights.1.refs_0_), channel_id=1, source_target_pairs={{0,224},{1,225},{2,226},{3,227},{4,228},{5,229},{6,230},{7,231},{8... | collective-permute-start | bytes 1572872 | tf_op jit(solution)/shard_map/ppermute | solution.py:46
  17.0 143.2 %all-gather.6.cloned.1.call-start = ((), (), s32[]{:S(2)}) async-start(), calls=%async_computation | async-start | bytes 1392640 | tf_op jit(solution)/shard_map/all_gather | solution.py:604
  29.8 15.0 %collective-permute-start.5 = (bf16[512,512]{1,0:T(8,128)(2,1)S(1)}, bf16[512,512]{1,0:T(8,128)(2,1)S(1)}, u32[]{:S(2)}, u32[]{:S(2)}) collective-permute-start(bf16[512,512]{1,0:T(8,128)(2,1)S(1)} %collective-permute-done.1.refs_2_), channel_id=1, source_target_pairs={{0,32},{1,33},{2,34},{3,35},{4,36},{5,37},{6,38},{7,39},{8,40},{9,... | collective-permute-start | bytes 1572872 | tf_op jit(solution)/shard_map/ppermute | solution.py:46
  29.8 15.0 %collective-permute-start.6 = (bf16[512,512]{1,0:T(8,128)(2,1)S(1)}, bf16[512,512]{1,0:T(8,128)(2,1)S(1)}, u32[]{:S(2)}, u32[]{:S(2)}) collective-permute-start(bf16[512,512]{1,0:T(8,128)(2,1)S(1)} %collective-permute-done.2.refs_3_), channel_id=1, source_target_pairs={{0,224},{1,225},{2,226},{3,227},{4,228},{5,229},{6,230},{7,231},{8... | collective-permute-start | bytes 1572872 | tf_op jit(solution)/shard_map/ppermute | solution.py:46
  44.7 14.1 %collective-permute-start.9 = (bf16[512,512]{1,0:T(8,128)(2,1)S(1)}, bf16[512,512]{1,0:T(8,128)(2,1)S(1)}, u32[]{:S(2)}, u32[]{:S(2)}) collective-permute-start(bf16[512,512]{1,0:T(8,128)(2,1)S(1)} %collective-permute-done.5.refs_6_), channel_id=1, source_target_pairs={{0,32},{1,33},{2,34},{3,35},{4,36},{5,37},{6,38},{7,39},{8,40},{9,... | collective-permute-start | bytes 1572872 | tf_op jit(solution)/shard_map/ppermute | solution.py:46
  44.8 14.1 %collective-permute-start.10 = (bf16[512,512]{1,0:T(8,128)(2,1)S(1)}, bf16[512,512]{1,0:T(8,128)(2,1)}, u32[]{:S(2)}, u32[]{:S(2)}) collective-permute-start(bf16[512,512]{1,0:T(8,128)(2,1)S(1)} %collective-permute-done.6.refs_7_), channel_id=1, source_target_pairs={{0,224},{1,225},{2,226},{3,227},{4,228},{5,229},{6,230},{7,231},{8... | collective-permute-start | bytes 1572872 | tf_op jit(solution)/shard_map/ppermute | solution.py:46
  49.0 15.2 %copy-start.15 = (s32[4,8]{1,0:T(4,128)S(1)}, s32[4,8]{1,0:T(4,128)}, u32[]{:S(2)}) copy-start(s32[4,8]{1,0:T(4,128)} %param.26) | copy-start | bytes 388
  49.0 15.2 %copy-start.14 = (s32[4,64]{1,0:T(4,128)S(1)}, s32[4,64]{1,0:T(4,128)}, u32[]{:S(2)}) copy-start(s32[4,64]{1,0:T(4,128)} %param.25) | copy-start | bytes 3076
  49.0 22.1 %collective-permute-start.3 = (bf16[512,512]{1,0:T(8,128)(2,1)S(1)}, bf16[512,512]{1,0:T(8,128)(2,1)}, u32[]{:S(2)}, u32[]{:S(2)}) collective-permute-start(bf16[512,512]{1,0:T(8,128)(2,1)S(1)} %collective-permute-done.1.refs_2_), channel_id=1, source_target_pairs={{0,16},{1,17},{2,18},{3,19},{4,20},{5,21},{6,22},{7,23},{8,24},{9,... | collective-permute-start | bytes 1572872 | tf_op jit(solution)/shard_map/ppermute | solution.py:46
  49.1 22.6 %collective-permute-start.4 = (bf16[512,512]{1,0:T(8,128)(2,1)S(1)}, bf16[512,512]{1,0:T(8,128)(2,1)}, u32[]{:S(2)}, u32[]{:S(2)}) collective-permute-start(bf16[512,512]{1,0:T(8,128)(2,1)S(1)} %collective-permute-done.2.refs_3_), channel_id=1, source_target_pairs={{0,16},{1,17},{2,18},{3,19},{4,20},{5,21},{6,22},{7,23},{8,24},{9,... | collective-permute-start | bytes 1572872 | tf_op jit(solution)/shard_map/ppermute | solution.py:46
  58.9 2.1 %copy-start.3 = (bf16[512,512]{1,0:T(8,128)(2,1)}, bf16[512,512]{1,0:T(8,128)(2,1)S(1)}, u32[]{:S(2)}) copy-start(bf16[512,512]{1,0:T(8,128)(2,1)S(1)} %collective-permute-done.9.up_ref.refs_10_) | copy-start | bytes 1572868
  60.9 7.9 %collective-permute-start.13 = (bf16[256,512]{1,0:T(8,128)(2,1)}, bf16[256,512]{1,0:T(8,128)(2,1)S(1)}, u32[]{:S(2)}, u32[]{:S(2)}) collective-permute-start(bf16[256,512]{1,0:T(8,128)(2,1)} %get-tuple-element.22), channel_id=1, source_target_pairs={{0,32},{1,33},{2,34},{3,35},{4,36},{5,37},{6,38},{7,39},{8,40},{9,... | collective-permute-start | bytes 786440 | tf_op jit(solution)/shard_map/ppermute | solution.py:46
  60.9 7.9 %collective-permute-start.14 = (bf16[256,512]{1,0:T(8,128)(2,1)}, bf16[256,512]{1,0:T(8,128)(2,1)S(1)}, u32[]{:S(2)}, u32[]{:S(2)}) collective-permute-start(bf16[256,512]{1,0:T(8,128)(2,1)} %get-tuple-element.23), channel_id=1, source_target_pairs={{0,224},{1,225},{2,226},{3,227},{4,228},{5,229},{6,230},{7,231},{8... | collective-permute-start | bytes 786440 | tf_op jit(solution)/shard_map/ppermute | solution.py:46
  68.8 9.6 %collective-permute-start.7 = (bf16[512,512]{1,0:T(8,128)(2,1)S(1)}, bf16[512,512]{1,0:T(8,128)(2,1)}, u32[]{:S(2)}, u32[]{:S(2)}) collective-permute-start(bf16[512,512]{1,0:T(8,128)(2,1)S(1)} %collective-permute-done.5.refs_6_), channel_id=1, source_target_pairs={{0,16},{1,17},{2,18},{3,19},{4,20},{5,21},{6,22},{7,23},{8,24},{9,... | collective-permute-start | bytes 1572872 | tf_op jit(solution)/shard_map/ppermute | solution.py:46
  68.8 0.7 copy-start.5
  69.5 8.9 %collective-permute-start.8 = (bf16[512,512]{1,0:T(8,128)(2,1)S(1)}, bf16[512,512]{1,0:T(8,128)(2,1)}, u32[]{:S(2)}, u32[]{:S(2)}) collective-permute-start(bf16[512,512]{1,0:T(8,128)(2,1)S(1)} %collective-permute-done.6.refs_7_), channel_id=1, source_target_pairs={{0,16},{1,17},{2,18},{3,19},{4,20},{5,21},{6,22},{7,23},{8,24},{9,... | collective-permute-start | bytes 1572872 | tf_op jit(solution)/shard_map/ppermute | solution.py:46
  70.0 0.9 copy-start.6
  71.0 7.4 %collective-permute-start.11 = (bf16[512,512]{1,0:T(8,128)(2,1)}, bf16[512,512]{1,0:T(8,128)(2,1)}, u32[]{:S(2)}, u32[]{:S(2)}) collective-permute-start(bf16[512,512]{1,0:T(8,128)(2,1)} %copy-done.3), channel_id=1, source_target_pairs={{0,16},{1,17},{2,18},{3,19},{4,20},{5,21},{6,22},{7,23},{8,24},{9,... | collective-permute-start | bytes 1572872 | tf_op jit(solution)/shard_map/ppermute | solution.py:46
  71.1 7.3 %collective-permute-start.12 = (bf16[512,512]{1,0:T(8,128)(2,1)}, bf16[512,512]{1,0:T(8,128)(2,1)}, u32[]{:S(2)}, u32[]{:S(2)}) collective-permute-start(bf16[512,512]{1,0:T(8,128)(2,1)} %collective-permute-done.10.down_ref.refs_11_), channel_id=1, source_target_pairs={{0,16},{1,17},{2,18},{3,19},{4,20},{5,21},{6,22},{7,23},{8,24},{9,... | collective-permute-start | bytes 1572872 | tf_op jit(solution)/shard_map/ppermute | solution.py:46
  71.6 6.8 %collective-permute-start.15 = (bf16[512,512]{1,0:T(8,128)(2,1)S(1)}, bf16[512,512]{1,0:T(8,128)(2,1)}, u32[]{:S(2)}, u32[]{:S(2)}) collective-permute-start(bf16[512,512]{1,0:T(8,128)(2,1)S(1)} %join.1.refs_14_), channel_id=1, source_target_pairs={{0,16},{1,17},{2,18},{3,19},{4,20},{5,21},{6,22},{7,23},{8,24},{9,... | collective-permute-start | bytes 1572872 | tf_op jit(solution)/shard_map/ppermute | solution.py:46
  74.5 2.1 %copy-start = (bf16[14848,128]{1,0:T(8,128)(2,1)S(1)}, bf16[14848,128]{1,0:T(8,128)(2,1)}, u32[]{:S(2)}) copy-start(bf16[14848,128]{1,0:T(8,128)(2,1)} %all-gather.8.cloned.1.call-done) | copy-start | bytes 11403268
  76.5 1.9 %copy-start.1 = (bf16[512,512]{1,0:T(8,128)(2,1)S(1)}, bf16[512,512]{1,0:T(8,128)(2,1)}, u32[]{:S(2)}) copy-start(bf16[512,512]{1,0:T(8,128)(2,1)} %pack_weights.1.refs_0_) | copy-start | bytes 1572868
  76.5 1.9 %copy-start.4 = (bf16[512,512]{1,0:T(8,128)(2,1)S(1)}, bf16[512,512]{1,0:T(8,128)(2,1)}, u32[]{:S(2)}) copy-start(bf16[512,512]{1,0:T(8,128)(2,1)} %copy-done.3) | copy-start | bytes 1572868
  84.7 15.6 %copy-start.10 = (bf16[128,576]{1,0:T(8,128)(2,1)}, bf16[128,576]{1,0:T(8,128)(2,1)S(1)}, u32[]{:S(2)}) copy-start(bf16[128,576]{1,0:T(8,128)(2,1)S(1)} %get-tuple-element.28.own_ref) | copy-start | bytes 442372
  84.7 6.6 %collective-permute-start.16 = (bf16[128,576]{1,0:T(8,128)(2,1)}, bf16[128,576]{1,0:T(8,128)(2,1)S(1)}, u32[]{:S(2)}, u32[]{:S(2)}) collective-permute-start(bf16[128,576]{1,0:T(8,128)(2,1)} %get-tuple-element.24.own_ref), channel_id=1, source_target_pairs={{0,1},{1,0},{2,3},{3,2},{4,5},{5,4},{6,7},{7,6},{8,9},{9,8},{10,11... | collective-permute-start | bytes 442376 | tf_op jit(solution)/shard_map/ppermute | solution.py:46
  88.8 13.8 %collective-permute-start.18 = (bf16[128,576]{1,0:T(8,128)(2,1)S(1)}, bf16[128,576]{1,0:T(8,128)(2,1)S(1)}, u32[]{:S(2)}, u32[]{:S(2)}) collective-permute-start(bf16[128,576]{1,0:T(8,128)(2,1)S(1)} %get-tuple-element.28.own_ref), channel_id=1, source_target_pairs={{0,1},{1,0},{2,3},{3,2},{4,5},{5,4},{6,7},{7,6},{8,9},{9,8},{10,11... | collective-permute-start | bytes 442376 | tf_op jit(solution)/shard_map/ppermute | solution.py:46
  100.3 13.8 %copy-start.13 = (bf16[2,16,128]{2,1,0:T(8,128)(2,1)S(1)}, bf16[2,16,128]{2,1,0:T(8,128)(2,1)}, u32[]{:S(2)}) copy-start(bf16[2,16,128]{2,1,0:T(8,128)(2,1)} %get-tuple-element.40) | copy-start | bytes 24580
  100.3 15.1 %collective-permute-start.17 = (bf16[128,512]{1,0:T(8,128)(2,1)}, bf16[128,512]{1,0:T(8,128)(2,1)S(1)}, u32[]{:S(2)}, u32[]{:S(2)}) collective-permute-start(bf16[128,512]{1,0:T(8,128)(2,1)} %get-tuple-element.27), channel_id=1, source_target_pairs={{0,1},{1,0},{2,3},{3,2},{4,5},{5,4},{6,7},{7,6},{8,9},{9,8},{10,11... | collective-permute-start | bytes 393224 | tf_op jit(solution)/shard_map/ppermute | solution.py:46
  111.6 5.5 %collective-permute-start.19 = (bf16[128,512]{1,0:T(8,128)(2,1)}, bf16[128,512]{1,0:T(8,128)(2,1)S(1)}, u32[]{:S(2)}, u32[]{:S(2)}) collective-permute-start(bf16[128,512]{1,0:T(8,128)(2,1)} %get-tuple-element.31), channel_id=1, source_target_pairs={{0,1},{1,0},{2,3},{3,2},{4,5},{5,4},{6,7},{7,6},{8,9},{9,8},{10,11... | collective-permute-start | bytes 393224 | tf_op jit(solution)/shard_map/ppermute | solution.py:46
  115.4 1.7 copy-start.11
  121.5 1.0 copy-start.7
  123.1 3.1 %copy-start.9 = (bf16[7168,448]{1,0:T(8,128)(2,1)S(1)}, bf16[7168,448]{1,0:T(8,128)(2,1)}, u32[]{:S(2)}) copy-start(bf16[7168,448]{1,0:T(8,128)(2,1)} %all-gather.10.cloned.1.call-done) | copy-start | bytes 19267588
  129.1 15.2 %collective-permute-start.20 = (bf16[4,896,128]{2,1,0:T(8,128)(2,1)}, bf16[4,896,128]{2,1,0:T(8,128)(2,1)S(1)}, u32[]{:S(2)}, u32[]{:S(2)}) collective-permute-start(bf16[4,896,128]{2,1,0:T(8,128)(2,1)} %get-tuple-element.33), channel_id=1, source_target_pairs={{0,2},{1,3},{2,0},{3,1},{4,6},{5,7},{6,4},{7,5},{8,10},{9,11},{10,... | collective-permute-start | bytes 2752520 | tf_op jit(solution)/shard_map/ppermute | solution.py:46
  134.4 19.7 %collective-permute-start.21 = (bf16[4,896,128]{2,1,0:T(8,128)(2,1)}, bf16[4,896,128]{2,1,0:T(8,128)(2,1)}, u32[]{:S(2)}, u32[]{:S(2)}) collective-permute-start(bf16[4,896,128]{2,1,0:T(8,128)(2,1)} %get-tuple-element.34), channel_id=1, source_target_pairs={{0,1},{1,2},{2,3},{3,0},{4,5},{5,6},{6,7},{7,4},{8,9},{9,10},{10,1... | collective-permute-start | bytes 2752520 | tf_op jit(solution)/shard_map/ppermute | solution.py:46
  134.4 19.7 %collective-permute-start.22 = (bf16[4,896,128]{2,1,0:T(8,128)(2,1)}, bf16[4,896,128]{2,1,0:T(8,128)(2,1)}, u32[]{:S(2)}, u32[]{:S(2)}) collective-permute-start(bf16[4,896,128]{2,1,0:T(8,128)(2,1)} %get-tuple-element.35), channel_id=1, source_target_pairs={{0,3},{1,0},{2,1},{3,2},{4,7},{5,4},{6,5},{7,6},{8,11},{9,8},{10,9... | collective-permute-start | bytes 2752520 | tf_op jit(solution)/shard_map/ppermute | solution.py:46
  154.1 7.0 %copy-start.22 = (s32[64]{0:T(128)S(1)}, s32[64]{0:T(128)}, u32[]{:S(2)}) copy-start(s32[64]{0:T(128)} %param.27) | copy-start | bytes 772
  154.1 13.5 %copy-start.2 = (bf16[4,64,448]{2,1,0:T(8,128)(2,1)S(1)}, bf16[4,64,448]{2,1,0:T(8,128)(2,1)}, u32[]{:S(2)}) copy-start(bf16[4,64,448]{2,1,0:T(8,128)(2,1)} %param.15) | copy-start | bytes 688132
  156.7 7.7 %collective-permute-start.23 = (bf16[896,128]{1,0:T(8,128)(2,1)}, bf16[896,128]{1,0:T(8,128)(2,1)S(1)}, u32[]{:S(2)}, u32[]{:S(2)}) collective-permute-start(bf16[896,128]{1,0:T(8,128)(2,1)} %get-tuple-element.37), channel_id=1, source_target_pairs={{0,8},{1,9},{2,10},{3,11},{4,12},{5,13},{6,14},{7,15},{8,0},{9,1},... | collective-permute-start | bytes 688136 | tf_op jit(solution)/shard_map/ppermute | solution.py:46
  158.1 6.7 %collective-permute-start.24 = (bf16[896,128]{1,0:T(8,128)(2,1)}, bf16[896,128]{1,0:T(8,128)(2,1)S(1)}, u32[]{:S(2)}, u32[]{:S(2)}) collective-permute-start(bf16[896,128]{1,0:T(8,128)(2,1)} %get-tuple-element.38), channel_id=1, source_target_pairs={{0,4},{1,5},{2,6},{3,7},{4,8},{5,9},{6,10},{7,11},{8,12},{9,13},{1... | collective-permute-start | bytes 688136 | tf_op jit(solution)/shard_map/ppermute | solution.py:46
  160.2 7.4 %collective-permute-start.25 = (bf16[896,128]{1,0:T(8,128)(2,1)}, bf16[896,128]{1,0:T(8,128)(2,1)S(1)}, u32[]{:S(2)}, u32[]{:S(2)}) collective-permute-start(bf16[896,128]{1,0:T(8,128)(2,1)} %get-tuple-element.39), channel_id=1, source_target_pairs={{0,12},{1,13},{2,14},{3,15},{4,0},{5,1},{6,2},{7,3},{8,4},{9,5},{1... | collective-permute-start | bytes 688136 | tf_op jit(solution)/shard_map/ppermute | solution.py:46
  (4 other events, 2.6 us)
Sparse Core Ops, SparseCore 0:
  10.5 57.7 all-gather.7
  70.1 50.6 all-gather.9
  122.7 37.5 all-gather.5

commit v2 on v1

--- a/solution.py
+++ b/solution.py
@@ -383,7 +383,7 @@
             jax.ShapeDtypeStruct((requests * nodes, 128), f32),
             jax.ShapeDtypeStruct((requests, pick.shape[1], 128), bf16),
         ],
-        compiler_params=params(56),
+        compiler_params=params(40),
         cost_estimate=pl.CostEstimate(
             flops=requests * ATTENTION_COST,
             bytes_accessed=requests * 2**20,
@@ -427,7 +427,7 @@
         out_shape=jax.ShapeDtypeStruct((2 * arrays[0].shape[0], 448), bf16),
         in_specs=[scalars()] + [whole()] * 8,
         out_specs=whole(),
-        compiler_params=params(56),
+        compiler_params=params(8),
         name="combine",
     )(place, *arrays)
 

time: 176 us -> 173 us (0.983)
  Pallas kernels: 43.1 us -> 38.1 us
  waiting for transfers between devices: 63.1 us -> 66.5 us
    pallas_call x2, Pallas kernels: 16.7 us -> 13.1 us  [attention(): pl.pallas_call(attention_kernel, grid_spec=pltpu.PrefetchScalarGridSpec(n...]
    all_gather x1, waiting for transfers between devices: 0.01 us -> 2.26 us  [shards(): out_weights = lax.all_gather(w_out, 'dp')]
    all_gather x1, waiting for transfers between devices: 0.06 us -> 2.01 us  [shards(): every_row = lax.all_gather(rows, 'dp', axis=0, tiled=True)[:, :picks]]
    unnamed x46 -> x42, local copies, waits for them, and re-layouts: 10.5 us -> 11 us
  transfers between devices with their start and end apart: 29 -> 29, of which waited for: 12 -> 14; matrix products, arithmetic and copies ran while one was open for 7% -> 7% of each run, Pallas kernels for 23% -> 21%
where the time goes in v2:
time: 173 us
  waiting for transfers between devices  66.5 us (38%)
  Pallas kernels  38.1 us (22%)
  starting transfers between devices  31.8 us (18%)
  local copies, waits for them, and re-layouts  15 us (9%)
  between operations  14.1 us (8%)
  other arithmetic  6.06 us (4%)
    ppermute x26, waiting for transfers between devices, moved(): return lax.ppermute(block, ('dp', 'mp'), route)  62.2 us
    ppermute x26, starting transfers between devices, moved(): return lax.ppermute(block, ('dp', 'mp'), route)  31.7 us
    pallas_call x2, Pallas kernels, attention(): pl.pallas_call(attention_kernel, grid_spec=pltpu.PrefetchScalarGridSpec(n...  13.1 us
    unnamed x42, local copies, waits for them, and re-layouts  11 us
    pallas_call x1, Pallas kernels, project(): pl.pallas_call(functools.partial(project_kernel, count, start, last), out...  6.22 us
    pallas_call x2, Pallas kernels, out_terms(): pl.pallas_call(functools.partial(out_kernel, steps), out_shape=[jax.Shape...  5.3 us
  transfers between devices with their start and end apart: 29, of which 14 were waited for; matrix products, arithmetic and copies ran while one was open for 7% of the time, Pallas kernels for 21%

profile of v2, /device:TPU:6, one launch (start us, length us, event | category | flops | bytes accessed | tf_op | source)
XLA Modules:
  0.0 172.9 jit_solution(9413404242985465407)
XLA Ops:
  7.3 1.7 pack.1
  9.1 2.1 %pack_weights.1.refs_0_ = bf16[512,512]{1,0:T(8,128)(2,1)} custom-call(bf16[448,448]{1,0:T(8,128)(2,1)} %query_ref.1, bf16[64,448]{1,0:T(8,128)(2,1)} %bitcast.46, bf16[64,448]{1,0:T(8,128)(2,1)} %bitcast.47), custom_call_target="tpu_custom_call" | custom-call | tf_op jit(solution)/shard_map/pack_weights/pallas_call | solution.py:126
  11.1 1.9 %collective-permute-start.1 = (bf16[512,512]{1,0:T(8,128)(2,1)}, bf16[512,512]{1,0:T(8,128)(2,1)S(1)}, u32[]{:S(2)}, u32[]{:S(2)}) collective-permute-start(bf16[512,512]{1,0:T(8,128)(2,1)} %pack_weights.1.refs_0_), channel_id=1, source_target_pairs={{0,32},{1,33},{2,34},{3,35},{4,36},{5,37},{6,38},{7,39},{8,40},{9,... | collective-permute-start | bytes 1572872 | tf_op jit(solution)/shard_map/ppermute | solution.py:46
  13.0 3.9 %collective-permute-start.2 = (bf16[512,512]{1,0:T(8,128)(2,1)}, bf16[512,512]{1,0:T(8,128)(2,1)S(1)}, u32[]{:S(2)}, u32[]{:S(2)}) collective-permute-start(bf16[512,512]{1,0:T(8,128)(2,1)} %pack_weights.1.refs_0_), channel_id=1, source_target_pairs={{0,224},{1,225},{2,226},{3,227},{4,228},{5,229},{6,230},{7,231},{8... | collective-permute-start | bytes 1572872 | tf_op jit(solution)/shard_map/ppermute | solution.py:46
  18.4 11.4 %collective-permute-done.1.refs_2_ = bf16[512,512]{1,0:T(8,128)(2,1)S(1)} collective-permute-done((bf16[512,512]{1,0:T(8,128)(2,1)}, bf16[512,512]{1,0:T(8,128)(2,1)S(1)}, u32[]{:S(2)}, u32[]{:S(2)}) %collective-permute-start.1) | collective-permute-done | bytes 524320 | tf_op jit(solution)/shard_map/ppermute | solution.py:46
  29.8 3.2 %collective-permute-start.6 = (bf16[512,512]{1,0:T(8,128)(2,1)S(1)}, bf16[512,512]{1,0:T(8,128)(2,1)S(1)}, u32[]{:S(2)}, u32[]{:S(2)}) collective-permute-start(bf16[512,512]{1,0:T(8,128)(2,1)S(1)} %collective-permute-done.2.refs_3_), channel_id=1, source_target_pairs={{0,224},{1,225},{2,226},{3,227},{4,228},{5,229},{6,230},{7,231},{8... | collective-permute-start | bytes 1572872 | tf_op jit(solution)/shard_map/ppermute | solution.py:46
  33.8 11.0 %collective-permute-done.5.refs_6_ = bf16[512,512]{1,0:T(8,128)(2,1)S(1)} collective-permute-done((bf16[512,512]{1,0:T(8,128)(2,1)S(1)}, bf16[512,512]{1,0:T(8,128)(2,1)S(1)}, u32[]{:S(2)}, u32[]{:S(2)}) %collective-permute-start.5) | collective-permute-done | bytes 524320 | tf_op jit(solution)/shard_map/ppermute | solution.py:46
  44.8 3.2 %collective-permute-start.10 = (bf16[512,512]{1,0:T(8,128)(2,1)S(1)}, bf16[512,512]{1,0:T(8,128)(2,1)}, u32[]{:S(2)}, u32[]{:S(2)}) collective-permute-start(bf16[512,512]{1,0:T(8,128)(2,1)S(1)} %collective-permute-done.6.refs_7_), channel_id=1, source_target_pairs={{0,224},{1,225},{2,226},{3,227},{4,228},{5,229},{6,230},{7,231},{8... | collective-permute-start | bytes 1572872 | tf_op jit(solution)/shard_map/ppermute | solution.py:46
  49.0 9.8 %collective-permute-done.9.up_ref.refs_10_ = bf16[512,512]{1,0:T(8,128)(2,1)S(1)} collective-permute-done((bf16[512,512]{1,0:T(8,128)(2,1)S(1)}, bf16[512,512]{1,0:T(8,128)(2,1)S(1)}, u32[]{:S(2)}, u32[]{:S(2)}) %collective-permute-start.9) | collective-permute-done | bytes 524320 | tf_op jit(solution)/shard_map/ppermute | solution.py:46
  58.9 2.1 %cut_blocks.1 = (bf16[256,512]{1,0:T(8,128)(2,1)}, bf16[256,512]{1,0:T(8,128)(2,1)}) custom-call(bf16[512,512]{1,0:T(8,128)(2,1)S(1)} %collective-permute-done.9.up_ref.refs_10_, bf16[512,512]{1,0:T(8,128)(2,1)} %collective-permute-done.10.down_ref.refs_11_), custom_call_target="tpu_custom_call" | custom-call | flops 20000000000 | bytes 1000000 | tf_op jit(solution)/shard_map/cut_blocks/pallas_call | solution.py:161
  60.9 3.2 %collective-permute-start.14 = (bf16[256,512]{1,0:T(8,128)(2,1)}, bf16[256,512]{1,0:T(8,128)(2,1)S(1)}, u32[]{:S(2)}, u32[]{:S(2)}) collective-permute-start(bf16[256,512]{1,0:T(8,128)(2,1)} %get-tuple-element.23), channel_id=1, source_target_pairs={{0,224},{1,225},{2,226},{3,227},{4,228},{5,229},{6,230},{7,231},{8... | collective-permute-start | bytes 786440 | tf_op jit(solution)/shard_map/ppermute | solution.py:46
  64.8 0.7 pad.8
  66.1 2.7 %collective-permute-done.13.upper_ref = bf16[256,512]{1,0:T(8,128)(2,1)S(1)} collective-permute-done((bf16[256,512]{1,0:T(8,128)(2,1)}, bf16[256,512]{1,0:T(8,128)(2,1)S(1)}, u32[]{:S(2)}, u32[]{:S(2)}) %collective-permute-start.13) | collective-permute-done | bytes 262176 | tf_op jit(solution)/shard_map/ppermute | solution.py:46
  68.8 0.7 copy-done.5
  70.0 0.9 copy-done.6
  71.9 0.7 pad_add_fusion.1.facts
  72.7 2.0 %fusion.18 = (f32[256,64]{1,0:T(8,128)}, f32[256,64]{1,0:T(8,128)}, f32[256,64]{1,0:T(8,128)}) fusion(f32[64]{0:T(128)} %multiply_exponential_fusion, f32[256]{0:T(256)S(1)} %add.106), kind=kLoop, calls=%fused_computation.29 | loop fusion | flops 32768 | bytes 197888 | tf_op jit(solution)/shard_map/neg | solution.py:569
  74.7 2.1 %copy-done = bf16[14848,128]{1,0:T(8,128)(2,1)S(1)} copy-done((bf16[14848,128]{1,0:T(8,128)(2,1)S(1)}, bf16[14848,128]{1,0:T(8,128)(2,1)}, u32[]{:S(2)}) %copy-start) | copy-done | bytes 3801112
  76.7 1.8 %norm.1.normed_ref = bf16[16,256,448]{2,1,0:T(8,128)(2,1)S(1)} custom-call(bf16[16,928,128]{2,1,0:T(8,128)(2,1)S(1)} %bitcast.35), custom_call_target="tpu_custom_call" | custom-call | flops 10000000 | bytes 8000000 | tf_op jit(solution)/shard_map/norm/pallas_call | solution.py:213
  78.7 6.2 %project.1 = (bf16[128,576]{1,0:T(8,128)(2,1)S(1)}, bf16[128,576]{1,0:T(8,128)(2,1)}) custom-call(s32[16]{0:T(128)S(1)} %and_select_fusion.order, bf16[16,256,448]{2,1,0:T(8,128)(2,1)S(1)} %norm.1.normed_ref, bf16[512,512]{1,0:T(8,128)(2,1)S(1)} %copy-done.1, bf16[512,512]{1,0:T(8,128)(2,1)S(1)} %collective-permute-done.refs_1_, ...), custom_call_target="tpu_custom_call" | custom-call | flops 2113929216 | bytes 16000000 | tf_op jit(solution)/shard_map/project/pallas_call | solution.py:258
  84.9 1.6 collective-permute-start.16
  86.5 1.3 pad_maximum_fusion
  88.3 3.4 %collective-permute-done.16.oth_ref = bf16[128,576]{1,0:T(8,128)(2,1)S(1)} collective-permute-done((bf16[128,576]{1,0:T(8,128)(2,1)S(1)}, bf16[128,576]{1,0:T(8,128)(2,1)S(1)}, u32[]{:S(2)}, u32[]{:S(2)}) %collective-permute-start.16) | collective-permute-done | bytes 147488 | tf_op jit(solution)/shard_map/ppermute | solution.py:46
  91.8 1.6 copy-done.8
  93.4 1.6 copy-done.9
  95.0 0.9 copy-done.11
  95.9 6.1 %attention.2 = (f32[128,448]{1,0:T(8,128)S(1)}, bf16[128,512]{1,0:T(8,128)(2,1)S(1)}, f32[128,128]{1,0:T(8,128)S(1)}, bf16[2,16,128]{2,1,0:T(8,128)(2,1)S(1)}) custom-call(s32[3]{0:T(128)S(1)} %pad_add_fusion.1.facts, bf16[128,576]{1,0:T(8,128)(2,1)S(1)} %copy-done.11, bf16[128,576]{1,0:T(8,128)(2,1)S(1)} %collective-permute-done.16.oth_ref, ...), custom_call_target="tpu_custom_call" | custom-call | flops 49999998976 | bytes 2097152 | tf_op jit(solution)/shard_map/attention/pallas_call | solution.py:367
  102.0 1.9 %collective-permute-start.17 = (bf16[128,512]{1,0:T(8,128)(2,1)S(1)}, bf16[128,512]{1,0:T(8,128)(2,1)S(1)}, u32[]{:S(2)}, u32[]{:S(2)}) collective-permute-start(bf16[128,512]{1,0:T(8,128)(2,1)S(1)} %get-tuple-element.27), channel_id=1, source_target_pairs={{0,1},{1,0},{2,3},{3,2},{4,5},{5,4},{6,7},{7,6},{8,9},{9,8},{10,11... | collective-permute-start | bytes 393224 | tf_op jit(solution)/shard_map/ppermute | solution.py:46
  103.9 7.0 %attention.3 = (f32[128,448]{1,0:T(8,128)S(1)}, bf16[128,512]{1,0:T(8,128)(2,1)S(1)}, f32[128,128]{1,0:T(8,128)S(1)}, bf16[2,16,128]{2,1,0:T(8,128)(2,1)S(1)}) custom-call(s32[3]{0:T(128)S(1)} %pad_add_fusion.2.facts, bf16[128,576]{1,0:T(8,128)(2,1)} %get-tuple-element.28.own_ref, bf16[128,576]{1,0:T(8,128)(2,1)S(1)} %collective-permute-done.18.oth_ref, ...), custom_call_target="tpu_custom_call" | custom-call | flops 49999998976 | bytes 2097152 | tf_op jit(solution)/shard_map/attention/pallas_call | solution.py:367
  111.9 0.6 fusion.9
  112.5 3.7 %collective-permute-done.19.refs_6_ = bf16[128,512]{1,0:T(8,128)(2,1)S(1)} collective-permute-done((bf16[128,512]{1,0:T(8,128)(2,1)S(1)}, bf16[128,512]{1,0:T(8,128)(2,1)S(1)}, u32[]{:S(2)}, u32[]{:S(2)}) %collective-permute-start.19) | collective-permute-done | bytes 131104 | tf_op jit(solution)/shard_map/ppermute | solution.py:46
  116.2 2.3 %combine.1.att_ref = bf16[256,448]{1,0:T(8,128)(2,1)S(1)} custom-call(s32[4]{0:T(128)S(1)} %pad_add_fusion.place, f32[128,448]{1,0:T(8,128)S(1)} %get-tuple-element.25.refs_0_, f32[128,128]{1,0:T(8,128)S(1)} %get-tuple-element.26.refs_1_, bf16[128,512]{1,0:T(8,128)(2,1)S(1)} %collective-permute-done.17.refs_2_, bf16[128,1]{1,0:T(8,128)(2,1)S(1)} %slice.28.refs_3_, ...), custom_call_target="tpu_custom_call" | custom-call | tf_op jit(solution)/shard_map/combine/pallas_call | solution.py:425
  118.6 2.3 %all-gather.10.cloned.1.call-done = bf16[7168,448]{1,0:T(8,128)(2,1)} async-done(((bf16[448,448]{1,0:T(8,128)(2,1)}), bf16[7168,448]{1,0:T(8,128)(2,1)}) %all-gather.10.cloned.1.call-update) | async-done | bytes 6422544 | tf_op jit(solution)/shard_map/all_gather | solution.py:555
  120.8 3.1 %copy-done.7 = bf16[7168,448]{1,0:T(8,128)(2,1)S(1)} copy-done((bf16[7168,448]{1,0:T(8,128)(2,1)S(1)}, bf16[7168,448]{1,0:T(8,128)(2,1)}, u32[]{:S(2)}) %copy-start.7) | copy-done | bytes 6422552
  123.9 2.9 %out_terms.3 = (bf16[4,896,128]{2,1,0:T(8,128)(2,1)}, bf16[4,896,128]{2,1,0:T(8,128)(2,1)}) custom-call(s32[4]{0:T(128)S(1)} %pad_add_fusion.place, bf16[256,448]{1,0:T(8,128)(2,1)S(1)} %combine.1.att_ref, bf16[16,448,448]{2,1,0:T(8,128)(2,1)S(1)} %bitcast.38), custom_call_target="tpu_custom_call" | custom-call | flops 20000000000 | bytes 20000000 | tf_op jit(solution)/shard_map/out_terms/pallas_call | solution.py:448
  126.8 3.0 %collective-permute-start.20 = (bf16[4,896,128]{2,1,0:T(8,128)(2,1)}, bf16[4,896,128]{2,1,0:T(8,128)(2,1)S(1)}, u32[]{:S(2)}, u32[]{:S(2)}) collective-permute-start(bf16[4,896,128]{2,1,0:T(8,128)(2,1)} %get-tuple-element.33), channel_id=1, source_target_pairs={{0,2},{1,3},{2,0},{3,1},{4,6},{5,7},{6,4},{7,5},{8,10},{9,11},{10,... | collective-permute-start | bytes 2752520 | tf_op jit(solution)/shard_map/ppermute | solution.py:46
  129.8 2.4 %out_terms.2 = (bf16[4,896,128]{2,1,0:T(8,128)(2,1)}, f32[4,896,128]{2,1,0:T(8,128)S(1)}) custom-call(s32[4]{0:T(128)S(1)} %pad_add_fusion.place, bf16[256,448]{1,0:T(8,128)(2,1)S(1)} %combine.1.att_ref, bf16[16,448,448]{2,1,0:T(8,128)(2,1)S(1)} %bitcast.39), custom_call_target="tpu_custom_call" | custom-call | flops 20000000000 | bytes 20000000 | tf_op jit(solution)/shard_map/out_terms/pallas_call | solution.py:448
  132.8 2.6 %collective-permute-start.22 = (bf16[4,896,128]{2,1,0:T(8,128)(2,1)}, bf16[4,896,128]{2,1,0:T(8,128)(2,1)}, u32[]{:S(2)}, u32[]{:S(2)}) collective-permute-start(bf16[4,896,128]{2,1,0:T(8,128)(2,1)} %get-tuple-element.35), channel_id=1, source_target_pairs={{0,3},{1,0},{2,1},{3,2},{4,7},{5,4},{6,5},{7,6},{8,11},{9,8},{10,9... | collective-permute-start | bytes 2752520 | tf_op jit(solution)/shard_map/ppermute | solution.py:46
  135.5 6.6 %collective-permute-done.20.refs_0_ = bf16[4,896,128]{2,1,0:T(8,128)(2,1)S(1)} collective-permute-done((bf16[4,896,128]{2,1,0:T(8,128)(2,1)}, bf16[4,896,128]{2,1,0:T(8,128)(2,1)S(1)}, u32[]{:S(2)}, u32[]{:S(2)}) %collective-permute-start.20) | collective-permute-done | bytes 917536 | tf_op jit(solution)/shard_map/ppermute | solution.py:46
  142.0 9.8 %collective-permute-done.21.refs_1_ = bf16[4,896,128]{2,1,0:T(8,128)(2,1)} collective-permute-done((bf16[4,896,128]{2,1,0:T(8,128)(2,1)}, bf16[4,896,128]{2,1,0:T(8,128)(2,1)}, u32[]{:S(2)}, u32[]{:S(2)}) %collective-permute-start.21) | collective-permute-done | bytes 917536 | tf_op jit(solution)/shard_map/ppermute | solution.py:46
  152.0 2.6 %partial_sums.1 = (f32[896,128]{1,0:T(8,128)S(1)}, bf16[896,128]{1,0:T(8,128)(2,1)}, bf16[896,128]{1,0:T(8,128)(2,1)}, bf16[896,128]{1,0:T(8,128)(2,1)}) custom-call(s32[1]{0:T(128)} %bitcast.1.place, f32[4,896,128]{2,1,0:T(8,128)S(1)} %get-tuple-element.32.own_ref, bf16[4,896,128]{2,1,0:T(8,128)(2,1)S(1)} %collective-permute-done.20.refs_0_, ...), custom_call_target="tpu_custom_call" | custom-call | tf_op jit(solution)/shard_map/partial_sums/pallas_call | solution.py:475
  154.6 1.4 collective-permute-start.23
  156.0 2.1 %collective-permute-start.24 = (bf16[896,128]{1,0:T(8,128)(2,1)}, bf16[896,128]{1,0:T(8,128)(2,1)S(1)}, u32[]{:S(2)}, u32[]{:S(2)}) collective-permute-start(bf16[896,128]{1,0:T(8,128)(2,1)} %get-tuple-element.38), channel_id=1, source_target_pairs={{0,4},{1,5},{2,6},{3,7},{4,8},{5,9},{6,10},{7,11},{8,12},{9,13},{1... | collective-permute-start | bytes 688136 | tf_op jit(solution)/shard_map/ppermute | solution.py:46
  158.1 2.0 %all-gather.6.cloned.1.call-done = bf16[64,80,128]{2,1,0:T(8,128)(2,1)} async-done(((bf16[4,80,128]{2,1,0:T(8,128)(2,1)}), bf16[64,80,128]{2,1,0:T(8,128)(2,1)}) %all-gather.6.cloned.1.call-update) | async-done | bytes 1310736 | tf_op jit(solution)/shard_map/all_gather | solution.py:604
  160.1 0.9 slice.30
  161.2 0.7 reshape.73
  162.6 2.9 %collective-permute-done.25.refs_2_ = bf16[896,128]{1,0:T(8,128)(2,1)S(1)} collective-permute-done((bf16[896,128]{1,0:T(8,128)(2,1)}, bf16[896,128]{1,0:T(8,128)(2,1)S(1)}, u32[]{:S(2)}, u32[]{:S(2)}) %collective-permute-start.25) | collective-permute-done | bytes 229408 | tf_op jit(solution)/shard_map/ppermute | solution.py:46
  165.5 0.9 final.1
  (96 shorter events, 9.1 us)
Async XLA Ops:
  7.2 10.7 %copy-start.17 = (s32[2]{0:T(128)S(1)}, s32[2]{0:T(128)}, u32[]{:S(2)}) copy-start(s32[2]{0:T(128)} %constant.91.clone) | copy-start | bytes 28
  7.2 10.7 %copy-start.18 = (s32[2]{0:T(128)S(1)}, s32[2]{0:T(128)}, u32[]{:S(2)}) copy-start(s32[2]{0:T(128)} %constant.92.clone) | copy-start | bytes 28
  7.2 9.9 %copy-start.15 = (s32[4]{0:T(128)S(1)}, s32[4]{0:T(128)}, u32[]{:S(2)}) copy-start(s32[4]{0:T(128)} %param.23) | copy-start | bytes 52
  7.2 25.8 %copy-start.19 = (s32[4,64]{1,0:T(4,128)S(1)}, s32[4,64]{1,0:T(4,128)}, u32[]{:S(2)}) copy-start(s32[4,64]{1,0:T(4,128)} %param.24) | copy-start | bytes 3076
  7.2 67.4 %all-gather.8.cloned.1.call-start = ((), (), s32[]{:S(2)}) async-start(), calls=%async_computation.1 | async-start | bytes 4038656 | tf_op jit(solution)/shard_map/all_gather | solution.py:553
  9.0 111.8 %all-gather.10.cloned.1.call-start = ((), (), s32[]{:S(2)}) async-start(), calls=%async_computation.2 | async-start | bytes 7798784 | tf_op jit(solution)/shard_map/all_gather | solution.py:555
  11.1 59.9 %collective-permute-start = (bf16[512,512]{1,0:T(8,128)(2,1)}, bf16[512,512]{1,0:T(8,128)(2,1)S(1)}, u32[]{:S(2)}, u32[]{:S(2)}) collective-permute-start(bf16[512,512]{1,0:T(8,128)(2,1)} %pack_weights.1.refs_0_), channel_id=1, source_target_pairs={{0,16},{1,17},{2,18},{3,19},{4,20},{5,21},{6,22},{7,23},{8,24},{9,... | collective-permute-start | bytes 1572872 | tf_op jit(solution)/shard_map/ppermute | solution.py:46
  11.1 18.7 %collective-permute-start.1 = (bf16[512,512]{1,0:T(8,128)(2,1)}, bf16[512,512]{1,0:T(8,128)(2,1)S(1)}, u32[]{:S(2)}, u32[]{:S(2)}) collective-permute-start(bf16[512,512]{1,0:T(8,128)(2,1)} %pack_weights.1.refs_0_), channel_id=1, source_target_pairs={{0,32},{1,33},{2,34},{3,35},{4,36},{5,37},{6,38},{7,39},{8,40},{9,... | collective-permute-start | bytes 1572872 | tf_op jit(solution)/shard_map/ppermute | solution.py:46
  13.0 16.7 %collective-permute-start.2 = (bf16[512,512]{1,0:T(8,128)(2,1)}, bf16[512,512]{1,0:T(8,128)(2,1)S(1)}, u32[]{:S(2)}, u32[]{:S(2)}) collective-permute-start(bf16[512,512]{1,0:T(8,128)(2,1)} %pack_weights.1.refs_0_), channel_id=1, source_target_pairs={{0,224},{1,225},{2,226},{3,227},{4,228},{5,229},{6,230},{7,231},{8... | collective-permute-start | bytes 1572872 | tf_op jit(solution)/shard_map/ppermute | solution.py:46
  17.0 143.1 %all-gather.6.cloned.1.call-start = ((), (), s32[]{:S(2)}) async-start(), calls=%async_computation | async-start | bytes 1392640 | tf_op jit(solution)/shard_map/all_gather | solution.py:604
  29.8 15.0 %collective-permute-start.5 = (bf16[512,512]{1,0:T(8,128)(2,1)S(1)}, bf16[512,512]{1,0:T(8,128)(2,1)S(1)}, u32[]{:S(2)}, u32[]{:S(2)}) collective-permute-start(bf16[512,512]{1,0:T(8,128)(2,1)S(1)} %collective-permute-done.1.refs_2_), channel_id=1, source_target_pairs={{0,32},{1,33},{2,34},{3,35},{4,36},{5,37},{6,38},{7,39},{8,40},{9,... | collective-permute-start | bytes 1572872 | tf_op jit(solution)/shard_map/ppermute | solution.py:46
  29.8 15.0 %collective-permute-start.6 = (bf16[512,512]{1,0:T(8,128)(2,1)S(1)}, bf16[512,512]{1,0:T(8,128)(2,1)S(1)}, u32[]{:S(2)}, u32[]{:S(2)}) collective-permute-start(bf16[512,512]{1,0:T(8,128)(2,1)S(1)} %collective-permute-done.2.refs_3_), channel_id=1, source_target_pairs={{0,224},{1,225},{2,226},{3,227},{4,228},{5,229},{6,230},{7,231},{8... | collective-permute-start | bytes 1572872 | tf_op jit(solution)/shard_map/ppermute | solution.py:46
  44.8 14.1 %collective-permute-start.9 = (bf16[512,512]{1,0:T(8,128)(2,1)S(1)}, bf16[512,512]{1,0:T(8,128)(2,1)S(1)}, u32[]{:S(2)}, u32[]{:S(2)}) collective-permute-start(bf16[512,512]{1,0:T(8,128)(2,1)S(1)} %collective-permute-done.5.refs_6_), channel_id=1, source_target_pairs={{0,32},{1,33},{2,34},{3,35},{4,36},{5,37},{6,38},{7,39},{8,40},{9,... | collective-permute-start | bytes 1572872 | tf_op jit(solution)/shard_map/ppermute | solution.py:46
  44.8 14.1 %collective-permute-start.10 = (bf16[512,512]{1,0:T(8,128)(2,1)S(1)}, bf16[512,512]{1,0:T(8,128)(2,1)}, u32[]{:S(2)}, u32[]{:S(2)}) collective-permute-start(bf16[512,512]{1,0:T(8,128)(2,1)S(1)} %collective-permute-done.6.refs_7_), channel_id=1, source_target_pairs={{0,224},{1,225},{2,226},{3,227},{4,228},{5,229},{6,230},{7,231},{8... | collective-permute-start | bytes 1572872 | tf_op jit(solution)/shard_map/ppermute | solution.py:46
  48.5 17.0 %copy-start.13 = (s32[4,64]{1,0:T(4,128)S(1)}, s32[4,64]{1,0:T(4,128)}, u32[]{:S(2)}) copy-start(s32[4,64]{1,0:T(4,128)} %param.25) | copy-start | bytes 3076
  48.5 22.7 %collective-permute-start.3 = (bf16[512,512]{1,0:T(8,128)(2,1)S(1)}, bf16[512,512]{1,0:T(8,128)(2,1)}, u32[]{:S(2)}, u32[]{:S(2)}) collective-permute-start(bf16[512,512]{1,0:T(8,128)(2,1)S(1)} %collective-permute-done.1.refs_2_), channel_id=1, source_target_pairs={{0,16},{1,17},{2,18},{3,19},{4,20},{5,21},{6,22},{7,23},{8,24},{9,... | collective-permute-start | bytes 1572872 | tf_op jit(solution)/shard_map/ppermute | solution.py:46
  48.5 23.1 %collective-permute-start.4 = (bf16[512,512]{1,0:T(8,128)(2,1)S(1)}, bf16[512,512]{1,0:T(8,128)(2,1)}, u32[]{:S(2)}, u32[]{:S(2)}) collective-permute-start(bf16[512,512]{1,0:T(8,128)(2,1)S(1)} %collective-permute-done.2.refs_3_), channel_id=1, source_target_pairs={{0,16},{1,17},{2,18},{3,19},{4,20},{5,21},{6,22},{7,23},{8,24},{9,... | collective-permute-start | bytes 1572872 | tf_op jit(solution)/shard_map/ppermute | solution.py:46
  58.9 2.1 %copy-start.3 = (bf16[512,512]{1,0:T(8,128)(2,1)}, bf16[512,512]{1,0:T(8,128)(2,1)S(1)}, u32[]{:S(2)}) copy-start(bf16[512,512]{1,0:T(8,128)(2,1)S(1)} %collective-permute-done.9.up_ref.refs_10_) | copy-start | bytes 1572868
  60.9 7.9 %collective-permute-start.13 = (bf16[256,512]{1,0:T(8,128)(2,1)}, bf16[256,512]{1,0:T(8,128)(2,1)S(1)}, u32[]{:S(2)}, u32[]{:S(2)}) collective-permute-start(bf16[256,512]{1,0:T(8,128)(2,1)} %get-tuple-element.22), channel_id=1, source_target_pairs={{0,32},{1,33},{2,34},{3,35},{4,36},{5,37},{6,38},{7,39},{8,40},{9,... | collective-permute-start | bytes 786440 | tf_op jit(solution)/shard_map/ppermute | solution.py:46
  60.9 7.9 %collective-permute-start.14 = (bf16[256,512]{1,0:T(8,128)(2,1)}, bf16[256,512]{1,0:T(8,128)(2,1)S(1)}, u32[]{:S(2)}, u32[]{:S(2)}) collective-permute-start(bf16[256,512]{1,0:T(8,128)(2,1)} %get-tuple-element.23), channel_id=1, source_target_pairs={{0,224},{1,225},{2,226},{3,227},{4,228},{5,229},{6,230},{7,231},{8... | collective-permute-start | bytes 786440 | tf_op jit(solution)/shard_map/ppermute | solution.py:46
  68.8 9.8 %collective-permute-start.7 = (bf16[512,512]{1,0:T(8,128)(2,1)S(1)}, bf16[512,512]{1,0:T(8,128)(2,1)}, u32[]{:S(2)}, u32[]{:S(2)}) collective-permute-start(bf16[512,512]{1,0:T(8,128)(2,1)S(1)} %collective-permute-done.5.refs_6_), channel_id=1, source_target_pairs={{0,16},{1,17},{2,18},{3,19},{4,20},{5,21},{6,22},{7,23},{8,24},{9,... | collective-permute-start | bytes 1572872 | tf_op jit(solution)/shard_map/ppermute | solution.py:46
  69.5 9.1 %collective-permute-start.8 = (bf16[512,512]{1,0:T(8,128)(2,1)S(1)}, bf16[512,512]{1,0:T(8,128)(2,1)}, u32[]{:S(2)}, u32[]{:S(2)}) collective-permute-start(bf16[512,512]{1,0:T(8,128)(2,1)S(1)} %collective-permute-done.6.refs_7_), channel_id=1, source_target_pairs={{0,16},{1,17},{2,18},{3,19},{4,20},{5,21},{6,22},{7,23},{8,24},{9,... | collective-permute-start | bytes 1572872 | tf_op jit(solution)/shard_map/ppermute | solution.py:46
  70.0 0.9 copy-start.6
  71.0 7.6 %collective-permute-start.11 = (bf16[512,512]{1,0:T(8,128)(2,1)}, bf16[512,512]{1,0:T(8,128)(2,1)}, u32[]{:S(2)}, u32[]{:S(2)}) collective-permute-start(bf16[512,512]{1,0:T(8,128)(2,1)} %copy-done.3), channel_id=1, source_target_pairs={{0,16},{1,17},{2,18},{3,19},{4,20},{5,21},{6,22},{7,23},{8,24},{9,... | collective-permute-start | bytes 1572872 | tf_op jit(solution)/shard_map/ppermute | solution.py:46
  71.1 7.5 %collective-permute-start.12 = (bf16[512,512]{1,0:T(8,128)(2,1)}, bf16[512,512]{1,0:T(8,128)(2,1)}, u32[]{:S(2)}, u32[]{:S(2)}) collective-permute-start(bf16[512,512]{1,0:T(8,128)(2,1)} %collective-permute-done.10.down_ref.refs_11_), channel_id=1, source_target_pairs={{0,16},{1,17},{2,18},{3,19},{4,20},{5,21},{6,22},{7,23},{8,24},{9,... | collective-permute-start | bytes 1572872 | tf_op jit(solution)/shard_map/ppermute | solution.py:46
  71.6 7.0 %collective-permute-start.15 = (bf16[512,512]{1,0:T(8,128)(2,1)S(1)}, bf16[512,512]{1,0:T(8,128)(2,1)}, u32[]{:S(2)}, u32[]{:S(2)}) collective-permute-start(bf16[512,512]{1,0:T(8,128)(2,1)S(1)} %join.1.refs_14_), channel_id=1, source_target_pairs={{0,16},{1,17},{2,18},{3,19},{4,20},{5,21},{6,22},{7,23},{8,24},{9,... | collective-permute-start | bytes 1572872 | tf_op jit(solution)/shard_map/ppermute | solution.py:46
  74.7 2.1 %copy-start = (bf16[14848,128]{1,0:T(8,128)(2,1)S(1)}, bf16[14848,128]{1,0:T(8,128)(2,1)}, u32[]{:S(2)}) copy-start(bf16[14848,128]{1,0:T(8,128)(2,1)} %all-gather.8.cloned.1.call-done) | copy-start | bytes 11403268
  76.7 1.9 %copy-start.1 = (bf16[512,512]{1,0:T(8,128)(2,1)S(1)}, bf16[512,512]{1,0:T(8,128)(2,1)}, u32[]{:S(2)}) copy-start(bf16[512,512]{1,0:T(8,128)(2,1)} %pack_weights.1.refs_0_) | copy-start | bytes 1572868
  76.7 1.9 %copy-start.4 = (bf16[512,512]{1,0:T(8,128)(2,1)S(1)}, bf16[512,512]{1,0:T(8,128)(2,1)}, u32[]{:S(2)}) copy-start(bf16[512,512]{1,0:T(8,128)(2,1)} %copy-done.3) | copy-start | bytes 1572868
  78.6 7.9 %copy-start.16 = (s32[2]{0:T(128)S(1)}, s32[2]{0:T(128)}, u32[]{:S(2)}) copy-start(s32[2]{0:T(128)} %get-tuple-element.47) | copy-start | bytes 28
  84.9 6.9 %copy-start.10 = (bf16[128,576]{1,0:T(8,128)(2,1)}, bf16[128,576]{1,0:T(8,128)(2,1)S(1)}, u32[]{:S(2)}) copy-start(bf16[128,576]{1,0:T(8,128)(2,1)S(1)} %get-tuple-element.24.own_ref) | copy-start | bytes 442372
  84.9 6.9 %collective-permute-start.16 = (bf16[128,576]{1,0:T(8,128)(2,1)S(1)}, bf16[128,576]{1,0:T(8,128)(2,1)S(1)}, u32[]{:S(2)}, u32[]{:S(2)}) collective-permute-start(bf16[128,576]{1,0:T(8,128)(2,1)S(1)} %get-tuple-element.24.own_ref), channel_id=1, source_target_pairs={{0,1},{1,0},{2,3},{3,2},{4,5},{5,4},{6,7},{7,6},{8,9},{9,8},{10,11... | collective-permute-start | bytes 442376 | tf_op jit(solution)/shard_map/ppermute | solution.py:46
  87.8 16.1 %collective-permute-start.18 = (bf16[128,576]{1,0:T(8,128)(2,1)}, bf16[128,576]{1,0:T(8,128)(2,1)S(1)}, u32[]{:S(2)}, u32[]{:S(2)}) collective-permute-start(bf16[128,576]{1,0:T(8,128)(2,1)} %get-tuple-element.28.own_ref), channel_id=1, source_target_pairs={{0,1},{1,0},{2,3},{3,2},{4,5},{5,4},{6,7},{7,6},{8,9},{9,8},{10,11... | collective-permute-start | bytes 442376 | tf_op jit(solution)/shard_map/ppermute | solution.py:46
  91.8 1.6 copy-start.8
  93.4 1.6 copy-start.9
  102.0 9.5 %copy-start.14 = (s32[2]{0:T(128)S(1)}, s32[2]{0:T(128)}, u32[]{:S(2)}) copy-start(s32[2]{0:T(128)} %broadcast_select_fusion) | copy-start | bytes 28
  102.0 9.5 %copy-start.12 = (bf16[2,64]{1,0:T(2,128)(2,1)S(1)}, bf16[2,64]{1,0:T(2,128)(2,1)}, u32[]{:S(2)}) copy-start(bf16[2,64]{1,0:T(2,128)(2,1)} %get-tuple-element.46) | copy-start | bytes 772
  102.0 10.5 %collective-permute-start.17 = (bf16[128,512]{1,0:T(8,128)(2,1)S(1)}, bf16[128,512]{1,0:T(8,128)(2,1)S(1)}, u32[]{:S(2)}, u32[]{:S(2)}) collective-permute-start(bf16[128,512]{1,0:T(8,128)(2,1)S(1)} %get-tuple-element.27), channel_id=1, source_target_pairs={{0,1},{1,0},{2,3},{3,2},{4,5},{5,4},{6,7},{7,6},{8,9},{9,8},{10,11... | collective-permute-start | bytes 393224 | tf_op jit(solution)/shard_map/ppermute | solution.py:46
  111.0 5.3 %collective-permute-start.19 = (bf16[128,512]{1,0:T(8,128)(2,1)S(1)}, bf16[128,512]{1,0:T(8,128)(2,1)S(1)}, u32[]{:S(2)}, u32[]{:S(2)}) collective-permute-start(bf16[128,512]{1,0:T(8,128)(2,1)S(1)} %get-tuple-element.31), channel_id=1, source_target_pairs={{0,1},{1,0},{2,3},{3,2},{4,5},{5,4},{6,7},{7,6},{8,9},{9,8},{10,11... | collective-permute-start | bytes 393224 | tf_op jit(solution)/shard_map/ppermute | solution.py:46
  120.8 3.1 %copy-start.7 = (bf16[7168,448]{1,0:T(8,128)(2,1)S(1)}, bf16[7168,448]{1,0:T(8,128)(2,1)}, u32[]{:S(2)}) copy-start(bf16[7168,448]{1,0:T(8,128)(2,1)} %all-gather.10.cloned.1.call-done) | copy-start | bytes 19267588
  126.8 15.2 %collective-permute-start.20 = (bf16[4,896,128]{2,1,0:T(8,128)(2,1)}, bf16[4,896,128]{2,1,0:T(8,128)(2,1)S(1)}, u32[]{:S(2)}, u32[]{:S(2)}) collective-permute-start(bf16[4,896,128]{2,1,0:T(8,128)(2,1)} %get-tuple-element.33), channel_id=1, source_target_pairs={{0,2},{1,3},{2,0},{3,1},{4,6},{5,7},{6,4},{7,5},{8,10},{9,11},{10,... | collective-permute-start | bytes 2752520 | tf_op jit(solution)/shard_map/ppermute | solution.py:46
  132.2 19.7 %collective-permute-start.21 = (bf16[4,896,128]{2,1,0:T(8,128)(2,1)}, bf16[4,896,128]{2,1,0:T(8,128)(2,1)}, u32[]{:S(2)}, u32[]{:S(2)}) collective-permute-start(bf16[4,896,128]{2,1,0:T(8,128)(2,1)} %get-tuple-element.34), channel_id=1, source_target_pairs={{0,1},{1,2},{2,3},{3,0},{4,5},{5,6},{6,7},{7,4},{8,9},{9,10},{10,1... | collective-permute-start | bytes 2752520 | tf_op jit(solution)/shard_map/ppermute | solution.py:46
  132.8 19.2 %collective-permute-start.22 = (bf16[4,896,128]{2,1,0:T(8,128)(2,1)}, bf16[4,896,128]{2,1,0:T(8,128)(2,1)}, u32[]{:S(2)}, u32[]{:S(2)}) collective-permute-start(bf16[4,896,128]{2,1,0:T(8,128)(2,1)} %get-tuple-element.35), channel_id=1, source_target_pairs={{0,3},{1,0},{2,1},{3,2},{4,7},{5,4},{6,5},{7,6},{8,11},{9,8},{10,9... | collective-permute-start | bytes 2752520 | tf_op jit(solution)/shard_map/ppermute | solution.py:46
  152.0 9.0 %copy-start.20 = (s32[64]{0:T(128)S(1)}, s32[64]{0:T(128)}, u32[]{:S(2)}) copy-start(s32[64]{0:T(128)} %param.27) | copy-start | bytes 772
  152.0 13.5 %copy-start.2 = (bf16[4,64,448]{2,1,0:T(8,128)(2,1)S(1)}, bf16[4,64,448]{2,1,0:T(8,128)(2,1)}, u32[]{:S(2)}) copy-start(bf16[4,64,448]{2,1,0:T(8,128)(2,1)} %param.15) | copy-start | bytes 688132
  154.6 7.7 %collective-permute-start.23 = (bf16[896,128]{1,0:T(8,128)(2,1)}, bf16[896,128]{1,0:T(8,128)(2,1)S(1)}, u32[]{:S(2)}, u32[]{:S(2)}) collective-permute-start(bf16[896,128]{1,0:T(8,128)(2,1)} %get-tuple-element.37), channel_id=1, source_target_pairs={{0,8},{1,9},{2,10},{3,11},{4,12},{5,13},{6,14},{7,15},{8,0},{9,1},... | collective-permute-start | bytes 688136 | tf_op jit(solution)/shard_map/ppermute | solution.py:46
  156.0 6.6 %collective-permute-start.24 = (bf16[896,128]{1,0:T(8,128)(2,1)}, bf16[896,128]{1,0:T(8,128)(2,1)S(1)}, u32[]{:S(2)}, u32[]{:S(2)}) collective-permute-start(bf16[896,128]{1,0:T(8,128)(2,1)} %get-tuple-element.38), channel_id=1, source_target_pairs={{0,4},{1,5},{2,6},{3,7},{4,8},{5,9},{6,10},{7,11},{8,12},{9,13},{1... | collective-permute-start | bytes 688136 | tf_op jit(solution)/shard_map/ppermute | solution.py:46
  158.1 7.4 %collective-permute-start.25 = (bf16[896,128]{1,0:T(8,128)(2,1)}, bf16[896,128]{1,0:T(8,128)(2,1)S(1)}, u32[]{:S(2)}, u32[]{:S(2)}) collective-permute-start(bf16[896,128]{1,0:T(8,128)(2,1)} %get-tuple-element.39), channel_id=1, source_target_pairs={{0,12},{1,13},{2,14},{3,15},{4,0},{5,1},{6,2},{7,3},{8,4},{9,5},{1... | collective-permute-start | bytes 688136 | tf_op jit(solution)/shard_map/ppermute | solution.py:46
  (2 other events, 1.6 us)
Sparse Core Ops, SparseCore 0:
  10.5 57.7 all-gather.7
  70.1 50.6 all-gather.9
  122.7 37.4 all-gather.5

commit v3 on v2

--- a/solution.py
+++ b/solution.py
@@ -593,9 +593,9 @@
         chosen.append(rows)
         arrays += [kept, stats, partner(sent), valid[at]]
     attended = combine(place, arrays)
-    two, one = out_terms((2, 1), place, attended, out_weights)
-    three, here = out_terms((3, 0), place, attended, out_weights)
-    got = [first_axis(two, 2), first_axis(one, 1), first_axis(three, 3)]
+    one, three = out_terms((1, 3), place, attended, out_weights)
+    two, here = out_terms((2, 0), place, attended, out_weights)
+    got = [first_axis(one, 1), first_axis(three, 3), first_axis(two, 2)]
     mine = partial_sums(me_second[None].astype(jnp.int32), here, got)
     parts = [mine[0]] + [second_axis(mine[s], s) for s in (2, 1, 3)]
     layer_out = final(hidden, parts).reshape(req_dev, tree_size, part_width)

time: 173 us -> 176 us (1.017)
  waiting for transfers between devices: 66.5 us -> 69.3 us
    ppermute x26, waiting for transfers between devices: 62.2 us -> 66.5 us  [moved(): return lax.ppermute(block, ('dp', 'mp'), route)]
  transfers between devices with their start and end apart: 29 -> 29, of which waited for: 14 -> 13; matrix products, arithmetic and copies ran while one was open for 7% -> 7% of each run, Pallas kernels for 21% -> 20%
where the time goes in v3:
time: 176 us; the launch traced here: 174 us
  waiting for transfers between devices  69.3 us (39%)
  Pallas kernels  38.1 us (22%)
  starting transfers between devices  30.6 us (17%)
  local copies, waits for them, and re-layouts  15 us (9%)
  between operations  14.1 us (8%)
  other arithmetic  6.06 us (3%)
    ppermute x26, waiting for transfers between devices, moved(): return lax.ppermute(block, ('dp', 'mp'), route)  66.5 us
    ppermute x26, starting transfers between devices, moved(): return lax.ppermute(block, ('dp', 'mp'), route)  30.5 us
    pallas_call x2, Pallas kernels, attention(): pl.pallas_call(attention_kernel, grid_spec=pltpu.PrefetchScalarGridSpec(n...  13.1 us
    unnamed x42, local copies, waits for them, and re-layouts  11 us
    pallas_call x1, Pallas kernels, project(): pl.pallas_call(functools.partial(project_kernel, count, start, last), out...  6.22 us
    pallas_call x2, Pallas kernels, out_terms(): pl.pallas_call(functools.partial(out_kernel, steps), out_shape=[jax.Shape...  5.3 us
  transfers between devices with their start and end apart: 29, of which 13 were waited for; matrix products, arithmetic and copies ran while one was open for 7% of the time, Pallas kernels for 20%

profile of v3, /device:TPU:6, one launch (start us, length us, event | category | flops | bytes accessed | tf_op | source)
XLA Modules:
  0.0 174.5 jit_solution(194384406176088380)
XLA Ops:
  7.3 1.7 pack.1
  9.1 2.1 %pack_weights.1.refs_0_ = bf16[512,512]{1,0:T(8,128)(2,1)} custom-call(bf16[448,448]{1,0:T(8,128)(2,1)} %query_ref.1, bf16[64,448]{1,0:T(8,128)(2,1)} %bitcast.46, bf16[64,448]{1,0:T(8,128)(2,1)} %bitcast.47), custom_call_target="tpu_custom_call" | custom-call | tf_op jit(solution)/shard_map/pack_weights/pallas_call | solution.py:126
  11.1 1.9 %collective-permute-start.1 = (bf16[512,512]{1,0:T(8,128)(2,1)}, bf16[512,512]{1,0:T(8,128)(2,1)S(1)}, u32[]{:S(2)}, u32[]{:S(2)}) collective-permute-start(bf16[512,512]{1,0:T(8,128)(2,1)} %pack_weights.1.refs_0_), channel_id=1, source_target_pairs={{0,32},{1,33},{2,34},{3,35},{4,36},{5,37},{6,38},{7,39},{8,40},{9,... | collective-permute-start | bytes 1572872 | tf_op jit(solution)/shard_map/ppermute | solution.py:46
  13.0 3.9 %collective-permute-start.2 = (bf16[512,512]{1,0:T(8,128)(2,1)}, bf16[512,512]{1,0:T(8,128)(2,1)S(1)}, u32[]{:S(2)}, u32[]{:S(2)}) collective-permute-start(bf16[512,512]{1,0:T(8,128)(2,1)} %pack_weights.1.refs_0_), channel_id=1, source_target_pairs={{0,224},{1,225},{2,226},{3,227},{4,228},{5,229},{6,230},{7,231},{8... | collective-permute-start | bytes 1572872 | tf_op jit(solution)/shard_map/ppermute | solution.py:46
  18.4 11.4 %collective-permute-done.1.refs_2_ = bf16[512,512]{1,0:T(8,128)(2,1)S(1)} collective-permute-done((bf16[512,512]{1,0:T(8,128)(2,1)}, bf16[512,512]{1,0:T(8,128)(2,1)S(1)}, u32[]{:S(2)}, u32[]{:S(2)}) %collective-permute-start.1) | collective-permute-done | bytes 524320 | tf_op jit(solution)/shard_map/ppermute | solution.py:46
  29.8 3.2 %collective-permute-start.6 = (bf16[512,512]{1,0:T(8,128)(2,1)S(1)}, bf16[512,512]{1,0:T(8,128)(2,1)S(1)}, u32[]{:S(2)}, u32[]{:S(2)}) collective-permute-start(bf16[512,512]{1,0:T(8,128)(2,1)S(1)} %collective-permute-done.2.refs_3_), channel_id=1, source_target_pairs={{0,224},{1,225},{2,226},{3,227},{4,228},{5,229},{6,230},{7,231},{8... | collective-permute-start | bytes 1572872 | tf_op jit(solution)/shard_map/ppermute | solution.py:46
  33.8 11.0 %collective-permute-done.5.refs_6_ = bf16[512,512]{1,0:T(8,128)(2,1)S(1)} collective-permute-done((bf16[512,512]{1,0:T(8,128)(2,1)S(1)}, bf16[512,512]{1,0:T(8,128)(2,1)S(1)}, u32[]{:S(2)}, u32[]{:S(2)}) %collective-permute-start.5) | collective-permute-done | bytes 524320 | tf_op jit(solution)/shard_map/ppermute | solution.py:46
  44.8 3.2 %collective-permute-start.10 = (bf16[512,512]{1,0:T(8,128)(2,1)S(1)}, bf16[512,512]{1,0:T(8,128)(2,1)}, u32[]{:S(2)}, u32[]{:S(2)}) collective-permute-start(bf16[512,512]{1,0:T(8,128)(2,1)S(1)} %collective-permute-done.6.refs_7_), channel_id=1, source_target_pairs={{0,224},{1,225},{2,226},{3,227},{4,228},{5,229},{6,230},{7,231},{8... | collective-permute-start | bytes 1572872 | tf_op jit(solution)/shard_map/ppermute | solution.py:46
  49.0 9.8 %collective-permute-done.9.up_ref.refs_10_ = bf16[512,512]{1,0:T(8,128)(2,1)S(1)} collective-permute-done((bf16[512,512]{1,0:T(8,128)(2,1)S(1)}, bf16[512,512]{1,0:T(8,128)(2,1)S(1)}, u32[]{:S(2)}, u32[]{:S(2)}) %collective-permute-start.9) | collective-permute-done | bytes 524320 | tf_op jit(solution)/shard_map/ppermute | solution.py:46
  58.9 2.1 %cut_blocks.1 = (bf16[256,512]{1,0:T(8,128)(2,1)}, bf16[256,512]{1,0:T(8,128)(2,1)}) custom-call(bf16[512,512]{1,0:T(8,128)(2,1)S(1)} %collective-permute-done.9.up_ref.refs_10_, bf16[512,512]{1,0:T(8,128)(2,1)} %collective-permute-done.10.down_ref.refs_11_), custom_call_target="tpu_custom_call" | custom-call | flops 20000000000 | bytes 1000000 | tf_op jit(solution)/shard_map/cut_blocks/pallas_call | solution.py:161
  60.9 3.2 %collective-permute-start.14 = (bf16[256,512]{1,0:T(8,128)(2,1)}, bf16[256,512]{1,0:T(8,128)(2,1)S(1)}, u32[]{:S(2)}, u32[]{:S(2)}) collective-permute-start(bf16[256,512]{1,0:T(8,128)(2,1)} %get-tuple-element.23), channel_id=1, source_target_pairs={{0,224},{1,225},{2,226},{3,227},{4,228},{5,229},{6,230},{7,231},{8... | collective-permute-start | bytes 786440 | tf_op jit(solution)/shard_map/ppermute | solution.py:46
  64.8 0.7 pad.8
  66.1 2.7 %collective-permute-done.13.upper_ref = bf16[256,512]{1,0:T(8,128)(2,1)S(1)} collective-permute-done((bf16[256,512]{1,0:T(8,128)(2,1)}, bf16[256,512]{1,0:T(8,128)(2,1)S(1)}, u32[]{:S(2)}, u32[]{:S(2)}) %collective-permute-start.13) | collective-permute-done | bytes 262176 | tf_op jit(solution)/shard_map/ppermute | solution.py:46
  68.8 0.7 copy-done.5
  70.0 0.9 copy-done.6
  71.9 0.7 pad_add_fusion.1.facts
  72.7 2.0 %fusion.18 = (f32[256,64]{1,0:T(8,128)}, f32[256,64]{1,0:T(8,128)}, f32[256,64]{1,0:T(8,128)}) fusion(f32[64]{0:T(128)} %multiply_exponential_fusion, f32[256]{0:T(256)S(1)} %add.106), kind=kLoop, calls=%fused_computation.29 | loop fusion | flops 32768 | bytes 197888 | tf_op jit(solution)/shard_map/neg | solution.py:569
  74.7 2.1 %copy-done = bf16[14848,128]{1,0:T(8,128)(2,1)S(1)} copy-done((bf16[14848,128]{1,0:T(8,128)(2,1)S(1)}, bf16[14848,128]{1,0:T(8,128)(2,1)}, u32[]{:S(2)}) %copy-start) | copy-done | bytes 3801112
  76.7 1.8 %norm.1.normed_ref = bf16[16,256,448]{2,1,0:T(8,128)(2,1)S(1)} custom-call(bf16[16,928,128]{2,1,0:T(8,128)(2,1)S(1)} %bitcast.35), custom_call_target="tpu_custom_call" | custom-call | flops 10000000 | bytes 8000000 | tf_op jit(solution)/shard_map/norm/pallas_call | solution.py:213
  78.7 6.2 %project.1 = (bf16[128,576]{1,0:T(8,128)(2,1)S(1)}, bf16[128,576]{1,0:T(8,128)(2,1)}) custom-call(s32[16]{0:T(128)S(1)} %and_select_fusion.order, bf16[16,256,448]{2,1,0:T(8,128)(2,1)S(1)} %norm.1.normed_ref, bf16[512,512]{1,0:T(8,128)(2,1)S(1)} %copy-done.1, bf16[512,512]{1,0:T(8,128)(2,1)S(1)} %collective-permute-done.refs_1_, ...), custom_call_target="tpu_custom_call" | custom-call | flops 2113929216 | bytes 16000000 | tf_op jit(solution)/shard_map/project/pallas_call | solution.py:258
  84.9 1.6 collective-permute-start.16
  86.5 1.3 pad_maximum_fusion
  88.3 3.4 %collective-permute-done.16.oth_ref = bf16[128,576]{1,0:T(8,128)(2,1)S(1)} collective-permute-done((bf16[128,576]{1,0:T(8,128)(2,1)S(1)}, bf16[128,576]{1,0:T(8,128)(2,1)S(1)}, u32[]{:S(2)}, u32[]{:S(2)}) %collective-permute-start.16) | collective-permute-done | bytes 147488 | tf_op jit(solution)/shard_map/ppermute | solution.py:46
  91.8 1.6 copy-done.8
  93.4 1.6 copy-done.9
  95.0 0.9 copy-done.11
  95.9 6.1 %attention.2 = (f32[128,448]{1,0:T(8,128)S(1)}, bf16[128,512]{1,0:T(8,128)(2,1)S(1)}, f32[128,128]{1,0:T(8,128)S(1)}, bf16[2,16,128]{2,1,0:T(8,128)(2,1)S(1)}) custom-call(s32[3]{0:T(128)S(1)} %pad_add_fusion.1.facts, bf16[128,576]{1,0:T(8,128)(2,1)S(1)} %copy-done.11, bf16[128,576]{1,0:T(8,128)(2,1)S(1)} %collective-permute-done.16.oth_ref, ...), custom_call_target="tpu_custom_call" | custom-call | flops 49999998976 | bytes 2097152 | tf_op jit(solution)/shard_map/attention/pallas_call | solution.py:367
  102.0 1.9 %collective-permute-start.17 = (bf16[128,512]{1,0:T(8,128)(2,1)S(1)}, bf16[128,512]{1,0:T(8,128)(2,1)S(1)}, u32[]{:S(2)}, u32[]{:S(2)}) collective-permute-start(bf16[128,512]{1,0:T(8,128)(2,1)S(1)} %get-tuple-element.27), channel_id=1, source_target_pairs={{0,1},{1,0},{2,3},{3,2},{4,5},{5,4},{6,7},{7,6},{8,9},{9,8},{10,11... | collective-permute-start | bytes 393224 | tf_op jit(solution)/shard_map/ppermute | solution.py:46
  103.9 7.0 %attention.3 = (f32[128,448]{1,0:T(8,128)S(1)}, bf16[128,512]{1,0:T(8,128)(2,1)S(1)}, f32[128,128]{1,0:T(8,128)S(1)}, bf16[2,16,128]{2,1,0:T(8,128)(2,1)S(1)}) custom-call(s32[3]{0:T(128)S(1)} %pad_add_fusion.2.facts, bf16[128,576]{1,0:T(8,128)(2,1)} %get-tuple-element.28.own_ref, bf16[128,576]{1,0:T(8,128)(2,1)S(1)} %collective-permute-done.18.oth_ref, ...), custom_call_target="tpu_custom_call" | custom-call | flops 49999998976 | bytes 2097152 | tf_op jit(solution)/shard_map/attention/pallas_call | solution.py:367
  112.5 3.7 %collective-permute-done.19.refs_6_ = bf16[128,512]{1,0:T(8,128)(2,1)S(1)} collective-permute-done((bf16[128,512]{1,0:T(8,128)(2,1)S(1)}, bf16[128,512]{1,0:T(8,128)(2,1)S(1)}, u32[]{:S(2)}, u32[]{:S(2)}) %collective-permute-start.19) | collective-permute-done | bytes 131104 | tf_op jit(solution)/shard_map/ppermute | solution.py:46
  116.2 2.3 %combine.1.att_ref = bf16[256,448]{1,0:T(8,128)(2,1)S(1)} custom-call(s32[4]{0:T(128)S(1)} %pad_add_fusion.place, f32[128,448]{1,0:T(8,128)S(1)} %get-tuple-element.25.refs_0_, f32[128,128]{1,0:T(8,128)S(1)} %get-tuple-element.26.refs_1_, bf16[128,512]{1,0:T(8,128)(2,1)S(1)} %collective-permute-done.17.refs_2_, bf16[128,1]{1,0:T(8,128)(2,1)S(1)} %slice.28.refs_3_, ...), custom_call_target="tpu_custom_call" | custom-call | tf_op jit(solution)/shard_map/combine/pallas_call | solution.py:425
  118.6 2.3 %all-gather.10.cloned.1.call-done = bf16[7168,448]{1,0:T(8,128)(2,1)} async-done(((bf16[448,448]{1,0:T(8,128)(2,1)}), bf16[7168,448]{1,0:T(8,128)(2,1)}) %all-gather.10.cloned.1.call-update) | async-done | bytes 6422544 | tf_op jit(solution)/shard_map/all_gather | solution.py:555
  120.8 3.1 %copy-done.7 = bf16[7168,448]{1,0:T(8,128)(2,1)S(1)} copy-done((bf16[7168,448]{1,0:T(8,128)(2,1)S(1)}, bf16[7168,448]{1,0:T(8,128)(2,1)}, u32[]{:S(2)}) %copy-start.7) | copy-done | bytes 6422552
  123.9 2.9 %out_terms.3 = (bf16[4,896,128]{2,1,0:T(8,128)(2,1)}, bf16[4,896,128]{2,1,0:T(8,128)(2,1)}) custom-call(s32[4]{0:T(128)S(1)} %pad_add_fusion.place, bf16[256,448]{1,0:T(8,128)(2,1)S(1)} %combine.1.att_ref, bf16[16,448,448]{2,1,0:T(8,128)(2,1)S(1)} %bitcast.38), custom_call_target="tpu_custom_call" | custom-call | flops 20000000000 | bytes 20000000 | tf_op jit(solution)/shard_map/out_terms/pallas_call | solution.py:448
  126.8 1.5 collective-permute-start.20
  128.3 2.4 %out_terms.2 = (bf16[4,896,128]{2,1,0:T(8,128)(2,1)}, f32[4,896,128]{2,1,0:T(8,128)S(1)}) custom-call(s32[4]{0:T(128)S(1)} %pad_add_fusion.place, bf16[256,448]{1,0:T(8,128)(2,1)S(1)} %combine.1.att_ref, bf16[16,448,448]{2,1,0:T(8,128)(2,1)S(1)} %bitcast.39), custom_call_target="tpu_custom_call" | custom-call | flops 20000000000 | bytes 20000000 | tf_op jit(solution)/shard_map/out_terms/pallas_call | solution.py:448
  130.7 1.8 %collective-permute-start.21 = (bf16[4,896,128]{2,1,0:T(8,128)(2,1)}, bf16[4,896,128]{2,1,0:T(8,128)(2,1)}, u32[]{:S(2)}, u32[]{:S(2)}) collective-permute-start(bf16[4,896,128]{2,1,0:T(8,128)(2,1)} %get-tuple-element.34), channel_id=1, source_target_pairs={{0,3},{1,0},{2,1},{3,2},{4,7},{5,4},{6,5},{7,6},{8,11},{9,8},{10,9... | collective-permute-start | bytes 2752520 | tf_op jit(solution)/shard_map/ppermute | solution.py:46
  132.4 1.8 %collective-permute-start.22 = (bf16[4,896,128]{2,1,0:T(8,128)(2,1)}, bf16[4,896,128]{2,1,0:T(8,128)(2,1)}, u32[]{:S(2)}, u32[]{:S(2)}) collective-permute-start(bf16[4,896,128]{2,1,0:T(8,128)(2,1)} %get-tuple-element.35), channel_id=1, source_target_pairs={{0,2},{1,3},{2,0},{3,1},{4,6},{5,7},{6,4},{7,5},{8,10},{9,11},{10,... | collective-permute-start | bytes 2752520 | tf_op jit(solution)/shard_map/ppermute | solution.py:46
  134.2 7.4 %collective-permute-done.20.refs_0_ = bf16[4,896,128]{2,1,0:T(8,128)(2,1)S(1)} collective-permute-done((bf16[4,896,128]{2,1,0:T(8,128)(2,1)}, bf16[4,896,128]{2,1,0:T(8,128)(2,1)S(1)}, u32[]{:S(2)}, u32[]{:S(2)}) %collective-permute-start.20) | collective-permute-done | bytes 917536 | tf_op jit(solution)/shard_map/ppermute | solution.py:46
  141.6 11.9 %collective-permute-done.21.refs_1_ = bf16[4,896,128]{2,1,0:T(8,128)(2,1)} collective-permute-done((bf16[4,896,128]{2,1,0:T(8,128)(2,1)}, bf16[4,896,128]{2,1,0:T(8,128)(2,1)}, u32[]{:S(2)}, u32[]{:S(2)}) %collective-permute-start.21) | collective-permute-done | bytes 917536 | tf_op jit(solution)/shard_map/ppermute | solution.py:46
  153.5 2.6 %partial_sums.1 = (f32[896,128]{1,0:T(8,128)S(1)}, bf16[896,128]{1,0:T(8,128)(2,1)}, bf16[896,128]{1,0:T(8,128)(2,1)}, bf16[896,128]{1,0:T(8,128)(2,1)}) custom-call(s32[1]{0:T(128)} %bitcast.1.place, f32[4,896,128]{2,1,0:T(8,128)S(1)} %get-tuple-element.32.own_ref, bf16[4,896,128]{2,1,0:T(8,128)(2,1)S(1)} %collective-permute-done.20.refs_0_, ...), custom_call_target="tpu_custom_call" | custom-call | tf_op jit(solution)/shard_map/partial_sums/pallas_call | solution.py:475
  156.1 1.4 collective-permute-start.23
  157.6 2.1 %collective-permute-start.24 = (bf16[896,128]{1,0:T(8,128)(2,1)}, bf16[896,128]{1,0:T(8,128)(2,1)S(1)}, u32[]{:S(2)}, u32[]{:S(2)}) collective-permute-start(bf16[896,128]{1,0:T(8,128)(2,1)} %get-tuple-element.38), channel_id=1, source_target_pairs={{0,4},{1,5},{2,6},{3,7},{4,8},{5,9},{6,10},{7,11},{8,12},{9,13},{1... | collective-permute-start | bytes 688136 | tf_op jit(solution)/shard_map/ppermute | solution.py:46
  160.1 0.9 slice.30
  161.2 0.7 reshape.73
  161.9 1.9 %collective-permute-done.23.refs_0_ = bf16[896,128]{1,0:T(8,128)(2,1)S(1)} collective-permute-done((bf16[896,128]{1,0:T(8,128)(2,1)}, bf16[896,128]{1,0:T(8,128)(2,1)S(1)}, u32[]{:S(2)}, u32[]{:S(2)}) %collective-permute-start.23) | collective-permute-done | bytes 229408 | tf_op jit(solution)/shard_map/ppermute | solution.py:46
  164.2 2.9 %collective-permute-done.25.refs_2_ = bf16[896,128]{1,0:T(8,128)(2,1)S(1)} collective-permute-done((bf16[896,128]{1,0:T(8,128)(2,1)}, bf16[896,128]{1,0:T(8,128)(2,1)S(1)}, u32[]{:S(2)}, u32[]{:S(2)}) %collective-permute-start.25) | collective-permute-done | bytes 229408 | tf_op jit(solution)/shard_map/ppermute | solution.py:46
  167.1 0.9 final.1
  (96 shorter events, 9.2 us)
Async XLA Ops:
  7.2 10.7 %copy-start.17 = (s32[2]{0:T(128)S(1)}, s32[2]{0:T(128)}, u32[]{:S(2)}) copy-start(s32[2]{0:T(128)} %constant.91.clone) | copy-start | bytes 28
  7.2 10.7 %copy-start.18 = (s32[2]{0:T(128)S(1)}, s32[2]{0:T(128)}, u32[]{:S(2)}) copy-start(s32[2]{0:T(128)} %constant.92.clone) | copy-start | bytes 28
  7.2 9.9 %copy-start.15 = (s32[4]{0:T(128)S(1)}, s32[4]{0:T(128)}, u32[]{:S(2)}) copy-start(s32[4]{0:T(128)} %param.23) | copy-start | bytes 52
  7.2 25.8 %copy-start.19 = (s32[4,64]{1,0:T(4,128)S(1)}, s32[4,64]{1,0:T(4,128)}, u32[]{:S(2)}) copy-start(s32[4,64]{1,0:T(4,128)} %param.24) | copy-start | bytes 3076
  7.2 67.4 %all-gather.8.cloned.1.call-start = ((), (), s32[]{:S(2)}) async-start(), calls=%async_computation.1 | async-start | bytes 4038656 | tf_op jit(solution)/shard_map/all_gather | solution.py:553
  9.0 111.8 %all-gather.10.cloned.1.call-start = ((), (), s32[]{:S(2)}) async-start(), calls=%async_computation.2 | async-start | bytes 7798784 | tf_op jit(solution)/shard_map/all_gather | solution.py:555
  11.1 59.9 %collective-permute-start = (bf16[512,512]{1,0:T(8,128)(2,1)}, bf16[512,512]{1,0:T(8,128)(2,1)S(1)}, u32[]{:S(2)}, u32[]{:S(2)}) collective-permute-start(bf16[512,512]{1,0:T(8,128)(2,1)} %pack_weights.1.refs_0_), channel_id=1, source_target_pairs={{0,16},{1,17},{2,18},{3,19},{4,20},{5,21},{6,22},{7,23},{8,24},{9,... | collective-permute-start | bytes 1572872 | tf_op jit(solution)/shard_map/ppermute | solution.py:46
  11.1 18.7 %collective-permute-start.1 = (bf16[512,512]{1,0:T(8,128)(2,1)}, bf16[512,512]{1,0:T(8,128)(2,1)S(1)}, u32[]{:S(2)}, u32[]{:S(2)}) collective-permute-start(bf16[512,512]{1,0:T(8,128)(2,1)} %pack_weights.1.refs_0_), channel_id=1, source_target_pairs={{0,32},{1,33},{2,34},{3,35},{4,36},{5,37},{6,38},{7,39},{8,40},{9,... | collective-permute-start | bytes 1572872 | tf_op jit(solution)/shard_map/ppermute | solution.py:46
  13.0 16.7 %collective-permute-start.2 = (bf16[512,512]{1,0:T(8,128)(2,1)}, bf16[512,512]{1,0:T(8,128)(2,1)S(1)}, u32[]{:S(2)}, u32[]{:S(2)}) collective-permute-start(bf16[512,512]{1,0:T(8,128)(2,1)} %pack_weights.1.refs_0_), channel_id=1, source_target_pairs={{0,224},{1,225},{2,226},{3,227},{4,228},{5,229},{6,230},{7,231},{8... | collective-permute-start | bytes 1572872 | tf_op jit(solution)/shard_map/ppermute | solution.py:46
  17.0 143.1 %all-gather.6.cloned.1.call-start = ((), (), s32[]{:S(2)}) async-start(), calls=%async_computation | async-start | bytes 1392640 | tf_op jit(solution)/shard_map/all_gather | solution.py:604
  29.8 15.0 %collective-permute-start.5 = (bf16[512,512]{1,0:T(8,128)(2,1)S(1)}, bf16[512,512]{1,0:T(8,128)(2,1)S(1)}, u32[]{:S(2)}, u32[]{:S(2)}) collective-permute-start(bf16[512,512]{1,0:T(8,128)(2,1)S(1)} %collective-permute-done.1.refs_2_), channel_id=1, source_target_pairs={{0,32},{1,33},{2,34},{3,35},{4,36},{5,37},{6,38},{7,39},{8,40},{9,... | collective-permute-start | bytes 1572872 | tf_op jit(solution)/shard_map/ppermute | solution.py:46
  29.8 15.0 %collective-permute-start.6 = (bf16[512,512]{1,0:T(8,128)(2,1)S(1)}, bf16[512,512]{1,0:T(8,128)(2,1)S(1)}, u32[]{:S(2)}, u32[]{:S(2)}) collective-permute-start(bf16[512,512]{1,0:T(8,128)(2,1)S(1)} %collective-permute-done.2.refs_3_), channel_id=1, source_target_pairs={{0,224},{1,225},{2,226},{3,227},{4,228},{5,229},{6,230},{7,231},{8... | collective-permute-start | bytes 1572872 | tf_op jit(solution)/shard_map/ppermute | solution.py:46
  44.8 14.1 %collective-permute-start.9 = (bf16[512,512]{1,0:T(8,128)(2,1)S(1)}, bf16[512,512]{1,0:T(8,128)(2,1)S(1)}, u32[]{:S(2)}, u32[]{:S(2)}) collective-permute-start(bf16[512,512]{1,0:T(8,128)(2,1)S(1)} %collective-permute-done.5.refs_6_), channel_id=1, source_target_pairs={{0,32},{1,33},{2,34},{3,35},{4,36},{5,37},{6,38},{7,39},{8,40},{9,... | collective-permute-start | bytes 1572872 | tf_op jit(solution)/shard_map/ppermute | solution.py:46
  44.8 14.1 %collective-permute-start.10 = (bf16[512,512]{1,0:T(8,128)(2,1)S(1)}, bf16[512,512]{1,0:T(8,128)(2,1)}, u32[]{:S(2)}, u32[]{:S(2)}) collective-permute-start(bf16[512,512]{1,0:T(8,128)(2,1)S(1)} %collective-permute-done.6.refs_7_), channel_id=1, source_target_pairs={{0,224},{1,225},{2,226},{3,227},{4,228},{5,229},{6,230},{7,231},{8... | collective-permute-start | bytes 1572872 | tf_op jit(solution)/shard_map/ppermute | solution.py:46
  48.5 17.0 %copy-start.13 = (s32[4,64]{1,0:T(4,128)S(1)}, s32[4,64]{1,0:T(4,128)}, u32[]{:S(2)}) copy-start(s32[4,64]{1,0:T(4,128)} %param.25) | copy-start | bytes 3076
  48.5 22.7 %collective-permute-start.3 = (bf16[512,512]{1,0:T(8,128)(2,1)S(1)}, bf16[512,512]{1,0:T(8,128)(2,1)}, u32[]{:S(2)}, u32[]{:S(2)}) collective-permute-start(bf16[512,512]{1,0:T(8,128)(2,1)S(1)} %collective-permute-done.1.refs_2_), channel_id=1, source_target_pairs={{0,16},{1,17},{2,18},{3,19},{4,20},{5,21},{6,22},{7,23},{8,24},{9,... | collective-permute-start | bytes 1572872 | tf_op jit(solution)/shard_map/ppermute | solution.py:46
  48.5 23.1 %collective-permute-start.4 = (bf16[512,512]{1,0:T(8,128)(2,1)S(1)}, bf16[512,512]{1,0:T(8,128)(2,1)}, u32[]{:S(2)}, u32[]{:S(2)}) collective-permute-start(bf16[512,512]{1,0:T(8,128)(2,1)S(1)} %collective-permute-done.2.refs_3_), channel_id=1, source_target_pairs={{0,16},{1,17},{2,18},{3,19},{4,20},{5,21},{6,22},{7,23},{8,24},{9,... | collective-permute-start | bytes 1572872 | tf_op jit(solution)/shard_map/ppermute | solution.py:46
  58.9 2.1 %copy-start.3 = (bf16[512,512]{1,0:T(8,128)(2,1)}, bf16[512,512]{1,0:T(8,128)(2,1)S(1)}, u32[]{:S(2)}) copy-start(bf16[512,512]{1,0:T(8,128)(2,1)S(1)} %collective-permute-done.9.up_ref.refs_10_) | copy-start | bytes 1572868
  60.9 7.9 %collective-permute-start.13 = (bf16[256,512]{1,0:T(8,128)(2,1)}, bf16[256,512]{1,0:T(8,128)(2,1)S(1)}, u32[]{:S(2)}, u32[]{:S(2)}) collective-permute-start(bf16[256,512]{1,0:T(8,128)(2,1)} %get-tuple-element.22), channel_id=1, source_target_pairs={{0,32},{1,33},{2,34},{3,35},{4,36},{5,37},{6,38},{7,39},{8,40},{9,... | collective-permute-start | bytes 786440 | tf_op jit(solution)/shard_map/ppermute | solution.py:46
  60.9 7.9 %collective-permute-start.14 = (bf16[256,512]{1,0:T(8,128)(2,1)}, bf16[256,512]{1,0:T(8,128)(2,1)S(1)}, u32[]{:S(2)}, u32[]{:S(2)}) collective-permute-start(bf16[256,512]{1,0:T(8,128)(2,1)} %get-tuple-element.23), channel_id=1, source_target_pairs={{0,224},{1,225},{2,226},{3,227},{4,228},{5,229},{6,230},{7,231},{8... | collective-permute-start | bytes 786440 | tf_op jit(solution)/shard_map/ppermute | solution.py:46
  68.8 9.8 %collective-permute-start.7 = (bf16[512,512]{1,0:T(8,128)(2,1)S(1)}, bf16[512,512]{1,0:T(8,128)(2,1)}, u32[]{:S(2)}, u32[]{:S(2)}) collective-permute-start(bf16[512,512]{1,0:T(8,128)(2,1)S(1)} %collective-permute-done.5.refs_6_), channel_id=1, source_target_pairs={{0,16},{1,17},{2,18},{3,19},{4,20},{5,21},{6,22},{7,23},{8,24},{9,... | collective-permute-start | bytes 1572872 | tf_op jit(solution)/shard_map/ppermute | solution.py:46
  69.5 9.1 %collective-permute-start.8 = (bf16[512,512]{1,0:T(8,128)(2,1)S(1)}, bf16[512,512]{1,0:T(8,128)(2,1)}, u32[]{:S(2)}, u32[]{:S(2)}) collective-permute-start(bf16[512,512]{1,0:T(8,128)(2,1)S(1)} %collective-permute-done.6.refs_7_), channel_id=1, source_target_pairs={{0,16},{1,17},{2,18},{3,19},{4,20},{5,21},{6,22},{7,23},{8,24},{9,... | collective-permute-start | bytes 1572872 | tf_op jit(solution)/shard_map/ppermute | solution.py:46
  70.0 0.9 copy-start.6
  71.0 7.6 %collective-permute-start.11 = (bf16[512,512]{1,0:T(8,128)(2,1)}, bf16[512,512]{1,0:T(8,128)(2,1)}, u32[]{:S(2)}, u32[]{:S(2)}) collective-permute-start(bf16[512,512]{1,0:T(8,128)(2,1)} %copy-done.3), channel_id=1, source_target_pairs={{0,16},{1,17},{2,18},{3,19},{4,20},{5,21},{6,22},{7,23},{8,24},{9,... | collective-permute-start | bytes 1572872 | tf_op jit(solution)/shard_map/ppermute | solution.py:46
  71.1 7.5 %collective-permute-start.12 = (bf16[512,512]{1,0:T(8,128)(2,1)}, bf16[512,512]{1,0:T(8,128)(2,1)}, u32[]{:S(2)}, u32[]{:S(2)}) collective-permute-start(bf16[512,512]{1,0:T(8,128)(2,1)} %collective-permute-done.10.down_ref.refs_11_), channel_id=1, source_target_pairs={{0,16},{1,17},{2,18},{3,19},{4,20},{5,21},{6,22},{7,23},{8,24},{9,... | collective-permute-start | bytes 1572872 | tf_op jit(solution)/shard_map/ppermute | solution.py:46
  71.6 7.0 %collective-permute-start.15 = (bf16[512,512]{1,0:T(8,128)(2,1)S(1)}, bf16[512,512]{1,0:T(8,128)(2,1)}, u32[]{:S(2)}, u32[]{:S(2)}) collective-permute-start(bf16[512,512]{1,0:T(8,128)(2,1)S(1)} %join.1.refs_14_), channel_id=1, source_target_pairs={{0,16},{1,17},{2,18},{3,19},{4,20},{5,21},{6,22},{7,23},{8,24},{9,... | collective-permute-start | bytes 1572872 | tf_op jit(solution)/shard_map/ppermute | solution.py:46
  74.7 2.1 %copy-start = (bf16[14848,128]{1,0:T(8,128)(2,1)S(1)}, bf16[14848,128]{1,0:T(8,128)(2,1)}, u32[]{:S(2)}) copy-start(bf16[14848,128]{1,0:T(8,128)(2,1)} %all-gather.8.cloned.1.call-done) | copy-start | bytes 11403268
  76.7 1.9 %copy-start.1 = (bf16[512,512]{1,0:T(8,128)(2,1)S(1)}, bf16[512,512]{1,0:T(8,128)(2,1)}, u32[]{:S(2)}) copy-start(bf16[512,512]{1,0:T(8,128)(2,1)} %pack_weights.1.refs_0_) | copy-start | bytes 1572868
  76.7 1.9 %copy-start.4 = (bf16[512,512]{1,0:T(8,128)(2,1)S(1)}, bf16[512,512]{1,0:T(8,128)(2,1)}, u32[]{:S(2)}) copy-start(bf16[512,512]{1,0:T(8,128)(2,1)} %copy-done.3) | copy-start | bytes 1572868
  78.6 7.9 %copy-start.16 = (s32[2]{0:T(128)S(1)}, s32[2]{0:T(128)}, u32[]{:S(2)}) copy-start(s32[2]{0:T(128)} %get-tuple-element.47) | copy-start | bytes 28
  84.9 6.9 %copy-start.10 = (bf16[128,576]{1,0:T(8,128)(2,1)}, bf16[128,576]{1,0:T(8,128)(2,1)S(1)}, u32[]{:S(2)}) copy-start(bf16[128,576]{1,0:T(8,128)(2,1)S(1)} %get-tuple-element.24.own_ref) | copy-start | bytes 442372
  84.9 6.9 %collective-permute-start.16 = (bf16[128,576]{1,0:T(8,128)(2,1)S(1)}, bf16[128,576]{1,0:T(8,128)(2,1)S(1)}, u32[]{:S(2)}, u32[]{:S(2)}) collective-permute-start(bf16[128,576]{1,0:T(8,128)(2,1)S(1)} %get-tuple-element.24.own_ref), channel_id=1, source_target_pairs={{0,1},{1,0},{2,3},{3,2},{4,5},{5,4},{6,7},{7,6},{8,9},{9,8},{10,11... | collective-permute-start | bytes 442376 | tf_op jit(solution)/shard_map/ppermute | solution.py:46
  87.8 16.1 %collective-permute-start.18 = (bf16[128,576]{1,0:T(8,128)(2,1)}, bf16[128,576]{1,0:T(8,128)(2,1)S(1)}, u32[]{:S(2)}, u32[]{:S(2)}) collective-permute-start(bf16[128,576]{1,0:T(8,128)(2,1)} %get-tuple-element.28.own_ref), channel_id=1, source_target_pairs={{0,1},{1,0},{2,3},{3,2},{4,5},{5,4},{6,7},{7,6},{8,9},{9,8},{10,11... | collective-permute-start | bytes 442376 | tf_op jit(solution)/shard_map/ppermute | solution.py:46
  91.8 1.6 copy-start.8
  93.4 1.6 copy-start.9
  102.0 9.5 %copy-start.14 = (s32[2]{0:T(128)S(1)}, s32[2]{0:T(128)}, u32[]{:S(2)}) copy-start(s32[2]{0:T(128)} %broadcast_select_fusion) | copy-start | bytes 28
  102.0 9.5 %copy-start.12 = (bf16[2,64]{1,0:T(2,128)(2,1)S(1)}, bf16[2,64]{1,0:T(2,128)(2,1)}, u32[]{:S(2)}) copy-start(bf16[2,64]{1,0:T(2,128)(2,1)} %get-tuple-element.46) | copy-start | bytes 772
  102.0 10.5 %collective-permute-start.17 = (bf16[128,512]{1,0:T(8,128)(2,1)S(1)}, bf16[128,512]{1,0:T(8,128)(2,1)S(1)}, u32[]{:S(2)}, u32[]{:S(2)}) collective-permute-start(bf16[128,512]{1,0:T(8,128)(2,1)S(1)} %get-tuple-element.27), channel_id=1, source_target_pairs={{0,1},{1,0},{2,3},{3,2},{4,5},{5,4},{6,7},{7,6},{8,9},{9,8},{10,11... | collective-permute-start | bytes 393224 | tf_op jit(solution)/shard_map/ppermute | solution.py:46
  111.0 5.3 %collective-permute-start.19 = (bf16[128,512]{1,0:T(8,128)(2,1)S(1)}, bf16[128,512]{1,0:T(8,128)(2,1)S(1)}, u32[]{:S(2)}, u32[]{:S(2)}) collective-permute-start(bf16[128,512]{1,0:T(8,128)(2,1)S(1)} %get-tuple-element.31), channel_id=1, source_target_pairs={{0,1},{1,0},{2,3},{3,2},{4,5},{5,4},{6,7},{7,6},{8,9},{9,8},{10,11... | collective-permute-start | bytes 393224 | tf_op jit(solution)/shard_map/ppermute | solution.py:46
  120.8 3.1 %copy-start.7 = (bf16[7168,448]{1,0:T(8,128)(2,1)S(1)}, bf16[7168,448]{1,0:T(8,128)(2,1)}, u32[]{:S(2)}) copy-start(bf16[7168,448]{1,0:T(8,128)(2,1)} %all-gather.10.cloned.1.call-done) | copy-start | bytes 19267588
  126.8 14.8 %collective-permute-start.20 = (bf16[4,896,128]{2,1,0:T(8,128)(2,1)}, bf16[4,896,128]{2,1,0:T(8,128)(2,1)S(1)}, u32[]{:S(2)}, u32[]{:S(2)}) collective-permute-start(bf16[4,896,128]{2,1,0:T(8,128)(2,1)} %get-tuple-element.33), channel_id=1, source_target_pairs={{0,1},{1,2},{2,3},{3,0},{4,5},{5,6},{6,7},{7,4},{8,9},{9,10},{10,1... | collective-permute-start | bytes 2752520 | tf_op jit(solution)/shard_map/ppermute | solution.py:46
  130.7 22.8 %collective-permute-start.21 = (bf16[4,896,128]{2,1,0:T(8,128)(2,1)}, bf16[4,896,128]{2,1,0:T(8,128)(2,1)}, u32[]{:S(2)}, u32[]{:S(2)}) collective-permute-start(bf16[4,896,128]{2,1,0:T(8,128)(2,1)} %get-tuple-element.34), channel_id=1, source_target_pairs={{0,3},{1,0},{2,1},{3,2},{4,7},{5,4},{6,5},{7,6},{8,11},{9,8},{10,9... | collective-permute-start | bytes 2752520 | tf_op jit(solution)/shard_map/ppermute | solution.py:46
  132.4 21.1 %collective-permute-start.22 = (bf16[4,896,128]{2,1,0:T(8,128)(2,1)}, bf16[4,896,128]{2,1,0:T(8,128)(2,1)}, u32[]{:S(2)}, u32[]{:S(2)}) collective-permute-start(bf16[4,896,128]{2,1,0:T(8,128)(2,1)} %get-tuple-element.35), channel_id=1, source_target_pairs={{0,2},{1,3},{2,0},{3,1},{4,6},{5,7},{6,4},{7,5},{8,10},{9,11},{10,... | collective-permute-start | bytes 2752520 | tf_op jit(solution)/shard_map/ppermute | solution.py:46
  153.5 7.5 %copy-start.20 = (s32[64]{0:T(128)S(1)}, s32[64]{0:T(128)}, u32[]{:S(2)}) copy-start(s32[64]{0:T(128)} %param.27) | copy-start | bytes 772
  153.5 13.5 %copy-start.2 = (bf16[4,64,448]{2,1,0:T(8,128)(2,1)S(1)}, bf16[4,64,448]{2,1,0:T(8,128)(2,1)}, u32[]{:S(2)}) copy-start(bf16[4,64,448]{2,1,0:T(8,128)(2,1)} %param.15) | copy-start | bytes 688132
  156.1 7.7 %collective-permute-start.23 = (bf16[896,128]{1,0:T(8,128)(2,1)}, bf16[896,128]{1,0:T(8,128)(2,1)S(1)}, u32[]{:S(2)}, u32[]{:S(2)}) collective-permute-start(bf16[896,128]{1,0:T(8,128)(2,1)} %get-tuple-element.37), channel_id=1, source_target_pairs={{0,8},{1,9},{2,10},{3,11},{4,12},{5,13},{6,14},{7,15},{8,0},{9,1},... | collective-permute-start | bytes 688136 | tf_op jit(solution)/shard_map/ppermute | solution.py:46
  157.6 6.6 %collective-permute-start.24 = (bf16[896,128]{1,0:T(8,128)(2,1)}, bf16[896,128]{1,0:T(8,128)(2,1)S(1)}, u32[]{:S(2)}, u32[]{:S(2)}) collective-permute-start(bf16[896,128]{1,0:T(8,128)(2,1)} %get-tuple-element.38), channel_id=1, source_target_pairs={{0,4},{1,5},{2,6},{3,7},{4,8},{5,9},{6,10},{7,11},{8,12},{9,13},{1... | collective-permute-start | bytes 688136 | tf_op jit(solution)/shard_map/ppermute | solution.py:46
  159.6 7.4 %collective-permute-start.25 = (bf16[896,128]{1,0:T(8,128)(2,1)}, bf16[896,128]{1,0:T(8,128)(2,1)S(1)}, u32[]{:S(2)}, u32[]{:S(2)}) collective-permute-start(bf16[896,128]{1,0:T(8,128)(2,1)} %get-tuple-element.39), channel_id=1, source_target_pairs={{0,12},{1,13},{2,14},{3,15},{4,0},{5,1},{6,2},{7,3},{8,4},{9,5},{1... | collective-permute-start | bytes 688136 | tf_op jit(solution)/shard_map/ppermute | solution.py:46
  (2 other events, 1.6 us)
Sparse Core Ops, SparseCore 0:
  10.5 57.7 all-gather.7
  70.1 50.6 all-gather.9
  122.7 37.4 all-gather.5
